TPU v7x, 128 devices: a whole 4x4x4 slice. The times are simulated.
128 devices in a mesh: order: 32 (over z, y, x_hi), mp: 4 (over x_lo, core).
Axes of the slice: x: 4 (x_hi: 2, x_lo: 2; x = x_hi * 2 + x_lo), y: 4, z: 4, core: 2. Of those that a mesh axis runs over, the one named last changes fastest.
Arguments:
- feats: float32 [256, 131072], P(None, 'order'), may hold values from -60 to 60
- serial_rank: int32 [131072], P('order'), may hold values from 0 to 131071, as said below
- neighbours: int32 [27, 131072], P(None, 'order'), may hold values from -1 to 131071, as said below
- norm_gain: float32 [5, 256], replicated, may hold values from 0.5 to 1.5
- norm_bias: float32 [5, 256], replicated, may hold values from -1.5 to 1.5
- qkv_weight: bfloat16 [2, 3, 256, 256], P(None, None, None, 'mp'), may hold values from -25 to 25
- qkv_bias: bfloat16 [2, 3, 256], P(None, None, 'mp'), may hold values from -1.5 to 1.5
- proj_weight: bfloat16 [2, 256, 256], P(None, 'mp'), may hold values from -0.375 to 0.375
- proj_bias: bfloat16 [2, 256], replicated, may hold values from -1.5 to 1.5
- fc1_weight: bfloat16 [2, 256, 1024], P(None, None, 'mp'), may hold values from -0.375 to 0.375
- fc1_bias: bfloat16 [2, 1024], P(None, 'mp'), may hold values from -2.5 to 2.5
- fc2_weight: bfloat16 [2, 1024, 256], P(None, 'mp'), may hold values from -0.1875 to 0.1875
- fc2_bias: bfloat16 [2, 256], replicated, may hold values from -1.5 to 1.5
- conv_weight: bfloat16 [27, 256, 256], P(None, None, 'mp'), may hold values from -0.109375 to 0.109375
- conv_bias: bfloat16 [256], P('mp'), may hold values from -2.5 to 2.5
- cpe_weight: bfloat16 [256, 256], replicated, may hold values from -0.375 to 0.375
- cpe_bias: bfloat16 [256], replicated, may hold values from -2.5 to 2.5
Outputs:
- result: float32 [256, 131072], P('mp', 'order')
Inputs may be any that keep to these rules, and one draw needn't show every extreme that they name: A permutation: the token at position t of the first order takes position serial_rank[t] of the second; order index j holds second-order positions j * 4096 to (j + 1) * 4096 - 1; of the 4096 tokens of one order index at most 256 take positions of any one order index, and exactly 256 do for some pairs. `neighbours`: each entry is -1 or a position within 128 of the column's own; row 13 is the column's own position; rows 0 and 26 are the own position minus and plus 128 wherever that lies inside the sequence.
All inputs are finite; a program needn't handle non-finite values.
Results may differ from a plain program's by a relative error of at most 0.018.
The roundings to bfloat16 on the way count: a program that leaves them out, or rounds other values in their place, can miss the bound.
Values may be sent and summed in bfloat16 or wider, within the bound.
A program may use at most 128 MiB of HBM per device.

v0:
```python
import math

import jax
import jax.numpy as jnp
from jax import lax
from jax.sharding import PartitionSpec as P

PATCH = 1024
HALO = 128
HDIM = 16


epsilon = 1e-05


def with_halo(value, sides, width):
    for axis, dim in sides:
        peers, length = (lax.axis_size(axis), value.shape[dim])
        up = [(i, (i + 1) % peers) for i in range(peers - 1)]
        down = [(j, i) for i, j in up]
        last = lax.slice_in_dim(value, length - width, length, axis=dim)
        initial = lax.slice_in_dim(value, 0, width, axis=dim)
        before = lax.ppermute(last, axis, up)
        after = lax.ppermute(initial, axis, down)
        value = jnp.concatenate([before, value, after], axis=dim)
    return value


def layer_norm(values, scale_row, shift_row):
    average = jnp.mean(values, axis=0, keepdims=True)
    centred = values - average
    variance = jnp.mean(centred * centred, axis=0, keepdims=True)
    return centred * lax.rsqrt(variance + epsilon) * scale_row[:, None] + shift_row[:, None]


def contract(left_side, right_side):
    return lax.dot_general(
        left_side, right_side, (((0,), (0,)), ((), ())), preferred_element_type=jnp.float32
    )


def add_heads(partial_value):
    return lax.psum(partial_value, "mp")


def patch_heads(normed, weight_block, bias_block):
    local_cols = weight_block.shape[2]
    tokens = normed.shape[1]
    head_count = local_cols // HDIM
    patch_count = tokens // PATCH
    projected = jnp.einsum("jcl,ct->jlt", weight_block, normed, preferred_element_type=jnp.float32)
    triples = (projected + bias_block.astype(jnp.float32)[:, :, None]).astype(jnp.bfloat16)
    triples = triples.reshape(3, head_count, HDIM, patch_count, PATCH).transpose(1, 3, 0, 2, 4)
    triples = triples.reshape(head_count * patch_count, 3, HDIM, PATCH)
    inverse_root = 1.0 / math.sqrt(HDIM)

    def single(triple):
        scores = (
            jnp.einsum("dq,dk->qk", triple[0], triple[1], preferred_element_type=jnp.float32)
            * inverse_root
        )
        largest = jnp.max(scores, axis=1, keepdims=True)
        weights = jnp.exp(scores - largest)
        chances = (weights / jnp.sum(weights, axis=1, keepdims=True)).astype(jnp.bfloat16)
        return jnp.einsum(
            "qk,dk->dq", chances, triple[2], preferred_element_type=jnp.float32
        ).astype(jnp.bfloat16)

    results = lax.map(single, triples)
    return (
        results.reshape(head_count, patch_count, HDIM, PATCH)
        .transpose(0, 2, 1, 3)
        .reshape(local_cols, tokens)
    )


def attend(
    stream, block_id, norm_id, norm_gain, norm_bias, qkv_weight, qkv_bias, proj_weight, proj_bias
):
    out_bias = proj_bias[block_id].astype(jnp.float32)[:, None]
    weight_block, proj_full, bias_block = (
        lax.all_gather(qkv_weight[block_id], "mp", axis=2, tiled=True),
        lax.all_gather(proj_weight[block_id], "mp", axis=0, tiled=True),
        lax.all_gather(qkv_bias[block_id], "mp", axis=1, tiled=True),
    )
    slice_width = stream.shape[1] // lax.axis_size("mp")
    first_token = lax.axis_index("mp") * slice_width
    own_rows = lax.dynamic_slice_in_dim(stream, first_token, slice_width, 1)
    normed = layer_norm(own_rows, norm_gain[norm_id], norm_bias[norm_id]).astype(jnp.bfloat16)
    head_out = patch_heads(normed, weight_block, bias_block)
    own_rows = own_rows + (contract(proj_full, head_out) + out_bias)
    return lax.all_gather(own_rows, "mp", axis=1, tiled=True)


def feed_forward(
    stream,
    block_id,
    norm_id,
    last_layer,
    norm_gain,
    norm_bias,
    fc1_weight,
    fc1_bias,
    fc2_weight,
    fc2_bias,
):
    normed = layer_norm(stream, norm_gain[norm_id], norm_bias[norm_id]).astype(jnp.bfloat16)
    out_bias = fc2_bias[block_id].astype(jnp.float32)[:, None]
    hidden = (
        contract(fc1_weight[block_id], normed) + fc1_bias[block_id].astype(jnp.float32)[:, None]
    )
    hidden = jax.nn.gelu(hidden, approximate=False).astype(jnp.bfloat16)
    weight_down = fc2_weight[block_id]
    if last_layer:
        share_rows = stream.shape[0] // lax.axis_size("mp")
        own_share = lax.psum_scatter(
            contract(weight_down, hidden).astype(jnp.bfloat16),
            "mp",
            scatter_dimension=0,
            tiled=True,
        ).astype(jnp.float32)
        first_row = lax.axis_index("mp") * share_rows
        kept_rows = lax.dynamic_slice_in_dim(stream, first_row, share_rows, 0)
        finished = kept_rows + (
            own_share + lax.dynamic_slice_in_dim(out_bias, first_row, share_rows, 0)
        )
    else:
        finished = stream + (add_heads(contract(weight_down, hidden)) + out_bias)
    return finished


def relay_rows(stream, serial_rank):
    groups = lax.axis_size("order")
    tokens = stream.shape[1]
    capacity = 2 * tokens // groups
    owners = serial_rank // tokens
    local_spot = serial_rank % tokens
    marked = (owners[:, None] == jnp.arange(groups, dtype=jnp.int32)[None, :]).astype(jnp.int32)
    before = jnp.cumsum(marked, axis=0) - marked
    slot_index = jnp.sum(before * marked, axis=1)
    flat_place = owners * capacity + slot_index
    source = (
        jnp.full((groups * capacity,), tokens, jnp.int32)
        .at[flat_place]
        .set(jnp.arange(tokens, dtype=jnp.int32))
    )
    target = jnp.full((groups * capacity,), tokens, jnp.int32).at[flat_place].set(local_spot)
    feature_rows = stream.shape[0]
    padded = jnp.concatenate([stream, jnp.zeros((feature_rows, 1), jnp.float32)], axis=1)
    packed = padded[:, source].reshape(feature_rows, groups, capacity)
    arrived, landing = (
        lax.all_to_all(packed, "order", split_axis=1, concat_axis=1, tiled=True),
        lax.all_to_all(
            target.reshape(1, groups, capacity), "order", split_axis=1, concat_axis=1, tiled=True
        ),
    )
    placed = (
        jnp.zeros((feature_rows, tokens + 1), jnp.float32)
        .at[:, landing.reshape(-1)]
        .set(arrived.reshape(feature_rows, groups * capacity))
    )
    placed = placed[:, :tokens]
    return placed


def position_code(
    stream, neighbours, conv_weight, conv_bias, cpe_weight, cpe_bias, scale_row, shift_row
):
    tokens = stream.shape[1]
    widened = with_halo(stream.astype(jnp.bfloat16), (("order", 1),), HALO)
    widened = jnp.concatenate([widened, jnp.zeros((widened.shape[0], 1), jnp.bfloat16)], axis=1)
    first_token = lax.axis_index("order") * tokens
    columns = jnp.where(neighbours < 0, tokens + 2 * HALO, neighbours - first_token + HALO)

    def offset_step(running, pieces):
        kernel, picked = pieces
        return (running + contract(kernel, widened[:, picked]), None)

    start_value = (
        jnp.zeros((conv_bias.shape[0], tokens), jnp.float32)
        + conv_bias.astype(jnp.float32)[:, None]
    )
    summed, _ = lax.scan(offset_step, start_value, (conv_weight, columns))
    conv_out = summed.astype(jnp.bfloat16)
    mixture = contract(cpe_weight, lax.all_gather(conv_out, "mp", axis=0, tiled=True))
    return stream + layer_norm(
        mixture + cpe_bias.astype(jnp.float32)[:, None], scale_row, shift_row
    )


def shards(
    feats,
    serial_rank,
    neighbours,
    norm_gain,
    norm_bias,
    qkv_weight,
    qkv_bias,
    proj_weight,
    proj_bias,
    fc1_weight,
    fc1_bias,
    fc2_weight,
    fc2_bias,
    conv_weight,
    conv_bias,
    cpe_weight,
    cpe_bias,
):
    stream = attend(feats, 0, 0, norm_gain, norm_bias, qkv_weight, qkv_bias, proj_weight, proj_bias)
    stream = feed_forward(
        stream, 0, 1, False, norm_gain, norm_bias, fc1_weight, fc1_bias, fc2_weight, fc2_bias
    )
    stream = relay_rows(stream, serial_rank)
    stream = position_code(
        stream, neighbours, conv_weight, conv_bias, cpe_weight, cpe_bias, norm_gain[2], norm_bias[2]
    )
    stream = attend(
        stream, 1, 3, norm_gain, norm_bias, qkv_weight, qkv_bias, proj_weight, proj_bias
    )
    return feed_forward(
        stream, 1, 4, True, norm_gain, norm_bias, fc1_weight, fc1_bias, fc2_weight, fc2_bias
    )


def solution(mesh):
    in_specs = (
        P(None, "order"),
        P("order"),
        P(None, "order"),
        P(),
        P(),
        P(None, None, None, "mp"),
        P(None, None, "mp"),
        P(None, "mp", None),
        P(),
        P(None, None, "mp"),
        P(None, "mp"),
        P(None, "mp", None),
        P(),
        P(None, None, "mp"),
        P("mp"),
        P(),
        P(),
    )
    out_specs = P("mp", "order")
    return jax.shard_map(shards, mesh=mesh, in_specs=in_specs, out_specs=out_specs, check_vma=False)
```

profile of v0, /device:TPU:1, one launch (start us, length us, event | category | flops | bytes accessed | tf_op | source)
XLA Modules:
  0.0 1345.9 jit_solution(14749455091742322049)
XLA Ops:
  10.0 7.8 all-gather
  17.9 5.4 all-gather.1
  24.5 103.9 %while.30 = (s32[]{:T(128)}, bf16[16,16,1024]{2,1,0:T(8,128)(2,1)S(1)}, bf16[16,3,16,1024]{3,2,1,0:T(8,128)(2,1)S(1)}, s32[]{:T(128)}, s32[]{:T(128)}, /*index=5*/s32[]{}, s32[]{}) while((s32[]{:T(128)}, bf16[16,16,1024]{2,1,0:T(8,128)(2,1)S(1)}, bf16[16,3,16,1024]{3,2,1,0:T(8,128)(2,1)S(1)}, s32[]{:T(128)}, s32[]{:T(128)}, /*index=5*/s32[]{}, ...), condition=%wide.region_9.10_spmd, body=%wide.region_6.0_spmd.sunk | while | flops 76560384 | bytes 29513864 | solution.py:69
  41.0 3.1 fusion.227
  47.4 3.1 fusion.227
  73.4 3.1 fusion.227
  79.9 3.1 fusion.227
  99.4 3.1 fusion.227
  105.9 3.1 fusion.227
  112.4 3.1 fusion.227
  129.0 5.4 all-gather.2
  137.3 47.7 %all-gather.10.cloned.1.call-done = f32[256,4096]{0,1:T(8,128)} async-done(((f32[256,1024]{0,1:T(8,128)}), f32[256,4096]{0,1:T(8,128)}) %all-gather.10.cloned.1.call-update) | async-done | bytes 4194320 | tf_op jit(solution)/shard_map/all_gather | solution.py:92
  190.8 13.4 convolution_bitcast_fusion
  205.1 9.2 reduce-window.6
  215.9 16.1 %scatter_custom_fusion = s32[8192]{0:T(1024)} fusion(s32[4096]{0:T(1024)S(1)} %compare_select_fusion.3, s32[4096]{0:T(1024)S(1)} %get-tuple-element.125, s32[]{:T(128)} %constant.82.clone.1), kind=kCustom, calls=%fused_computation.206 | custom fusion | bytes 32772 | tf_op jit(solution)/shard_map/scatter | solution.py:147
  232.0 9.1 all-to-all-start
  241.1 15.5 %scatter_custom_fusion.1 = s32[8192]{0:T(1024)S(1)} fusion(s32[4096]{0:T(1024)S(1)} %compare_select_fusion.3, s32[4096]{0:T(1024)S(1)} %iota.11, s32[]{:T(128)} %constant.82.clone.1), kind=kCustom, calls=%fused_computation.204 | custom fusion | bytes 32772 | tf_op jit(solution)/shard_map/scatter | solution.py:145
  257.3 39.9 %all-reduce.3.cloned.1.call-done = f32[256,4096]{0,1:T(8,128)} async-done(((f32[256,4096]{0,1:T(8,128)}), f32[256,4096]{0,1:T(8,128)}) %all-reduce.3.cloned.1.call-update) | async-done | bytes 4194320 | tf_op jit(solution)/shard_map/psum | solution.py:43
  297.1 4.0 add_add_fusion
  303.3 33.5 %gather_fusion.1 = f32[8192,256]{1,0:T(8,128)} fusion(f32[256,4097]{0,1:T(8,128)} %concatenate.6, s32[8192]{0:T(1024)S(1)} %fusion.136), kind=kCustom, calls=%fused_computation.1 | custom fusion | bytes 16809984 | tf_op jit(solution)/shard_map/gather | solution.py:150
  336.9 9.2 all-to-all-start.1
  346.2 123.1 %all-to-all-done.1 = f32[256,32,256]{0,2,1:T(8,128)} async-done(((f32[256,32,256]{0,2,1:T(8,128)}), f32[256,32,256]{0,2,1:T(8,128)}, u32[]{:S(2)}, u32[]{:S(2)}) %all-to-all-start.1) | async-done | bytes 8388640 | tf_op jit(solution)/shard_map/all_to_all | solution.py:152
  469.3 36.7 %scatter_custom_fusion.2 = f32[256,4097]{0,1:T(8,128)} fusion(s32[8192]{0:T(1024)S(1)} %bitcast.327, f32[8192,256]{1,0:T(8,128)} %bitcast.40, f32[]{:T(128)} %constant.52.clone.1), kind=kCustom, calls=%fused_computation.105 | custom fusion | bytes 4195840 | tf_op jit(solution)/shard_map/scatter | solution.py:160
  506.1 4.4 slice.154
  510.5 5.6 copy.66
  518.6 6.9 collective-permute-start
  527.7 4.3 collective-permute-done.1
  533.8 3.1 copy.52
  537.1 548.4 %while.31 = (s32[]{:T(128)}, f32[64,4096]{1,0:T(8,128)S(1)}, bf16[27,256,64]{1,2,0:T(8,128)(2,1)}, s32[27,4096]{1,0:T(8,128)}, bf16[256,4353]{0,1:T(8,128)(2,1)S(1)}, /*index=5*/s32[]{:T(128)}) while((s32[]{:T(128)}, f32[64,4096]{1,0:T(8,128)S(1)}, bf16[27,256,64]{1,2,0:T(8,128)(2,1)}, s32[27,4096]{1,0:T(8,128)}, ...), condition=%wide.region_16.17_spmd, body=%wide.region_15.16_spmd.sunk | while | flops 134496256 | bytes 8503881 | solution.py:183
  538.0 17.0 %gather_fusion = bf16[4096,256]{1,0:T(8,128)(2,1)} fusion(bf16[256,4353]{0,1:T(8,128)(2,1)S(1)} %get-tuple-element.261, s32[4096]{0:T(1024)S(1)} %broadcast_clamp_fusion.2), kind=kCustom, calls=%fused_computation.clone.1 | custom fusion | bytes 4210688 | tf_op jit(solution)/shard_map/while/body/eval_jaxpr/gather | solution.py:177
  558.4 17.0 %gather_fusion = bf16[4096,256]{1,0:T(8,128)(2,1)} fusion(bf16[256,4353]{0,1:T(8,128)(2,1)S(1)} %get-tuple-element.261, s32[4096]{0:T(1024)S(1)} %broadcast_clamp_fusion.2), kind=kCustom, calls=%fused_computation.clone.1 | custom fusion | bytes 4210688 | tf_op jit(solution)/shard_map/while/body/eval_jaxpr/gather | solution.py:177
  578.7 17.0 %gather_fusion = bf16[4096,256]{1,0:T(8,128)(2,1)} fusion(bf16[256,4353]{0,1:T(8,128)(2,1)S(1)} %get-tuple-element.261, s32[4096]{0:T(1024)S(1)} %broadcast_clamp_fusion.2), kind=kCustom, calls=%fused_computation.clone.1 | custom fusion | bytes 4210688 | tf_op jit(solution)/shard_map/while/body/eval_jaxpr/gather | solution.py:177
  599.0 17.0 %gather_fusion = bf16[4096,256]{1,0:T(8,128)(2,1)} fusion(bf16[256,4353]{0,1:T(8,128)(2,1)S(1)} %get-tuple-element.261, s32[4096]{0:T(1024)S(1)} %broadcast_clamp_fusion.2), kind=kCustom, calls=%fused_computation.clone.1 | custom fusion | bytes 4210688 | tf_op jit(solution)/shard_map/while/body/eval_jaxpr/gather | solution.py:177
  619.3 17.0 %gather_fusion = bf16[4096,256]{1,0:T(8,128)(2,1)} fusion(bf16[256,4353]{0,1:T(8,128)(2,1)S(1)} %get-tuple-element.261, s32[4096]{0:T(1024)S(1)} %broadcast_clamp_fusion.2), kind=kCustom, calls=%fused_computation.clone.1 | custom fusion | bytes 4210688 | tf_op jit(solution)/shard_map/while/body/eval_jaxpr/gather | solution.py:177
  639.6 17.0 %gather_fusion = bf16[4096,256]{1,0:T(8,128)(2,1)} fusion(bf16[256,4353]{0,1:T(8,128)(2,1)S(1)} %get-tuple-element.261, s32[4096]{0:T(1024)S(1)} %broadcast_clamp_fusion.2), kind=kCustom, calls=%fused_computation.clone.1 | custom fusion | bytes 4210688 | tf_op jit(solution)/shard_map/while/body/eval_jaxpr/gather | solution.py:177
  659.9 17.0 %gather_fusion = bf16[4096,256]{1,0:T(8,128)(2,1)} fusion(bf16[256,4353]{0,1:T(8,128)(2,1)S(1)} %get-tuple-element.261, s32[4096]{0:T(1024)S(1)} %broadcast_clamp_fusion.2), kind=kCustom, calls=%fused_computation.clone.1 | custom fusion | bytes 4210688 | tf_op jit(solution)/shard_map/while/body/eval_jaxpr/gather | solution.py:177
  680.2 17.0 %gather_fusion = bf16[4096,256]{1,0:T(8,128)(2,1)} fusion(bf16[256,4353]{0,1:T(8,128)(2,1)S(1)} %get-tuple-element.261, s32[4096]{0:T(1024)S(1)} %broadcast_clamp_fusion.2), kind=kCustom, calls=%fused_computation.clone.1 | custom fusion | bytes 4210688 | tf_op jit(solution)/shard_map/while/body/eval_jaxpr/gather | solution.py:177
  700.5 17.0 %gather_fusion = bf16[4096,256]{1,0:T(8,128)(2,1)} fusion(bf16[256,4353]{0,1:T(8,128)(2,1)S(1)} %get-tuple-element.261, s32[4096]{0:T(1024)S(1)} %broadcast_clamp_fusion.2), kind=kCustom, calls=%fused_computation.clone.1 | custom fusion | bytes 4210688 | tf_op jit(solution)/shard_map/while/body/eval_jaxpr/gather | solution.py:177
  720.8 17.0 %gather_fusion = bf16[4096,256]{1,0:T(8,128)(2,1)} fusion(bf16[256,4353]{0,1:T(8,128)(2,1)S(1)} %get-tuple-element.261, s32[4096]{0:T(1024)S(1)} %broadcast_clamp_fusion.2), kind=kCustom, calls=%fused_computation.clone.1 | custom fusion | bytes 4210688 | tf_op jit(solution)/shard_map/while/body/eval_jaxpr/gather | solution.py:177
  741.2 17.0 %gather_fusion = bf16[4096,256]{1,0:T(8,128)(2,1)} fusion(bf16[256,4353]{0,1:T(8,128)(2,1)S(1)} %get-tuple-element.261, s32[4096]{0:T(1024)S(1)} %broadcast_clamp_fusion.2), kind=kCustom, calls=%fused_computation.clone.1 | custom fusion | bytes 4210688 | tf_op jit(solution)/shard_map/while/body/eval_jaxpr/gather | solution.py:177
  761.5 17.0 %gather_fusion = bf16[4096,256]{1,0:T(8,128)(2,1)} fusion(bf16[256,4353]{0,1:T(8,128)(2,1)S(1)} %get-tuple-element.261, s32[4096]{0:T(1024)S(1)} %broadcast_clamp_fusion.2), kind=kCustom, calls=%fused_computation.clone.1 | custom fusion | bytes 4210688 | tf_op jit(solution)/shard_map/while/body/eval_jaxpr/gather | solution.py:177
  781.8 17.0 %gather_fusion = bf16[4096,256]{1,0:T(8,128)(2,1)} fusion(bf16[256,4353]{0,1:T(8,128)(2,1)S(1)} %get-tuple-element.261, s32[4096]{0:T(1024)S(1)} %broadcast_clamp_fusion.2), kind=kCustom, calls=%fused_computation.clone.1 | custom fusion | bytes 4210688 | tf_op jit(solution)/shard_map/while/body/eval_jaxpr/gather | solution.py:177
  802.1 17.0 %gather_fusion = bf16[4096,256]{1,0:T(8,128)(2,1)} fusion(bf16[256,4353]{0,1:T(8,128)(2,1)S(1)} %get-tuple-element.261, s32[4096]{0:T(1024)S(1)} %broadcast_clamp_fusion.2), kind=kCustom, calls=%fused_computation.clone.1 | custom fusion | bytes 4210688 | tf_op jit(solution)/shard_map/while/body/eval_jaxpr/gather | solution.py:177
  822.4 17.0 %gather_fusion = bf16[4096,256]{1,0:T(8,128)(2,1)} fusion(bf16[256,4353]{0,1:T(8,128)(2,1)S(1)} %get-tuple-element.261, s32[4096]{0:T(1024)S(1)} %broadcast_clamp_fusion.2), kind=kCustom, calls=%fused_computation.clone.1 | custom fusion | bytes 4210688 | tf_op jit(solution)/shard_map/while/body/eval_jaxpr/gather | solution.py:177
  842.7 17.0 %gather_fusion = bf16[4096,256]{1,0:T(8,128)(2,1)} fusion(bf16[256,4353]{0,1:T(8,128)(2,1)S(1)} %get-tuple-element.261, s32[4096]{0:T(1024)S(1)} %broadcast_clamp_fusion.2), kind=kCustom, calls=%fused_computation.clone.1 | custom fusion | bytes 4210688 | tf_op jit(solution)/shard_map/while/body/eval_jaxpr/gather | solution.py:177
  863.0 17.0 %gather_fusion = bf16[4096,256]{1,0:T(8,128)(2,1)} fusion(bf16[256,4353]{0,1:T(8,128)(2,1)S(1)} %get-tuple-element.261, s32[4096]{0:T(1024)S(1)} %broadcast_clamp_fusion.2), kind=kCustom, calls=%fused_computation.clone.1 | custom fusion | bytes 4210688 | tf_op jit(solution)/shard_map/while/body/eval_jaxpr/gather | solution.py:177
  883.3 17.0 %gather_fusion = bf16[4096,256]{1,0:T(8,128)(2,1)} fusion(bf16[256,4353]{0,1:T(8,128)(2,1)S(1)} %get-tuple-element.261, s32[4096]{0:T(1024)S(1)} %broadcast_clamp_fusion.2), kind=kCustom, calls=%fused_computation.clone.1 | custom fusion | bytes 4210688 | tf_op jit(solution)/shard_map/while/body/eval_jaxpr/gather | solution.py:177
  903.6 17.0 %gather_fusion = bf16[4096,256]{1,0:T(8,128)(2,1)} fusion(bf16[256,4353]{0,1:T(8,128)(2,1)S(1)} %get-tuple-element.261, s32[4096]{0:T(1024)S(1)} %broadcast_clamp_fusion.2), kind=kCustom, calls=%fused_computation.clone.1 | custom fusion | bytes 4210688 | tf_op jit(solution)/shard_map/while/body/eval_jaxpr/gather | solution.py:177
  924.0 17.0 %gather_fusion = bf16[4096,256]{1,0:T(8,128)(2,1)} fusion(bf16[256,4353]{0,1:T(8,128)(2,1)S(1)} %get-tuple-element.261, s32[4096]{0:T(1024)S(1)} %broadcast_clamp_fusion.2), kind=kCustom, calls=%fused_computation.clone.1 | custom fusion | bytes 4210688 | tf_op jit(solution)/shard_map/while/body/eval_jaxpr/gather | solution.py:177
  944.3 17.0 %gather_fusion = bf16[4096,256]{1,0:T(8,128)(2,1)} fusion(bf16[256,4353]{0,1:T(8,128)(2,1)S(1)} %get-tuple-element.261, s32[4096]{0:T(1024)S(1)} %broadcast_clamp_fusion.2), kind=kCustom, calls=%fused_computation.clone.1 | custom fusion | bytes 4210688 | tf_op jit(solution)/shard_map/while/body/eval_jaxpr/gather | solution.py:177
  964.6 17.0 %gather_fusion = bf16[4096,256]{1,0:T(8,128)(2,1)} fusion(bf16[256,4353]{0,1:T(8,128)(2,1)S(1)} %get-tuple-element.261, s32[4096]{0:T(1024)S(1)} %broadcast_clamp_fusion.2), kind=kCustom, calls=%fused_computation.clone.1 | custom fusion | bytes 4210688 | tf_op jit(solution)/shard_map/while/body/eval_jaxpr/gather | solution.py:177
  984.9 17.0 %gather_fusion = bf16[4096,256]{1,0:T(8,128)(2,1)} fusion(bf16[256,4353]{0,1:T(8,128)(2,1)S(1)} %get-tuple-element.261, s32[4096]{0:T(1024)S(1)} %broadcast_clamp_fusion.2), kind=kCustom, calls=%fused_computation.clone.1 | custom fusion | bytes 4210688 | tf_op jit(solution)/shard_map/while/body/eval_jaxpr/gather | solution.py:177
  1005.2 17.0 %gather_fusion = bf16[4096,256]{1,0:T(8,128)(2,1)} fusion(bf16[256,4353]{0,1:T(8,128)(2,1)S(1)} %get-tuple-element.261, s32[4096]{0:T(1024)S(1)} %broadcast_clamp_fusion.2), kind=kCustom, calls=%fused_computation.clone.1 | custom fusion | bytes 4210688 | tf_op jit(solution)/shard_map/while/body/eval_jaxpr/gather | solution.py:177
  1025.5 17.0 %gather_fusion = bf16[4096,256]{1,0:T(8,128)(2,1)} fusion(bf16[256,4353]{0,1:T(8,128)(2,1)S(1)} %get-tuple-element.261, s32[4096]{0:T(1024)S(1)} %broadcast_clamp_fusion.2), kind=kCustom, calls=%fused_computation.clone.1 | custom fusion | bytes 4210688 | tf_op jit(solution)/shard_map/while/body/eval_jaxpr/gather | solution.py:177
  1045.8 17.0 %gather_fusion = bf16[4096,256]{1,0:T(8,128)(2,1)} fusion(bf16[256,4353]{0,1:T(8,128)(2,1)S(1)} %get-tuple-element.261, s32[4096]{0:T(1024)S(1)} %broadcast_clamp_fusion.2), kind=kCustom, calls=%fused_computation.clone.1 | custom fusion | bytes 4210688 | tf_op jit(solution)/shard_map/while/body/eval_jaxpr/gather | solution.py:177
  1066.1 17.0 %gather_fusion = bf16[4096,256]{1,0:T(8,128)(2,1)} fusion(bf16[256,4353]{0,1:T(8,128)(2,1)S(1)} %get-tuple-element.261, s32[4096]{0:T(1024)S(1)} %broadcast_clamp_fusion.2), kind=kCustom, calls=%fused_computation.clone.1 | custom fusion | bytes 4210688 | tf_op jit(solution)/shard_map/while/body/eval_jaxpr/gather | solution.py:177
  1086.6 8.8 all-gather.4
  1095.5 5.6 all-gather.5
  1101.1 6.7 all-gather.3
  1107.9 19.7 %all-gather.12.cloned.1.call-done = bf16[256,4096]{1,0:T(8,128)(2,1)} async-done(((bf16[64,4096]{1,0:T(8,128)(2,1)}), bf16[256,4096]{1,0:T(8,128)(2,1)}) %all-gather.12.cloned.1.call-update) | async-done | bytes 2097168 | tf_op jit(solution)/shard_map/all_gather | solution.py:185
  1134.1 103.9 %while.32 = (s32[]{:T(128)}, bf16[16,16,1024]{2,1,0:T(8,128)(2,1)S(1)}, bf16[16,3,16,1024]{3,2,1,0:T(8,128)(2,1)S(1)}, s32[]{:T(128)}, s32[]{:T(128)}, /*index=5*/s32[]{}, s32[]{}) while((s32[]{:T(128)}, bf16[16,16,1024]{2,1,0:T(8,128)(2,1)S(1)}, bf16[16,3,16,1024]{3,2,1,0:T(8,128)(2,1)S(1)}, s32[]{:T(128)}, s32[]{:T(128)}, /*index=5*/s32[]{}, ...), condition=%wide.region_24.25_spmd, body=%wide.region_21.24_spmd.sunk | while | flops 76560384 | bytes 29513864 | solution.py:69
  1239.6 49.3 %all-gather.14.cloned.1.call-done = f32[256,4096]{1,0:T(8,128)} async-done(((f32[256,1024]{1,0:T(8,128)}), f32[256,4096]{1,0:T(8,128)}) %all-gather.14.cloned.1.call-update) | async-done | bytes 4194320 | tf_op jit(solution)/shard_map/all_gather | solution.py:92
  1294.0 13.4 fusion.21
  1307.6 29.0 %reduce-scatter.2.cloned.1.call-done = bf16[64,4096]{1,0:T(8,128)(2,1)} async-done(((bf16[256,4096]{1,0:T(8,128)(2,1)}), bf16[64,4096]{1,0:T(8,128)(2,1)}) %reduce-scatter.2.cloned.1.call-update) | async-done | bytes 524304 | tf_op jit(solution)/shard_map/reduce_scatter | solution.py:116
  (364 shorter events, 318.0 us)
Async XLA Ops:
  6.5 1121.0 %copy-start = (bf16[256,256]{1,0:T(8,128)(2,1)S(1)}, bf16[256,256]{1,0:T(8,128)(2,1)}, u32[]{:S(2)}) copy-start(bf16[256,256]{1,0:T(8,128)(2,1)} %param.38) | copy-start | bytes 393220
  6.5 2.3 copy-start.14
  6.5 2.9 copy-start.15
  6.5 3.4 copy-start.4
  6.5 11.3 copy-start.7
  6.5 178.5 %all-gather.10.cloned.1.call-start = ((), (), s32[]{:S(2)}) async-start(), calls=%async_computation.3 | async-start | bytes 5242880 | tf_op jit(solution)/shard_map/all_gather | solution.py:92
  24.5 103.9 %copy-start.5 = (bf16[2,64,256]{2,1,0:T(8,128)(2,1)S(1)}, bf16[2,64,256]{2,1,0:T(8,128)(2,1)}, u32[]{:S(2)}) copy-start(bf16[2,64,256]{2,1,0:T(8,128)(2,1)} %param.30) | copy-start | bytes 196612
  24.5 110.0 %copy-start.11 = (bf16[2,256]{1,0:T(2,128)(2,1)S(1)}, bf16[2,256]{1,0:T(2,128)(2,1)}, u32[]{:S(2)}) copy-start(bf16[2,256]{1,0:T(2,128)(2,1)} %param.31) | copy-start | bytes 3076
  24.5 112.2 %copy-start.12 = (bf16[2,256]{1,0:T(2,128)(2,1)S(1)}, bf16[2,256]{1,0:T(2,128)(2,1)}, u32[]{:S(2)}) copy-start(bf16[2,256]{1,0:T(2,128)(2,1)} %param.33) | copy-start | bytes 3076
  25.3 1.9 copy-start.1
  31.8 1.9 copy-start.1
  38.3 1.9 copy-start.1
  44.8 1.9 copy-start.1
  51.3 1.9 copy-start.1
  57.8 1.9 copy-start.1
  64.3 1.9 copy-start.1
  70.7 1.9 copy-start.1
  77.2 1.9 copy-start.1
  83.7 1.9 copy-start.1
  90.2 1.9 copy-start.1
  96.7 1.9 copy-start.1
  103.2 1.9 copy-start.1
  109.7 1.9 copy-start.1
  116.2 1.9 copy-start.1
  122.7 1.9 copy-start.1
  136.4 160.7 %all-reduce.3.cloned.1.call-start = ((), (), s32[]{:S(2)}) async-start(), calls=%async_computation.4 | async-start | bytes 8388608 | tf_op jit(solution)/shard_map/psum | solution.py:43
  137.3 53.5 %copy-start.23 = (bf16[2,256,256]{2,1,0:T(8,128)(2,1)S(1)}, bf16[2,256,256]{2,1,0:T(8,128)(2,1)}, u32[]{:S(2)}) copy-start(bf16[2,256,256]{2,1,0:T(8,128)(2,1)} %param.34) | copy-start | bytes 786436
  137.3 53.5 %copy-start.25 = (bf16[2,256,256]{2,1,0:T(8,128)(2,1)S(1)}, bf16[2,256,256]{2,1,0:T(8,128)(2,1)}, u32[]{:S(2)}) copy-start(bf16[2,256,256]{2,1,0:T(8,128)(2,1)} %param.32) | copy-start | bytes 786436
  204.3 52.4 %copy-start.13 = (bf16[2,256]{1,0:T(2,128)(2,1)S(1)}, bf16[2,256]{1,0:T(2,128)(2,1)}, u32[]{:S(2)}) copy-start(bf16[2,256]{1,0:T(2,128)(2,1)} %param.35) | copy-start | bytes 3076
  232.0 104.9 %all-to-all-start = ((s32[1,32,256]{2,0,1:T(1,128)}), s32[1,32,256]{2,0,1:T(1,128)S(1)}, u32[]{:S(2)}, u32[]{:S(2)}) async-start(s32[1,32,256]{2,0,1:T(1,128)} %bitcast.13), calls=%async_computation | async-start | bytes 65536 | tf_op jit(solution)/shard_map/all_to_all | solution.py:153
  336.9 132.5 %all-to-all-start.1 = ((f32[256,32,256]{0,2,1:T(8,128)}), f32[256,32,256]{0,2,1:T(8,128)}, u32[]{:S(2)}, u32[]{:S(2)}) async-start(f32[256,32,256]{0,2,1:T(8,128)} %bitcast.315), calls=%async_computation.1 | async-start | bytes 16777216 | tf_op jit(solution)/shard_map/all_to_all | solution.py:152
  346.1 781.5 %all-gather.12.cloned.1.call-start = ((), (), s32[]{:S(2)}) async-start(), calls=%async_computation.5 | async-start | bytes 2621440 | tf_op jit(solution)/shard_map/all_gather | solution.py:185
  516.1 10.8 copy-start.3
  518.6 9.1 collective-permute-start
  525.5 6.5 collective-permute-start.1
  527.7 9.2 copy-start.22
  537.1 549.3 %copy-start.27 = (bf16[256]{0:T(256)(128)(2,1)S(1)}, bf16[256]{0:T(256)(128)(2,1)}, u32[]{:S(2)}) copy-start(bf16[256]{0:T(256)(128)(2,1)} %param.39) | copy-start | bytes 1540
  1086.4 202.5 %all-gather.14.cloned.1.call-start = ((), (), s32[]{:S(2)}) async-start(), calls=%async_computation.6 | async-start | bytes 5242880 | tf_op jit(solution)/shard_map/all_gather | solution.py:92
  1131.5 1.6 copy-start.18
  1131.5 1.6 copy-start.19
  1134.0 103.9 %copy-start.8 = (f32[1,256]{1,0:T(1,128)S(1)}, f32[1,256]{1,0:T(1,128)}, u32[]{:S(2)}) copy-start(f32[1,256]{1,0:T(1,128)} %get-tuple-element.143) | copy-start | bytes 3076
  1134.8 1.9 copy-start.2
  1141.3 1.9 copy-start.2
  1147.8 1.9 copy-start.2
  1154.3 1.9 copy-start.2
  1160.8 1.9 copy-start.2
  1167.3 1.9 copy-start.2
  1173.8 1.9 copy-start.2
  1180.3 1.9 copy-start.2
  1186.8 1.9 copy-start.2
  1193.3 1.9 copy-start.2
  1199.8 1.9 copy-start.2
  1206.3 1.9 copy-start.2
  1212.8 1.9 copy-start.2
  1219.2 1.9 copy-start.2
  1225.7 1.9 copy-start.2
  1232.2 1.9 copy-start.2
  1239.3 54.7 %copy-start.16 = (f32[1,256]{1,0:T(1,128)S(1)}, f32[1,256]{1,0:T(1,128)}, u32[]{:S(2)}) copy-start(f32[1,256]{1,0:T(1,128)} %get-tuple-element.127) | copy-start | bytes 3076
  1239.3 54.7 %copy-start.17 = (f32[1,256]{1,0:T(1,128)S(1)}, f32[1,256]{1,0:T(1,128)}, u32[]{:S(2)}) copy-start(f32[1,256]{1,0:T(1,128)} %get-tuple-element.132) | copy-start | bytes 3076
  1239.3 54.7 %copy-start.20 = (f32[1,256]{1,0:T(1,128)S(1)}, f32[1,256]{1,0:T(1,128)}, u32[]{:S(2)}) copy-start(f32[1,256]{1,0:T(1,128)} %get-tuple-element.141) | copy-start | bytes 3076
  1239.3 54.7 %copy-start.24 = (bf16[2,256,256]{2,1,0:T(8,128)(2,1)S(1)}, bf16[2,256,256]{2,1,0:T(8,128)(2,1)}, u32[]{:S(2)}) copy-start(bf16[2,256,256]{2,1,0:T(8,128)(2,1)} %param.34) | copy-start | bytes 786436
  1239.4 54.7 %copy-start.26 = (bf16[2,256,256]{2,1,0:T(8,128)(2,1)S(1)}, bf16[2,256,256]{2,1,0:T(8,128)(2,1)}, u32[]{:S(2)}) copy-start(bf16[2,256,256]{2,1,0:T(8,128)(2,1)} %param.32) | copy-start | bytes 786436
  1239.4 97.2 %reduce-scatter.2.cloned.1.call-start = ((), (), s32[]{:S(2)}) async-start(), calls=%async_computation.7 | async-start | bytes 2621440 | tf_op jit(solution)/shard_map/reduce_scatter | solution.py:116
  1294.0 13.5 %copy-start.21 = (bf16[1,256]{1,0:T(2,128)(2,1)S(1)}, bf16[1,256]{1,0:T(2,128)(2,1)}, u32[]{:S(2)}) copy-start(bf16[1,256]{1,0:T(2,128)(2,1)} %get-tuple-element.139) | copy-start | bytes 1540
  (3 other events, 2.0 us)
Sparse Core Ops, SparseCore 0:
  136.5 48.5 all-gather.9
  204.4 92.6 all-reduce.2
  1086.5 41.0 all-gather.11
  1239.4 49.4 all-gather.13
  1307.6 28.9 reduce-scatter.1
where the time goes:
time: 1350 us
  local copies, waits for them, and re-layouts  642 us (48%)
  waiting for transfers between devices  313 us (23%)
  matrix products  220 us (16%)
  other arithmetic  88.8 us (7%)
  blocking collectives  39.8 us (3%)
  starting transfers between devices  27.2 us (2%)
  between operations  14 us (1%)
    gather x27, local copies, waits for them, and re-layouts, offset_step(): return (running + contract(kernel, widened[:, picked]), None)  458 us
    all_to_all x1, waiting for transfers between devices, relay_rows(): lax.all_to_all(packed, 'order', split_axis=1, concat_axis=1, tiled=True)  123 us
    dot_general x32, matrix products, single(): jnp.einsum('qk,dk->dq', chances, triple[2], preferred_element_type=jnp.fl...  97.8 us
    all_gather x2, waiting for transfers between devices, attend(): return lax.all_gather(own_rows, 'mp', axis=1, tiled=True)  97 us
    dot_general x32, matrix products, contract(): lax.dot_general(left_side, right_side, (((0,), (0,)), ((), ())), preferre...  96.3 us
    while x64, local copies, waits for them, and re-layouts  61.6 us
    psum x1, waiting for transfers between devices, add_heads(): return lax.psum(partial_value, 'mp')  39.9 us
    scatter x1, local copies, waits for them, and re-layouts, relay_rows(): placed = jnp.zeros((feature_rows, tokens + 1), jnp.float32).at[:, landing...  36.7 us
  transfers between devices with their start and end apart: 9, of which 7 were waited for; matrix products, arithmetic and copies ran while one was open for 6% of the time, Pallas kernels for 0%

commit v1 on v0

v1 whole, which is shorter than its diff:
```python
import functools
import math

import jax
import jax.numpy as jnp
from jax import lax
from jax.experimental import pallas as pl
from jax.experimental.pallas import tpu as pltpu
from jax.sharding import PartitionSpec as P

C = 256
PATCH = 1024
HALO = 128
HDIM = 16
HEADS = 16
OFFS = 27
TOK = 4096
SLOTS = 64
CAP = 288
EPS = 1e-05
LOG2E = math.log2(math.e)
f32, bf16, i32 = jnp.float32, jnp.bfloat16, jnp.int32
VMEM = pl.BlockSpec(memory_space=pltpu.VMEM)
SMEM = pl.BlockSpec(memory_space=pltpu.SMEM)
ANY = pl.BlockSpec(memory_space=pl.ANY)
S = jax.ShapeDtypeStruct
COL_GAIN, COL_SHIFT, COL_PROJ, COL_FC2, COL_QKV, COL_FC1, COL_CONV, COL_CPE = 0, 5, 10, 12, 14, 20, 28, 29


def kernel_params(**more):
    return pltpu.CompilerParams(vmem_limit_bytes=56 * 2**20, **more)


def iota(shape, dim):
    return lax.broadcasted_iota(i32, shape, dim)


def one_hot(left, right):
    return jnp.where(left == right, 1.0, 0.0).astype(bf16)


def dot(left, right):
    return jnp.dot(left, right, preferred_element_type=f32)


def norm_columns(values, gain, shift):
    average = jnp.mean(values, axis=0, keepdims=True)
    centred = values - average
    variance = jnp.mean(centred * centred, axis=0, keepdims=True)
    return centred * lax.rsqrt(variance + EPS) * gain + shift


def send_map_kernel(rank_ref, src_ref, pos_ref, oh_ref, prefix_ref):
    member = lax.axis_index("mp")
    chunks = TOK // 128
    rank = rank_ref[...]
    by_lane = jnp.concatenate([rank, jnp.zeros((128 - chunks, 128), i32)], axis=0).T
    lower = jnp.where(iota((128, 128), 1) < iota((128, 128), 0), 1.0, 0.0).astype(bf16)
    lanes = iota((128, 128), 1)
    carry = jnp.zeros((1, 128), f32)
    for c in range(chunks):
        hot = jnp.where(by_lane[:, c : c + 1] // PATCH == lanes, 1.0, 0.0)
        oh_ref[c] = hot
        prefix_ref[c] = dot(lower, hot.astype(bf16)) + carry
        carry = carry + jnp.sum(hot, axis=0, keepdims=True)
    row, col = iota((128, 128), 0), iota((128, 128), 1)
    ahead = jnp.where((row // 4 == col // 4) & (row < col), 1.0, 0.0).astype(bf16)
    base = dot(jnp.broadcast_to(carry, (8, 128)).astype(bf16), ahead)[0:1]
    acc = jnp.zeros((160, 128), f32)
    slot_ids = iota((1, 128), 1) * 4 + member
    slot_ids = jnp.where(iota((1, 128), 1) < SLOTS, slot_ids, -1)
    lane_row = iota((1, 128), 1)
    for c in range(chunks):
        slot = jnp.sum(oh_ref[c] * (prefix_ref[c] + base), axis=1, keepdims=True).astype(i32)
        right = one_hot(slot, slot_ids)
        rank_row = rank[c : c + 1, :]
        owner = jnp.where(iota((32, 128), 0) == rank_row // TOK, 1.0, 0.0)
        spot = rank_row % TOK
        token = c * 128 + lane_row
        pieces = [token // 256, token % 256, spot // 256, spot % 256]
        left = jnp.concatenate([owner * piece.astype(f32) for piece in pieces] + [owner], axis=0)
        acc = acc + dot(left.astype(bf16), right)
    acc = acc[:, :SLOTS]
    src_ref[...] = (acc[0:32] * 256.0 + acc[32:64]).astype(i32)
    pos_ref[...] = jnp.where(
        acc[128:160] > 0.5, (acc[64:96] * 256.0 + acc[96:128]).astype(i32), TOK
    )


def send_map(rank):
    return pl.pallas_call(
        send_map_kernel,
        out_shape=[S((32, SLOTS), i32), S((32, SLOTS), i32)],
        in_specs=[VMEM],
        out_specs=[VMEM, VMEM],
        scratch_shapes=[pltpu.VMEM((32, 128, 128), f32), pltpu.VMEM((32, 128, 128), f32)],
        compiler_params=kernel_params(),
        name="send_map",
    )(rank)


def list_map_kernel(pos_ref, src_ref, place_ref):
    pos = pos_ref[...]
    wide = jnp.concatenate([pos, jnp.full((32, 128 - SLOTS), TOK, i32)], axis=1)
    wide = jnp.concatenate([wide, jnp.full((96, 128), TOK, i32)], axis=0)
    by_lane = wide.T[:SLOTS]
    lower = jnp.where(iota((SLOTS, SLOTS), 1) < iota((SLOTS, SLOTS), 0), 1.0, 0.0).astype(bf16)
    lanes = iota((SLOTS, 128), 1)
    carry = jnp.zeros((1, 128), f32)
    acc = jnp.zeros((40, 384), f32)
    unit = iota((1, SLOTS), 1)
    for i in range(32):
        hot = jnp.where(by_lane[:, i : i + 1] // PATCH == lanes, 1.0, 0.0)
        spot = jnp.sum(hot * (dot(lower, hot.astype(bf16)) + carry), axis=1, keepdims=True)
        carry = carry + jnp.sum(hot, axis=0, keepdims=True)
        right = one_hot(spot.astype(i32), iota((SLOTS, 384), 1))
        row = pos[i : i + 1, :]
        member = jnp.where(iota((8, SLOTS), 0) == row // PATCH, 1.0, 0.0)
        inside = row % PATCH
        pieces = [jnp.full((1, SLOTS), i, i32), unit, inside // 32, inside % 32]
        left = jnp.concatenate([member * p.astype(f32) for p in pieces] + [member], axis=0)
        acc = acc + dot(left.astype(bf16), right)
    acc = acc[:, :CAP]
    src_ref[...] = (acc[0:4] * float(SLOTS) + acc[8:12]).astype(i32)
    place_ref[...] = jnp.where(
        acc[32:36] > 0.5, (acc[16:20] * 32.0 + acc[24:28]).astype(i32), -1
    )


def list_map(pos):
    return pl.pallas_call(
        list_map_kernel,
        out_shape=[S((4, CAP), i32), S((4, CAP), i32)],
        in_specs=[VMEM],
        out_specs=[VMEM, VMEM],
        compiler_params=kernel_params(),
        name="list_map",
    )(pos)


def place_map_kernel(place_ref, src_ref):
    place = jnp.concatenate([place_ref[...], jnp.full((4, CAP), -1, i32)], axis=0)
    place = jnp.concatenate([place, jnp.full((8, 384 - CAP), -1, i32)], axis=1)
    acc = jnp.zeros((8, PATCH), f32)
    lane = iota((1, 384), 1)
    by_lane = place.T
    rows = iota((8, 384), 0)
    for q in range(4):
        right = one_hot(by_lane[:, q : q + 1], iota((384, PATCH), 1))
        entry = q * CAP + lane
        left = jnp.where(rows == 0, entry // 64, jnp.where(rows == 1, entry % 64, 0))
        acc = acc + dot(left.astype(f32).astype(bf16), right)
    src_ref[...] = (acc[0:1] * 64.0 + acc[1:2]).astype(i32)


def place_map(place):
    return pl.pallas_call(
        place_map_kernel,
        out_shape=S((1, PATCH), i32),
        in_specs=[VMEM],
        out_specs=VMEM,
        compiler_params=kernel_params(),
        name="place_map",
    )(place)


def pick_kernel(rows, width, index_ref, src_ref, out_ref):
    def step(i, carry):
        for u in range(16):
            r = i * 16 + u
            out_ref[r] = src_ref[index_ref[r // width, r % width]]
        return carry

    lax.fori_loop(0, rows // 16, step, 0)


def pick_rows(index, source, name):
    rows, width = index.shape[0] * index.shape[1], index.shape[1]
    return pl.pallas_call(
        functools.partial(pick_kernel, rows, width),
        out_shape=S((rows, 2, 128), f32),
        in_specs=[SMEM, VMEM],
        out_specs=VMEM,
        compiler_params=kernel_params(),
        name=name,
    )(index, source)


def land_kernel(index_ref, src_ref, moved_ref, low_ref, rows_ref):
    def step(i, carry):
        for u in range(16):
            r = i * 16 + u
            rows_ref[r] = src_ref[index_ref[0, r]]
        return carry

    lax.fori_loop(0, PATCH // 16, step, 0)
    for half in range(2):
        part = rows_ref[:, half, :].T
        moved_ref[half * 128 : half * 128 + 128, :] = part
        low_ref[half * 128 : half * 128 + 128, :] = part.astype(bf16)


def land_rows(index, source):
    return pl.pallas_call(
        land_kernel,
        out_shape=[S((C, PATCH), f32), S((C, PATCH), bf16)],
        in_specs=[SMEM, VMEM],
        out_specs=[VMEM, VMEM],
        scratch_shapes=[pltpu.VMEM((PATCH, 2, 128), f32)],
        compiler_params=kernel_params(),
        name="land",
    )(index, source)


def block_scratch():
    return [
        pltpu.VMEM((C, PATCH), bf16),
        pltpu.VMEM((3, C, PATCH), bf16),
        pltpu.VMEM((2, PATCH, 128), bf16),
        pltpu.VMEM((PATCH, PATCH), f32),
        pltpu.VMEM((PATCH, PATCH), f32),
        pltpu.VMEM((2, 8, PATCH), f32),
        pltpu.VMEM((C, PATCH), bf16),
    ]


def run_block(block, first_norm, x_ref, w_ref, cols_ref, scratch, emit):
    normed_ref, qkv_ref, keys_ref, s0_ref, s1_ref, top_ref, heads_ref = scratch

    def column(k):
        return cols_ref[:, k : k + 1]

    for c in range(4):
        span = slice(c * 256, c * 256 + 256)
        normed_ref[:, span] = norm_columns(
            x_ref[:, span], column(COL_GAIN + first_norm), column(COL_SHIFT + first_norm)
        ).astype(bf16)
    for r in range(4):
        made = dot(w_ref[r, 0:192, :], normed_ref[...])
        for j in range(3):
            bias = cols_ref[r * 64 : r * 64 + 64, COL_QKV + 3 * block + j : COL_QKV + 3 * block + j + 1]
            qkv_ref[j, r * 64 : r * 64 + 64, :] = (made[j * 64 : j * 64 + 64] + bias).astype(bf16)
    for g in range(2):
        keys_ref[g] = qkv_ref[1, g * 128 : g * 128 + 128, :].T

    head_of_row = iota((128, 1), 0) // HDIM
    buffers = (s0_ref, s1_ref)

    def scores(h, b):
        g = h // 8
        queries = qkv_ref[0, pl.ds(pl.multiple_of(g * 128, 128), 128), :]
        queries = jnp.where(head_of_row == h % 8, queries.astype(f32), 0.0).astype(bf16)
        s = dot(keys_ref[g], queries)
        buffers[b][...] = s
        top_ref[b, 0:1, :] = jnp.max(s, axis=0, keepdims=True)

    def finish(h, b):
        p = jnp.exp2((buffers[b][...] - top_ref[b, 0:1, :]) * (0.25 * LOG2E))
        inverse = 1.0 / jnp.sum(p, axis=0, keepdims=True)
        chances = (p * inverse).astype(bf16)
        rows = pl.ds(pl.multiple_of(h * HDIM, HDIM), HDIM)
        heads_ref[rows, :] = dot(qkv_ref[2, rows, :], chances).astype(bf16)

    scores(0, 0)

    def pair(j, carry):
        h = 2 * j
        scores(h + 1, 1)
        finish(h, 0)
        scores(jnp.minimum(h + 2, HEADS - 1), 0)
        finish(h + 1, 1)
        return carry

    lax.fori_loop(0, HEADS // 2, pair, 0)

    proj = [w_ref[r, 192:256, :].T for r in range(4)]
    for c in range(4):
        span = slice(c * 256, c * 256 + 256)
        mixed = dot(proj[0], heads_ref[0:64, span])
        for r in range(1, 4):
            mixed = mixed + dot(proj[r], heads_ref[r * 64 : r * 64 + 64, span])
        attended = x_ref[:, span] + (mixed + column(COL_PROJ + block))
        normed = norm_columns(
            attended, column(COL_GAIN + first_norm + 1), column(COL_SHIFT + first_norm + 1)
        ).astype(bf16)
        total = None
        for r in range(4):
            hidden = dot(w_ref[r, 256:512, :], normed) + column(COL_FC1 + 4 * block + r)
            hidden = 0.5 * hidden * (1.0 + lax.erf(hidden * math.sqrt(0.5)))
            part = dot(w_ref[r, 512:768, :], hidden.astype(bf16))
            total = part if total is None else total + part
        emit(c, attended + (total + column(COL_FC2 + block)))


def first_kernel(feats_ref, w_ref, cols_ref, out_ref, x_ref, sem, *scratch):
    start = pl.multiple_of(lax.axis_index("mp") * PATCH, PATCH)
    copy = pltpu.make_async_copy(feats_ref.at[:, pl.ds(start, PATCH)], x_ref, sem)
    copy.start()
    copy.wait()

    def emit(c, value):
        rows = value.T
        for half in range(2):
            out_ref[c * 256 : c * 256 + 256, half, :] = rows[:, half * 128 : half * 128 + 128]

    run_block(0, 0, x_ref, w_ref, cols_ref, scratch, emit)


def first_block(feats, weights, cols):
    return pl.pallas_call(
        first_kernel,
        out_shape=S((PATCH, 2, 128), f32),
        in_specs=[ANY, VMEM, VMEM],
        out_specs=VMEM,
        scratch_shapes=[pltpu.VMEM((C, PATCH), f32), pltpu.SemaphoreType.DMA] + block_scratch(),
        compiler_params=kernel_params(),
        name="first_block",
    )(feats, weights, cols)


def second_kernel(
    wide_ref, moved_ref, near_ref, conv_ref, cpe_ref, w_ref, cols_ref, out_ref,
    x_ref, index_ref, picked_ref, sem, *scratch
):
    member, group = lax.axis_index("mp"), lax.axis_index("order")
    start = pl.multiple_of(member * PATCH, PATCH)
    copy = pltpu.make_async_copy(near_ref.at[:, pl.ds(start, PATCH)], index_ref, sem)
    copy.start()
    copy.wait()
    first_token = group * TOK + member * PATCH

    def column(k):
        return cols_ref[:, k : k + 1]

    cpe = cpe_ref[...].T
    places = iota((512, 256), 0)
    for c in range(4):
        span = slice(c * 256, c * 256 + 256)
        window = wide_ref[:, c * 256 : c * 256 + 512]
        origin = first_token + c * 256 - HALO

        def pick(k, carry):
            near = index_ref[pl.ds(k, 1), span]
            near = jnp.where(near < 0, -1, near - origin)
            rows = pl.ds(pl.multiple_of(k * C, C), C)
            picked_ref[rows, :] = dot(window, one_hot(places, near)).astype(bf16)
            return carry

        lax.fori_loop(0, OFFS, pick, 0, unroll=3)
        conv = (dot(conv_ref[...], picked_ref[...]) + column(COL_CONV)).astype(bf16)
        mixture = dot(cpe, conv) + column(COL_CPE)
        x_ref[:, span] = moved_ref[:, span] + norm_columns(
            mixture, column(COL_GAIN + 2), column(COL_SHIFT + 2)
        )

    def emit(c, value):
        out_ref[:, c * 256 : c * 256 + 256] = value

    run_block(1, 3, x_ref, w_ref, cols_ref, scratch, emit)


def second_block(wide, moved, neighbours, conv, cpe, weights, cols):
    return pl.pallas_call(
        second_kernel,
        out_shape=S((C, PATCH), f32),
        in_specs=[VMEM, VMEM, ANY, VMEM, VMEM, VMEM, VMEM],
        out_specs=VMEM,
        scratch_shapes=[
            pltpu.VMEM((C, PATCH), f32),
            pltpu.VMEM((OFFS, PATCH), i32),
            pltpu.VMEM((OFFS * C, 256), bf16),
            pltpu.SemaphoreType.DMA,
        ]
        + block_scratch(),
        compiler_params=kernel_params(),
        name="second_block",
    )(wide, moved, neighbours, conv, cpe, weights, cols)


def shards(
    feats, serial_rank, neighbours, norm_gain, norm_bias, qkv_weight, qkv_bias, proj_weight, proj_bias,
    fc1_weight, fc1_bias, fc2_weight, fc2_bias, conv_weight, conv_bias, cpe_weight, cpe_bias,
):
    weights = []
    for b in range(2):
        own = jnp.concatenate(
            [
                qkv_weight[b].transpose(0, 2, 1).reshape(192, C),
                proj_weight[b],
                fc1_weight[b].T,
                fc2_weight[b].T,
            ],
            axis=0,
        )
        weights.append(lax.all_gather(own, "mp", axis=0, tiled=False))
    conv = conv_weight.transpose(2, 0, 1).reshape(64, OFFS * C)
    conv = lax.all_gather(conv, "mp", axis=0, tiled=True)
    small = jnp.concatenate([qkv_bias.reshape(6, 64), fc1_bias.reshape(8, 64), conv_bias[None]], axis=0)
    small = lax.all_gather(small, "mp", axis=0, tiled=False).astype(f32)
    qkv_rows = small[:, 0:6].transpose(1, 0, 2).reshape(6, C)
    fc1_rows = small[:, 6:14].reshape(4, 2, C).transpose(1, 0, 2).reshape(8, C)
    conv_row = small[:, 14].reshape(1, C)
    cols = jnp.concatenate(
        [
            norm_gain, norm_bias, proj_bias.astype(f32), fc2_bias.astype(f32), qkv_rows, fc1_rows, conv_row,
            cpe_bias.astype(f32)[None],
        ],
        axis=0,
    ).T

    send, spots = send_map(serial_rank.reshape(32, 128))
    spots = lax.all_to_all(spots, "order", split_axis=0, concat_axis=0, tiled=True)
    listed, places = list_map(spots)
    places = lax.all_to_all(places, "mp", split_axis=0, concat_axis=0, tiled=True)
    landing = place_map(places)

    rows = first_block(feats, weights[0], cols)
    rows = lax.all_gather(rows, "mp", axis=0, tiled=True)
    frames = pick_rows(send, rows, "pack")
    frames = lax.all_to_all(frames, "order", split_axis=0, concat_axis=0, tiled=True)
    lists = pick_rows(listed, frames, "repack")
    lists = lax.all_to_all(lists, "mp", split_axis=0, concat_axis=0, tiled=True)
    moved, low = land_rows(landing, lists)

    count = 128
    up = [(i, i + 1) for i in range(count - 1)]
    down = [(i + 1, i) for i in range(count - 1)]
    before = lax.ppermute(low[:, PATCH - HALO :], ("order", "mp"), up)
    after = lax.ppermute(low[:, :HALO], ("order", "mp"), down)
    wide = jnp.concatenate([before, low, after], axis=1)
    result = second_block(wide, moved, neighbours, conv, cpe_weight, weights[1], cols)
    return lax.all_to_all(result, "mp", split_axis=0, concat_axis=1, tiled=True)


def solution(mesh):
    in_specs = (
        P(None, "order"),
        P("order"),
        P(None, "order"),
        P(),
        P(),
        P(None, None, None, "mp"),
        P(None, None, "mp"),
        P(None, "mp", None),
        P(),
        P(None, None, "mp"),
        P(None, "mp"),
        P(None, "mp", None),
        P(),
        P(None, None, "mp"),
        P("mp"),
        P(),
        P(),
    )
    return jax.shard_map(shards, mesh=mesh, in_specs=in_specs, out_specs=P("mp", "order"), check_vma=False)
```

time: 1350 us -> 324 us (0.24)
  local copies, waits for them, and re-layouts: 642 us -> 16.6 us
  matrix products: 220 us -> 0 us
  waiting for transfers between devices: 313 us -> 98 us
  Pallas kernels: 0 us -> 135 us
  other arithmetic: 88.8 us -> 2.66 us
  blocking collectives: 39.8 us -> 23.3 us
    gather x28 -> x0, local copies, waits for them, and re-layouts: 491 us -> none  [the longest x27 458 us: offset_step(): return (running + contract(kernel, widened[:, picked]), None)]
    dot_general x98 -> x0, matrix products: 220 us -> none  [the longest x32 97.8 us: single(): jnp.einsum('qk,dk->dq', chances, triple[2], preferred_element_type=jnp.fl...]
    pallas_call x0 -> x8, Pallas kernels: none -> 135 us  [the longest x1 52.5 us: second_block(): pl.pallas_call(second_kernel, out_shape=S((C, PATCH), f32), in_specs=[VME...]
    all_to_all x2 -> x4, waiting for transfers between devices: 123 us -> 43.2 us  [the longest x1 30.9 us: shards(): lax.all_to_all(frames, 'order', split_axis=0, concat_axis=0, tiled=True)]
    scatter x3 -> x0, local copies, waits for them, and re-layouts: 68.4 us -> none  [the longest x1 36.7 us: relay_rows(): placed = jnp.zeros((feature_rows, tokens + 1), jnp.float32).at[:, landing...]
    while x65 -> x0, local copies, waits for them, and re-layouts: 64.7 us -> none
    all_gather x3 -> x4, waiting for transfers between devices: 117 us -> 53.7 us  [the longest x1 33.2 us: shards(): rows = lax.all_gather(rows, 'mp', axis=0, tiled=True)]
    psum x1 -> x0, waiting for transfers between devices: 39.9 us -> none  [add_heads(): return lax.psum(partial_value, 'mp')]
  transfers between devices with their start and end apart: 9 -> 10, of which waited for: 7 -> 5; matrix products, arithmetic and copies ran while one was open for 6% -> 3% of each run, Pallas kernels for 0% -> 16%
where the time goes in v1:
time: 324 us; the launch traced here: 320 us
  Pallas kernels  135 us (42%)
  waiting for transfers between devices  98 us (30%)
  starting transfers between devices  31.4 us (10%)
  blocking collectives  23.3 us (7%)
  local copies, waits for them, and re-layouts  16.6 us (5%)
  between operations  13.4 us (4%)
    pallas_call x1, Pallas kernels, second_block(): pl.pallas_call(second_kernel, out_shape=S((C, PATCH), f32), in_specs=[VME...  52.5 us
    pallas_call x2, Pallas kernels, pick_rows(): pl.pallas_call(functools.partial(pick_kernel, rows, width), out_shape=S((...  33.4 us
    all_gather x1, waiting for transfers between devices, shards(): rows = lax.all_gather(rows, 'mp', axis=0, tiled=True)  33.2 us
    all_to_all x1, waiting for transfers between devices, shards(): lax.all_to_all(frames, 'order', split_axis=0, concat_axis=0, tiled=True)  30.9 us
    pallas_call x1, Pallas kernels, first_block(): pl.pallas_call(first_kernel, out_shape=S((PATCH, 2, 128), f32), in_specs=...  30 us
    all_gather x2, waiting for transfers between devices, shards(): weights.append(lax.all_gather(own, 'mp', axis=0, tiled=False))  20.5 us
    all_to_all x1, blocking collectives, shards(): return lax.all_to_all(result, 'mp', split_axis=0, concat_axis=1, tiled=True)  16.9 us
    all_to_all x1, waiting for transfers between devices, shards(): lists = lax.all_to_all(lists, 'mp', split_axis=0, concat_axis=0, tiled=True)  12.4 us
  transfers between devices with their start and end apart: 10, of which 5 were waited for; matrix products, arithmetic and copies ran while one was open for 3% of the time, Pallas kernels for 16%

profile of v1, /device:TPU:1, one launch (start us, length us, event | category | flops | bytes accessed | tf_op | source)
XLA Modules:
  0.0 320.2 jit_solution(11987478403885515406)
XLA Ops:
  6.5 1.0 fusion.1
  7.5 0.0 copy-start.12
  7.5 0.0 copy-start.5
  7.6 0.0 copy-start.6
  7.6 0.0 copy-start.8
  7.6 0.0 copy-start.9
  7.6 0.1 copy.65
  7.7 0.8 fusion.2
  8.5 0.1 copy.77
  8.6 1.1 slice_bitcast_fusion
  9.7 0.9 pad_maximum_fusion.1
  10.6 0.0 all-gather.13.cloned.1.call-update
  10.6 0.0 all-gather.9.cloned.1.call-start
  10.7 0.1 reshape.37
  10.8 6.4 %all-gather.3 = bf16[4,15,64]{2,1,0:T(8,128)(2,1)S(1)} all-gather(bf16[1,15,64]{2,1,0:T(8,128)(2,1)S(1)} %maximum_bitcast_fusion), channel_id=3, replica_groups=mesh['order'=32,'mp'=4] {'mp'}, dimensions={0}, use_global_device_ids=true | all-gather | bytes 9600 | tf_op jit(solution)/shard_map/all_gather | solution.py:399
  17.3 0.1 reshape.38
  17.4 0.1 reshape_squeeze.3
  17.4 0.1 reshape.39
  17.6 0.0 copy-done.5
  17.6 0.3 concatenate.17
  17.9 0.8 copy.70
  18.7 20.5 %all-gather.13.cloned.1.call-done = bf16[3072,256]{0,1:T(8,128)(2,1)} async-done(((bf16[768,256]{0,1:T(8,128)(2,1)}), bf16[3072,256]{0,1:T(8,128)(2,1)}) %all-gather.13.cloned.1.call-update) | async-done | bytes 1572880 | tf_op jit(solution)/shard_map/all_gather | solution.py:395
  39.2 2.6 copy.66
  41.8 30.0 %first_block.1 = f32[1024,2,128]{2,1,0:T(2,128)} custom-call(f32[256,4096]{1,0:T(8,128)} %feats_ref.1, bf16[4,768,256]{2,1,0:T(8,128)(2,1)} %bitcast.54, f32[256,30]{1,0:T(8,128)} %bitcast.59), custom_call_target="tpu_custom_call" | custom-call | tf_op jit(solution)/shard_map/first_block/pallas_call | solution.py:310
  71.8 0.0 copy-start.2
  71.8 0.0 all-gather.9.cloned.1.call-update
  71.9 0.0 all-gather.15.cloned.1.call-start
  71.9 0.1 copy.73
  72.0 0.1 copy.78
  72.1 0.9 pad_maximum_fusion.2
  73.0 0.0 all-gather.15.cloned.1.call-update
  73.0 0.0 all-gather.11.cloned.1.call-start
  73.1 1.0 copy.79
  74.1 0.0 all-gather.11.cloned.1.call-update
  74.1 3.2 %send_map.1 = (s32[32,64]{1,0:T(8,128)}, s32[32,64]{1,0:T(8,128)}) custom-call(s32[32,128]{1,0:T(8,128)} %bitcast.69), custom_call_target="tpu_custom_call" | custom-call | tf_op jit(solution)/shard_map/send_map/pallas_call | solution.py:91
  77.3 9.1 %all-to-all-start = ((s32[32,1,64]{2,1,0:T(1,128)}), s32[32,1,64]{2,1,0:T(1,128)S(1)}, u32[]{:S(2)}, u32[]{:S(2)}) async-start(s32[32,1,64]{2,1,0:T(1,128)} %bitcast.70), calls=%async_computation | async-start | bytes 32768 | tf_op jit(solution)/shard_map/all_to_all | solution.py:412
  86.4 33.2 %all-gather.9.cloned.1.call-done.src_ref = f32[4096,2,128]{2,1,0:T(2,128)} async-done(((f32[1024,2,128]{2,1,0:T(2,128)}), f32[4096,2,128]{2,1,0:T(2,128)}) %all-gather.9.cloned.1.call-update) | async-done | bytes 4194320 | tf_op jit(solution)/shard_map/all_gather | solution.py:418
  119.6 19.5 %pack.1 = f32[2048,2,128]{2,1,0:T(2,128)} custom-call(s32[32,64]{1,0:T(8,128)} %get-tuple-element.14.index_ref, f32[4096,2,128]{2,1,0:T(2,128)} %all-gather.9.cloned.1.call-done.src_ref), custom_call_target="tpu_custom_call" | custom-call | tf_op jit(solution)/shard_map/pack/pallas_call | solution.py:179
  139.1 0.0 all-to-all-done
  139.1 0.6 copy-done.4
  139.7 9.1 %all-to-all-start.2 = ((f32[2048,2,128]{2,1,0:T(2,128)}), f32[2048,2,128]{2,1,0:T(2,128)S(1)}, u32[]{:S(2)}, u32[]{:S(2)}) async-start(f32[2048,2,128]{2,1,0:T(2,128)} %pack.1), calls=%async_computation.2 | async-start | bytes 4194304 | tf_op jit(solution)/shard_map/all_to_all | solution.py:420
  148.8 9.1 %list_map.1 = (s32[4,288]{1,0:T(4,128)}, s32[4,288]{1,0:T(4,128)}) custom-call(s32[32,64]{1,0:T(8,128)} %bitcast.66), custom_call_target="tpu_custom_call" | custom-call | tf_op jit(solution)/shard_map/list_map/pallas_call | solution.py:131
  157.9 1.3 copy.63
  159.2 30.9 %all-to-all-done.2.src_ref = f32[2048,2,128]{2,1,0:T(2,128)S(1)} async-done(((f32[2048,2,128]{2,1,0:T(2,128)}), f32[2048,2,128]{2,1,0:T(2,128)S(1)}, u32[]{:S(2)}, u32[]{:S(2)}) %all-to-all-start.2) | async-done | bytes 2097184 | tf_op jit(solution)/shard_map/all_to_all | solution.py:420
  190.1 4.8 %all-to-all-start.1 = ((s32[4,1,288]{2,1,0:T(1,128)}), s32[4,1,288]{2,1,0:T(1,128)S(1)}, u32[]{:S(2)}, u32[]{:S(2)}) async-start(s32[4,1,288]{2,1,0:T(1,128)} %copy.63), calls=%async_computation.1 | async-start | bytes 12288 | tf_op jit(solution)/shard_map/all_to_all | solution.py:414
  194.8 13.9 %repack.1 = f32[1152,2,128]{2,1,0:T(2,128)} custom-call(s32[4,288]{1,0:T(4,128)} %get-tuple-element.13.index_ref, f32[2048,2,128]{2,1,0:T(2,128)} %copy-done), custom_call_target="tpu_custom_call" | custom-call | tf_op jit(solution)/shard_map/repack/pallas_call | solution.py:179
  208.8 0.0 all-to-all-done.1
  208.8 3.5 %all-to-all-start.3 = ((f32[1152,2,128]{2,1,0:T(2,128)}), f32[1152,2,128]{2,1,0:T(2,128)S(1)}, u32[]{:S(2)}, u32[]{:S(2)}) async-start(f32[1152,2,128]{2,1,0:T(2,128)} %repack.1), calls=%async_computation.3 | async-start | bytes 2359296 | tf_op jit(solution)/shard_map/all_to_all | solution.py:422
  212.3 0.6 copy.82
  212.9 2.0 place_map.1.index_ref
  214.9 12.4 %all-to-all-done.3.src_ref = f32[1152,2,128]{2,1,0:T(2,128)S(1)} async-done(((f32[1152,2,128]{2,1,0:T(2,128)}), f32[1152,2,128]{2,1,0:T(2,128)S(1)}, u32[]{:S(2)}, u32[]{:S(2)}) %all-to-all-start.3) | async-done | bytes 1179680 | tf_op jit(solution)/shard_map/all_to_all | solution.py:422
  227.3 1.1 copy-done.1
  228.4 4.5 %land.1 = (f32[256,1024]{1,0:T(8,128)}, bf16[256,1024]{1,0:T(8,128)(2,1)}) custom-call(s32[1,1024]{1,0:T(1,128)} %place_map.1.index_ref, f32[1152,2,128]{2,1,0:T(2,128)} %copy-done.1), custom_call_target="tpu_custom_call" | custom-call | tf_op jit(solution)/shard_map/land/pallas_call | solution.py:204
  232.9 0.9 fusion
  233.8 2.7 collective-permute-start
  236.5 2.1 collective-permute-start.1
  238.6 0.0 all-gather.15.cloned.1.call-done
  238.6 2.6 copy.74
  241.3 0.0 collective-permute-done
  241.3 1.0 collective-permute-done.1
  242.3 0.9 pad_maximum_fusion.wide_ref
  243.1 52.5 %second_block.1 = f32[256,1024]{1,0:T(8,128)} custom-call(bf16[256,1280]{1,0:T(8,128)(2,1)} %pad_maximum_fusion.wide_ref, f32[256,1024]{1,0:T(8,128)} %get-tuple-element.16.moved_ref, s32[27,4096]{1,0:T(8,128)} %near_ref.1, bf16[256,6912]{1,0:T(8,128)(2,1)} %all-gather.11.cloned.1.call-done.conv_ref, bf16[256,256]{1,0:T(8,128)(2,1)} %cpe_ref.1, ...), custom_call_target="tpu_custom_call" | custom-call | tf_op jit(solution)/shard_map/second_block/pallas_call | solution.py:363
  295.6 16.9 %all_to_all.51 = f32[4,64,1024]{2,1,0:T(8,128)S(1)} all-to-all(f32[4,64,1024]{2,1,0:T(8,128)} %bitcast.56), channel_id=1, replica_groups=mesh['order'=32,'mp'=4] {'mp'}, dimensions={0} | all-to-all | bytes 2097152 | tf_op jit(solution)/shard_map/all_to_all | solution.py:432
  312.6 1.1 copy.80
  (30 shorter events, 0.1 us)
Async XLA Ops:
  6.5 4.1 %copy-start.7 = (bf16[2,3,64]{2,0,1:T(2,128)(2,1)S(1)}, bf16[2,3,64]{2,0,1:T(2,128)(2,1)}, u32[]{:S(2)}) copy-start(bf16[2,3,64]{2,0,1:T(2,128)(2,1)} %param.23) | copy-start | bytes 2308
  6.5 4.2 %copy-start.10 = (bf16[2,256]{1,0:T(2,128)(2,1)S(1)}, bf16[2,256]{1,0:T(2,128)(2,1)}, u32[]{:S(2)}) copy-start(bf16[2,256]{1,0:T(2,128)(2,1)} %param.27) | copy-start | bytes 3076
  6.5 4.3 %copy-start.11 = (bf16[64]{0:T(256)(128)(2,1)S(1)}, bf16[64]{0:T(256)(128)(2,1)}, u32[]{:S(2)}) copy-start(bf16[64]{0:T(256)(128)(2,1)} %param.31) | copy-start | bytes 388
  6.5 32.6 %all-gather.13.cloned.1.call-start = ((), (), s32[]{:S(2)}) async-start(), calls=%async_computation.7 | async-start | bytes 1966080 | tf_op jit(solution)/shard_map/all_gather | solution.py:395
  7.5 10.0 %copy-start.12 = (bf16[256]{0:T(256)(128)(2,1)S(1)}, bf16[256]{0:T(256)(128)(2,1)}, u32[]{:S(2)}) copy-start(bf16[256]{0:T(256)(128)(2,1)} %param.33) | copy-start | bytes 1540
  7.5 10.0 %copy-start.5 = (f32[5,256]{1,0:T(8,128)S(1)}, f32[5,256]{1,0:T(8,128)}, u32[]{:S(2)}) copy-start(f32[5,256]{1,0:T(8,128)} %param.20) | copy-start | bytes 15364
  7.6 10.0 %copy-start.6 = (f32[5,256]{1,0:T(8,128)S(1)}, f32[5,256]{1,0:T(8,128)}, u32[]{:S(2)}) copy-start(f32[5,256]{1,0:T(8,128)} %param.21) | copy-start | bytes 15364
  7.6 10.0 %copy-start.8 = (bf16[2,256]{1,0:T(2,128)(2,1)S(1)}, bf16[2,256]{1,0:T(2,128)(2,1)}, u32[]{:S(2)}) copy-start(bf16[2,256]{1,0:T(2,128)(2,1)} %param.25) | copy-start | bytes 3076
  7.6 10.0 %copy-start.9 = (bf16[2,256]{1,0:T(2,128)(2,1)S(1)}, bf16[2,256]{1,0:T(2,128)(2,1)}, u32[]{:S(2)}) copy-start(bf16[2,256]{1,0:T(2,128)(2,1)} %param.29) | copy-start | bytes 3076
  10.6 109.0 %all-gather.9.cloned.1.call-start = ((), (), s32[]{:S(2)}) async-start(), calls=%async_computation.5 | async-start | bytes 5242880 | tf_op jit(solution)/shard_map/all_gather | solution.py:418
  71.8 1.3 copy-start.2
  71.9 166.8 %all-gather.15.cloned.1.call-start = ((), (), s32[]{:S(2)}) async-start(), calls=%async_computation.8 | async-start | bytes 1966080 | tf_op jit(solution)/shard_map/all_gather | solution.py:395
  73.0 170.1 %all-gather.11.cloned.1.call-start = ((), (), s32[]{:S(2)}) async-start(), calls=%async_computation.6 | async-start | bytes 4423680 | tf_op jit(solution)/shard_map/all_gather | solution.py:397
  77.3 61.8 %all-to-all-start = ((s32[32,1,64]{2,1,0:T(1,128)}), s32[32,1,64]{2,1,0:T(1,128)S(1)}, u32[]{:S(2)}, u32[]{:S(2)}) async-start(s32[32,1,64]{2,1,0:T(1,128)} %bitcast.70), calls=%async_computation | async-start | bytes 32768 | tf_op jit(solution)/shard_map/all_to_all | solution.py:412
  139.1 0.6 copy-start.4
  139.7 50.4 %all-to-all-start.2 = ((f32[2048,2,128]{2,1,0:T(2,128)}), f32[2048,2,128]{2,1,0:T(2,128)S(1)}, u32[]{:S(2)}, u32[]{:S(2)}) async-start(f32[2048,2,128]{2,1,0:T(2,128)} %pack.1), calls=%async_computation.2 | async-start | bytes 4194304 | tf_op jit(solution)/shard_map/all_to_all | solution.py:420
  190.1 4.8 %copy-start = (f32[2048,2,128]{2,1,0:T(2,128)}, f32[2048,2,128]{2,1,0:T(2,128)S(1)}, u32[]{:S(2)}) copy-start(f32[2048,2,128]{2,1,0:T(2,128)S(1)} %all-to-all-done.2.src_ref) | copy-start | bytes 6291460
  190.1 18.7 %all-to-all-start.1 = ((s32[4,1,288]{2,1,0:T(1,128)}), s32[4,1,288]{2,1,0:T(1,128)S(1)}, u32[]{:S(2)}, u32[]{:S(2)}) async-start(s32[4,1,288]{2,1,0:T(1,128)} %copy.63), calls=%async_computation.1 | async-start | bytes 12288 | tf_op jit(solution)/shard_map/all_to_all | solution.py:414
  208.8 18.5 %all-to-all-start.3 = ((f32[1152,2,128]{2,1,0:T(2,128)}), f32[1152,2,128]{2,1,0:T(2,128)S(1)}, u32[]{:S(2)}, u32[]{:S(2)}) async-start(f32[1152,2,128]{2,1,0:T(2,128)} %repack.1), calls=%async_computation.3 | async-start | bytes 2359296 | tf_op jit(solution)/shard_map/all_to_all | solution.py:422
  227.3 1.1 copy-start.1
  233.8 7.5 %collective-permute-start = (bf16[256,128]{1,0:T(8,128)(2,1)S(1)}, bf16[256,128]{1,0:T(8,128)(2,1)S(1)}, u32[]{:S(2)}, u32[]{:S(2)}) collective-permute-start(bf16[256,128]{1,0:T(8,128)(2,1)S(1)} %get-tuple-element.17), channel_id=1, source_target_pairs={{0,1},{1,2},{2,3},{3,4},{4,5},{5,6},{6,7},{7,8},{8,9},{9,10},{10,1... | collective-permute-start | bytes 196616 | tf_op jit(solution)/shard_map/ppermute | solution.py:428
  236.5 5.7 %copy-start.3 = (bf16[256,1024]{1,0:T(8,128)(2,1)S(1)}, bf16[256,1024]{1,0:T(8,128)(2,1)}, u32[]{:S(2)}) copy-start(bf16[256,1024]{1,0:T(8,128)(2,1)} %get-tuple-element.15) | copy-start | bytes 1572868
  236.5 5.7 %collective-permute-start.1 = (bf16[256,128]{1,0:T(8,128)(2,1)S(1)}, bf16[256,128]{1,0:T(8,128)(2,1)S(1)}, u32[]{:S(2)}, u32[]{:S(2)}) collective-permute-start(bf16[256,128]{1,0:T(8,128)(2,1)S(1)} %get-tuple-element.18), channel_id=1, source_target_pairs={{1,0},{2,1},{3,2},{4,3},{5,4},{6,5},{7,6},{8,7},{9,8},{10,9},{11,1... | collective-permute-start | bytes 196616 | tf_op jit(solution)/shard_map/ppermute | solution.py:429
Sparse Core Ops, SparseCore 0:
  10.7 28.3 all-gather.12
  72.0 47.5 all-gather.8
  121.3 25.6 all-gather.14
  148.5 53.0 all-gather.10

commit v2 on v1

v2 whole, which is shorter than its diff:
```python
import functools
import math

import jax
import jax.numpy as jnp
from jax import lax
from jax.experimental import pallas as pl
from jax.experimental.pallas import tpu as pltpu
from jax.sharding import PartitionSpec as P

C = 256
PATCH = 1024
HALO = 128
HDIM = 16
HEADS = 16
OFFS = 27
TOK = 4096
SLOTS = 64
CAP = 288
CAP_OUT = 352
ORDERS = 32
MESH = pl.DeviceIdType.MESH
EPS = 1e-05
LOG2E = math.log2(math.e)
f32, bf16, i32 = jnp.float32, jnp.bfloat16, jnp.int32
VMEM = pl.BlockSpec(memory_space=pltpu.VMEM)
SMEM = pl.BlockSpec(memory_space=pltpu.SMEM)
ANY = pl.BlockSpec(memory_space=pl.ANY)
S = jax.ShapeDtypeStruct
COL_GAIN, COL_SHIFT, COL_PROJ, COL_FC2, COL_QKV, COL_FC1, COL_CONV, COL_CPE = 0, 5, 10, 12, 14, 20, 28, 29


def kernel_params(**more):
    return pltpu.CompilerParams(vmem_limit_bytes=56 * 2**20, **more)


def iota(shape, dim):
    return lax.broadcasted_iota(i32, shape, dim)


def one_hot(left, right):
    return jnp.where(left == right, 1.0, 0.0).astype(bf16)


def dot_rows(left, right):
    return lax.dot_general(left, right, (((1,), (1,)), ((), ())), preferred_element_type=f32)


def dot(left, right):
    return jnp.dot(left, right, preferred_element_type=f32)


def norm_columns(values, gain, shift):
    average = jnp.mean(values, axis=0, keepdims=True)
    centred = values - average
    variance = jnp.mean(centred * centred, axis=0, keepdims=True)
    return centred * lax.rsqrt(variance + EPS) * gain + shift


def greet(order_peers, halo):
    barrier = pltpu.get_barrier_semaphore()
    group, member = lax.axis_index("order"), lax.axis_index("mp")
    for d in range(1, 4):
        pl.semaphore_signal(barrier, inc=1, device_id=(group, member ^ d), device_id_type=MESH)
    count = 3
    if order_peers:

        def step(d, carry):
            pl.semaphore_signal(barrier, inc=1, device_id=(group ^ d, member), device_id_type=MESH)
            return carry

        lax.fori_loop(1, ORDERS, step, 0)
        count += ORDERS - 1
    if halo:
        for shift in (1, 127):
            pl.semaphore_signal(barrier, inc=1, device_id=neighbour(shift), device_id_type=MESH)
        count += 2
    return barrier, count


def neighbour(shift):
    place = (lax.axis_index("order") * 4 + lax.axis_index("mp") + shift) % 128
    return (place // 4, place % 4)


def remote(src, dst, send, recv, device):
    return pltpu.make_async_remote_copy(
        src_ref=src, dst_ref=dst, send_sem=send, recv_sem=recv, device_id=device, device_id_type=MESH
    )


def routes_kernel(
    rank_ref, send_ref, listed_ref, landing_ref, leave_ref,
    made_ref, slot_ref, spot_ref, left_ref, right_ref, left2_ref, right2_ref,
    pos_out, pos_in, place_out, place_in, send_sem, recv_sem, send2_sem, recv2_sem,
):
    group, member = lax.axis_index("order"), lax.axis_index("mp")
    barrier, count = greet(True, False)
    rank = rank_ref[...]
    upper = jnp.where(iota((128, 128), 0) < iota((128, 128), 1), 1.0, 0.0).astype(bf16)
    both = jnp.concatenate([upper, jnp.ones((128, 128), bf16)], axis=1)
    lane = iota((1, 128), 1)

    def classes(c):
        return jnp.where(iota((128, 128), 0) == rank_ref[pl.ds(c, 1), :] // PATCH, 1.0, 0.0)

    def count_classes(c, total):
        made = dot(classes(c).astype(bf16), both)
        made_ref[c] = made
        return total + made[:, 128:]

    total = lax.fori_loop(0, 32, count_classes, jnp.zeros((128, 128), f32), unroll=8)
    row, col = iota((128, 128), 0), iota((128, 128), 1)
    ahead = jnp.where((row // 4 == col // 4) & (col < row), 1.0, 0.0).astype(bf16)

    def number(c, carry):
        made = made_ref[c]
        slot = jnp.sum(classes(c) * (made[:, :128] + carry), axis=0, keepdims=True)
        slot_ref[pl.ds(c, 1), :] = slot.astype(i32)
        return carry + made[:, 128:]

    lax.fori_loop(0, 32, number, dot(ahead, total.astype(bf16)), unroll=4)

    slots = slot_ref[...]
    hot = jnp.where(iota((32, 8, 128), 1) == (slots % 4)[:, None, :], 1.0, 0.0).reshape(256, 128)
    made = dot(hot.astype(bf16), both)
    row, col = iota((256, 256), 0), iota((256, 256), 1)
    earlier = (row % 8 == col % 8) & (row // 64 == col // 64) & (col < row)
    carry = dot(jnp.where(earlier, 1.0, 0.0).astype(bf16), made[:, 128:].astype(bf16))
    spot_ref[...] = jnp.sum((hot * (made[:, :128] + carry)).reshape(32, 8, 128), axis=1).astype(i32)

    def frames(c, carry):
        span = pl.ds(pl.multiple_of(c * 128, 128), 128)
        rank_row, spot_row = rank_ref[pl.ds(c, 1), :], spot_ref[pl.ds(c, 1), :]
        owner = jnp.where(iota((32, 128), 0) == rank_row // TOK, 1.0, 0.0)
        entry = (c // 8) * CAP_OUT + spot_row
        inside = rank_row % TOK
        pieces = [entry // 64, entry % 64, inside // 64, inside % 64]
        left = jnp.concatenate([owner * p.astype(f32) for p in pieces] + [owner], axis=0)
        left_ref[:, span] = left.astype(bf16)
        right_ref[:, span] = one_hot(iota((SLOTS, 128), 0) * 4 + member, slot_ref[pl.ds(c, 1), :])
        return carry

    lax.fori_loop(0, 32, frames, 0, unroll=2)
    acc = dot_rows(left_ref[...], right_ref[...])
    send_ref[...] = (acc[0:32] * 64.0 + acc[32:64]).astype(i32)
    inside = jnp.where(acc[128:160] > 0.5, (acc[64:96] * 64.0 + acc[96:128]).astype(i32), TOK)
    inside = jnp.concatenate([inside, jnp.full((32, 128 - SLOTS), TOK, i32)], axis=1)
    pos_out[...] = jnp.broadcast_to(inside[:, None, :], (32, 8, 128))
    pos_in[group] = pos_out[group]

    pl.semaphore_wait(barrier, count)

    def frame_copy(d):
        return remote(
            pos_out.at[group ^ d], pos_in.at[group], send_sem.at[d], recv_sem.at[d], (group ^ d, member)
        )

    def frame_start(d, carry):
        frame_copy(d).start()
        return carry

    def frame_wait(d, carry):
        frame_copy(d).wait()
        return carry

    lax.fori_loop(1, ORDERS, frame_start, 0)

    def leaving(c, carry):
        span = pl.ds(pl.multiple_of(c * 128, 128), 128)
        at = pl.ds(member * 8 + c, 1)
        hot = jnp.where(iota((8, 128), 0) == slot_ref[at, :] % 4, 1.0, 0.0)
        token = c * 128 + lane
        left = jnp.concatenate([hot * (token // 64).astype(f32), hot * (token % 64).astype(f32)], axis=0)
        left2_ref[:, span] = left.astype(bf16)
        right2_ref[:, span] = one_hot(iota((CAP_OUT, 128), 0), spot_ref[at, :])
        return carry

    lax.fori_loop(0, 8, leaving, 0)
    acc = dot_rows(left2_ref[...], right2_ref[...])
    leave_ref[...] = (acc[0:4] * 64.0 + acc[8:12]).astype(i32)

    lax.fori_loop(1, ORDERS, frame_wait, 0)

    pos = pos_in[:, 0, :]
    hot = jnp.where(iota((32, 8, 128), 1) == (pos // PATCH)[:, None, :], 1.0, 0.0).reshape(256, 128)
    made = dot(hot.astype(bf16), both)
    earlier = (row % 8 == col % 8) & (col < row)
    carry = dot(jnp.where(earlier, 1.0, 0.0).astype(bf16), made[:, 128:].astype(bf16))
    spot_ref[...] = jnp.sum((hot * (made[:, :128] + carry)).reshape(32, 8, 128), axis=1).astype(i32)
    slot_ref[...] = pos

    def lists(c, acc):
        inside = slot_ref[pl.ds(c, 1), :]
        hot = jnp.where(iota((8, 128), 0) == inside // PATCH, 1.0, 0.0)
        inside = inside % PATCH
        pieces = [jnp.broadcast_to(c, (1, 128)), lane, inside // 32, inside % 32]
        left = jnp.concatenate([hot * p.astype(f32) for p in pieces] + [hot], axis=0)
        right = one_hot(iota((384, 128), 0), spot_ref[pl.ds(c, 1), :])
        return acc + dot_rows(left.astype(bf16), right)

    acc = lax.fori_loop(0, 32, lists, jnp.zeros((40, 384), f32), unroll=4)
    listed_ref[...] = (acc[0:4] * float(SLOTS) + acc[8:12]).astype(i32)[:, :CAP]
    place = jnp.where(acc[32:36] > 0.5, (acc[16:20] * 32.0 + acc[24:28]).astype(i32), -1)
    place_out[...] = jnp.broadcast_to(place[:, None, :], (4, 8, 384))
    place_in[member] = place_out[member]
    copies = [
        remote(
            place_out.at[member ^ d], place_in.at[member], send2_sem.at[d], recv2_sem.at[d],
            (group, member ^ d),
        )
        for d in range(1, 4)
    ]
    for copy in copies:
        copy.start()
    for copy in copies:
        copy.wait()

    acc = jnp.zeros((8, PATCH), f32)
    entry = iota((1, 384), 1)
    kind = iota((8, 384), 0)
    for q in range(4):
        right = one_hot(iota((PATCH, 384), 0), place_in[q, 0:1, :])
        at = q * CAP + entry
        left = jnp.where(kind == 0, at // 64, jnp.where(kind == 1, at % 64, 0))
        acc = acc + dot_rows(left.astype(f32).astype(bf16), right)
    landing_ref[...] = (acc[0:1] * 64.0 + acc[1:2]).astype(i32)


def routes(rank):
    return pl.pallas_call(
        routes_kernel,
        out_shape=[S((32, SLOTS), i32), S((4, CAP), i32), S((1, PATCH), i32), S((4, CAP_OUT), i32)],
        in_specs=[VMEM],
        out_specs=[VMEM] * 4,
        scratch_shapes=[
            pltpu.VMEM((32, 128, 256), f32),
            pltpu.VMEM((32, 128), i32),
            pltpu.VMEM((32, 128), i32),
            pltpu.VMEM((160, TOK), bf16),
            pltpu.VMEM((SLOTS, TOK), bf16),
            pltpu.VMEM((16, PATCH), bf16),
            pltpu.VMEM((CAP_OUT, PATCH), bf16),
            pltpu.VMEM((32, 8, 128), i32),
            pltpu.VMEM((32, 8, 128), i32),
            pltpu.VMEM((4, 8, 384), i32),
            pltpu.VMEM((4, 8, 384), i32),
            pltpu.SemaphoreType.DMA((ORDERS,)),
            pltpu.SemaphoreType.DMA((ORDERS,)),
            pltpu.SemaphoreType.DMA((4,)),
            pltpu.SemaphoreType.DMA((4,)),
        ],
        compiler_params=kernel_params(collective_id=0, has_side_effects=True),
        name="routes",
    )(rank)


def move_rows(count, index, source, store):
    def step(i, carry):
        records = [source[index(i * 16 + u)] for u in range(16)]
        for u in range(16):
            store(i * 16 + u, records[u])
        return carry

    lax.fori_loop(0, count // 16, step, 0)


def relay_kernel(
    rows_ref, send_ref, listed_ref, landing_ref, moved_ref, wide_ref,
    out_ref, frames_ref, sorted_ref, lists_ref, land_ref,
    send_sem, recv_sem, send2_sem, recv2_sem, send3_sem, recv3_sem,
):
    group, member = lax.axis_index("order"), lax.axis_index("mp")
    barrier, count = greet(True, True)
    pl.semaphore_wait(barrier, count)

    def frame_copy(d):
        return remote(
            out_ref.at[d], frames_ref.at[pl.ds(pl.multiple_of(group * SLOTS, SLOTS), SLOTS)],
            send_sem.at[d], recv_sem.at[d], (group ^ d, member),
        )

    def pack(d, carry):
        target = group ^ d

        def store(r, record):
            out_ref[d, r] = record

        move_rows(SLOTS, lambda r: send_ref[target, r], rows_ref, store)
        frame_copy(d).start()
        return carry

    lax.fori_loop(1, ORDERS, pack, 0)

    def store_own(r, record):
        frames_ref[group * SLOTS + r] = record

    move_rows(SLOTS, lambda r: send_ref[group, r], rows_ref, store_own)

    def frame_wait(d, carry):
        frame_copy(d).wait()
        return carry

    lax.fori_loop(1, ORDERS, frame_wait, 0)

    copies = []
    for d in (2, 3, 1):
        target = member ^ d

        def store(r, record, d=d):
            sorted_ref[d, r] = record

        move_rows(CAP, lambda r: listed_ref[target, r], frames_ref, store)
        copy = remote(
            sorted_ref.at[d], lists_ref.at[pl.ds(member * CAP, CAP)], send2_sem.at[d], recv2_sem.at[d],
            (group, target),
        )
        copy.start()
        copies.append(copy)

    def store_mine(r, record):
        lists_ref[member * CAP + r] = record

    move_rows(CAP, lambda r: listed_ref[member, r], frames_ref, store_mine)
    for copy in copies:
        copy.wait()

    def land(start, rows):
        def store(r, record):
            land_ref[start + r] = record

        move_rows(rows, lambda r: landing_ref[0, start + r], lists_ref, store)
        for half in range(2):
            part = land_ref[start : start + rows, half, :].T
            at = slice(half * 128, half * 128 + 128)
            moved_ref[at, start : start + rows] = part
            wide_ref[at, HALO + start : HALO + start + rows] = part.astype(bf16)

    land(0, HALO)
    land(PATCH - HALO, HALO)
    halos = [
        remote(
            wide_ref.at[:, HALO : 2 * HALO], wide_ref.at[:, HALO + PATCH : 2 * HALO + PATCH],
            send3_sem.at[0], recv3_sem.at[0], neighbour(127),
        ),
        remote(
            wide_ref.at[:, PATCH : PATCH + HALO], wide_ref.at[:, 0:HALO],
            send3_sem.at[1], recv3_sem.at[1], neighbour(1),
        ),
    ]
    for copy in halos:
        copy.start()
    for c in range(3):
        land(HALO + c * 256, 256)
    for copy in halos:
        copy.wait()


def relay(rows, send, listed, landing):
    return pl.pallas_call(
        relay_kernel,
        out_shape=[S((C, PATCH), f32), S((C, PATCH + 2 * HALO), bf16)],
        in_specs=[VMEM, SMEM, SMEM, SMEM],
        out_specs=[VMEM, VMEM],
        scratch_shapes=[
            pltpu.VMEM((ORDERS, SLOTS, 2, 128), f32),
            pltpu.VMEM((ORDERS * SLOTS, 2, 128), f32),
            pltpu.VMEM((4, CAP, 2, 128), f32),
            pltpu.VMEM((4 * CAP, 2, 128), f32),
            pltpu.VMEM((PATCH, 2, 128), f32),
            pltpu.SemaphoreType.DMA((ORDERS,)),
            pltpu.SemaphoreType.DMA((ORDERS,)),
            pltpu.SemaphoreType.DMA((4,)),
            pltpu.SemaphoreType.DMA((4,)),
            pltpu.SemaphoreType.DMA((2,)),
            pltpu.SemaphoreType.DMA((2,)),
        ],
        compiler_params=kernel_params(collective_id=2, has_side_effects=True),
        name="relay",
    )(rows, send, listed, landing)


def block_scratch():
    return [
        pltpu.VMEM((C, PATCH), bf16),
        pltpu.VMEM((3, C, PATCH), bf16),
        pltpu.VMEM((2, PATCH, 128), bf16),
        pltpu.VMEM((PATCH, PATCH), f32),
        pltpu.VMEM((PATCH, PATCH), f32),
        pltpu.VMEM((2, 8, PATCH), f32),
        pltpu.VMEM((C, PATCH), bf16),
    ]


def run_block(block, first_norm, x_ref, w_ref, base, cols_ref, scratch, emit, arrive):
    normed_ref, qkv_ref, keys_ref, s0_ref, s1_ref, top_ref, heads_ref = scratch

    def column(k):
        return cols_ref[:, k : k + 1]

    for c in range(4):
        span = slice(c * 256, c * 256 + 256)
        normed_ref[:, span] = norm_columns(
            x_ref[:, span], column(COL_GAIN + first_norm), column(COL_SHIFT + first_norm)
        ).astype(bf16)
    for r in range(4):
        made = dot(w_ref[r, base : base + 192, :], normed_ref[...])
        for j in range(3):
            bias = cols_ref[r * 64 : r * 64 + 64, COL_QKV + 3 * block + j : COL_QKV + 3 * block + j + 1]
            qkv_ref[j, r * 64 : r * 64 + 64, :] = (made[j * 64 : j * 64 + 64] + bias).astype(bf16)
    for g in range(2):
        keys_ref[g] = qkv_ref[1, g * 128 : g * 128 + 128, :].T

    head_of_row = iota((128, 1), 0) // HDIM
    buffers = (s0_ref, s1_ref)

    def scores(h, b):
        g = h // 8
        queries = qkv_ref[0, pl.ds(pl.multiple_of(g * 128, 128), 128), :]
        queries = jnp.where(head_of_row == h % 8, queries.astype(f32), 0.0).astype(bf16)
        s = dot(keys_ref[g], queries)
        buffers[b][...] = s
        top_ref[b, 0:1, :] = jnp.max(s, axis=0, keepdims=True)

    def finish(h, b):
        p = jnp.exp2((buffers[b][...] - top_ref[b, 0:1, :]) * (0.25 * LOG2E))
        inverse = 1.0 / jnp.sum(p, axis=0, keepdims=True)
        chances = (p * inverse).astype(bf16)
        rows = pl.ds(pl.multiple_of(h * HDIM, HDIM), HDIM)
        heads_ref[rows, :] = dot(qkv_ref[2, rows, :], chances).astype(bf16)

    scores(0, 0)

    def pair(j, carry):
        h = 2 * j
        scores(h + 1, 1)
        finish(h, 0)
        scores(jnp.minimum(h + 2, HEADS - 1), 0)
        finish(h + 1, 1)
        return carry

    lax.fori_loop(0, HEADS // 2, pair, 0)

    arrive()
    proj = [w_ref[r, base + 192 : base + 256, :].T for r in range(4)]
    for c in range(4):
        span = slice(c * 256, c * 256 + 256)
        mixed = dot(proj[0], heads_ref[0:64, span])
        for r in range(1, 4):
            mixed = mixed + dot(proj[r], heads_ref[r * 64 : r * 64 + 64, span])
        attended = x_ref[:, span] + (mixed + column(COL_PROJ + block))
        normed = norm_columns(
            attended, column(COL_GAIN + first_norm + 1), column(COL_SHIFT + first_norm + 1)
        ).astype(bf16)
        total = None
        for r in range(4):
            hidden = dot(w_ref[r, base + 256 : base + 512, :], normed) + column(COL_FC1 + 4 * block + r)
            hidden = 0.5 * hidden * (1.0 + lax.erf(hidden * math.sqrt(0.5)))
            part = dot(w_ref[r, base + 512 : base + 768, :], hidden.astype(bf16))
            total = part if total is None else total + part
        emit(c, attended + (total + column(COL_FC2 + block)))


def first_kernel(
    feats_ref, qkv_w_ref, proj_w_ref, fc1_w_ref, fc2_w_ref, gain_ref, shift_ref, qkv_b_ref, proj_b_ref,
    fc1_b_ref, fc2_b_ref, conv_b_ref, cpe_b_ref, leave_ref, rows_ref, cols_ref,
    x_ref, w_ref, params_ref, records_ref, sorted_ref, sem, send_sem, recv_sem, send2_sem, recv2_sem, *scratch
):
    group, member = lax.axis_index("order"), lax.axis_index("mp")
    barrier, count = greet(False, False)
    start = pl.multiple_of(member * PATCH, PATCH)
    load = pltpu.make_async_copy(feats_ref.at[:, pl.ds(start, PATCH)], x_ref, sem)
    load.start()

    pad = jnp.zeros((16, C - 64), f32)
    narrow = jnp.concatenate(
        [qkv_b_ref[0].astype(f32), qkv_b_ref[1].astype(f32), conv_b_ref[...].astype(f32), jnp.zeros((9, 64), f32)],
        axis=0,
    )
    narrow = jnp.concatenate([narrow, pad], axis=1)
    wide = jnp.concatenate([jnp.zeros((8, C), f32), fc1_b_ref[...].astype(f32), jnp.zeros((6, C), f32)], axis=0)
    w_ref[member, 0:16, :] = (narrow + wide).astype(bf16)
    for j in range(3):
        w_ref[member, 16 + j * 64 : 80 + j * 64, :] = qkv_w_ref[0, j].T

    def weight_copy(part, d):
        rows = (pl.ds(0, 208), pl.ds(208, 576))[part]
        return remote(
            w_ref.at[member, rows], w_ref.at[member, rows], send_sem.at[part, d], recv_sem.at[part, d],
            (group, member ^ d),
        )

    pl.semaphore_wait(barrier, count)
    for d in (2, 3, 1):
        weight_copy(0, d).start()
    w_ref[member, 208:272, :] = proj_w_ref[0]
    w_ref[member, 272:528, :] = fc1_w_ref[0].T
    w_ref[member, 528:784, :] = fc2_w_ref[0].T
    for d in (2, 3, 1):
        weight_copy(1, d).start()
    load.wait()
    for d in (2, 3, 1):
        weight_copy(0, d).wait()

    params_ref[...] = jnp.zeros_like(params_ref)
    params_ref[COL_GAIN : COL_GAIN + 5, :] = gain_ref[...]
    params_ref[COL_SHIFT : COL_SHIFT + 5, :] = shift_ref[...]
    params_ref[COL_PROJ : COL_PROJ + 2, :] = proj_b_ref[...].astype(f32)
    params_ref[COL_FC2 : COL_FC2 + 2, :] = fc2_b_ref[...].astype(f32)
    bias = [w_ref[r, 0:16, :].astype(f32) for r in range(4)]
    narrow = jnp.concatenate([b[0:8, 0:64] for b in bias], axis=1)
    params_ref[COL_QKV : COL_QKV + 6, :] = narrow[0:6]
    params_ref[COL_CONV : COL_CONV + 1, :] = narrow[6:7]
    for r in range(4):
        for b in range(2):
            params_ref[COL_FC1 + 4 * b + r : COL_FC1 + 4 * b + r + 1, :] = bias[r][8 + b : 9 + b]
    params_ref[COL_CPE : COL_CPE + 1, :] = cpe_b_ref[...].astype(f32)
    cols_ref[...] = params_ref[...].T

    def emit(c, value):
        rows = value.T
        for half in range(2):
            records_ref[c * 256 : c * 256 + 256, half, :] = rows[:, half * 128 : half * 128 + 128]

    def arrive():
        for d in (2, 3, 1):
            weight_copy(1, d).wait()

    run_block(0, 0, x_ref, w_ref, 16, cols_ref, scratch, emit, arrive)

    copies = []
    for d in (2, 3, 1):
        target = member ^ d

        def store(r, record, d=d):
            sorted_ref[d, r] = record

        move_rows(CAP_OUT, lambda r: leave_ref[target, r], records_ref, store)
        copy = remote(
            sorted_ref.at[d], rows_ref.at[pl.ds(member * CAP_OUT, CAP_OUT)], send2_sem.at[d], recv2_sem.at[d],
            (group, target),
        )
        copy.start()
        copies.append(copy)

    def store_mine(r, record):
        rows_ref[member * CAP_OUT + r] = record

    move_rows(CAP_OUT, lambda r: leave_ref[member, r], records_ref, store_mine)
    for copy in copies:
        copy.wait()


def first_block(*operands):
    return pl.pallas_call(
        first_kernel,
        out_shape=[S((4 * CAP_OUT, 2, 128), f32), S((C, 128), f32)],
        in_specs=[ANY] + [VMEM] * 12 + [SMEM],
        out_specs=[VMEM, VMEM],
        scratch_shapes=[
            pltpu.VMEM((C, PATCH), f32),
            pltpu.VMEM((4, 784, C), bf16),
            pltpu.VMEM((128, C), f32),
            pltpu.VMEM((PATCH, 2, 128), f32),
            pltpu.VMEM((4, CAP_OUT, 2, 128), f32),
            pltpu.SemaphoreType.DMA,
            pltpu.SemaphoreType.DMA((2, 4)),
            pltpu.SemaphoreType.DMA((2, 4)),
            pltpu.SemaphoreType.DMA((4,)),
            pltpu.SemaphoreType.DMA((4,)),
        ]
        + block_scratch(),
        compiler_params=kernel_params(collective_id=1, has_side_effects=True),
        name="first_block",
    )(*operands)


def second_kernel(
    wide_ref, moved_ref, near_ref, conv_ref, cpe_ref, w_ref, cols_ref, out_ref,
    x_ref, index_ref, picked_ref, leave_ref, sem, send_sem, recv_sem, *scratch
):
    member, group = lax.axis_index("mp"), lax.axis_index("order")
    barrier, count = greet(False, False)
    start = pl.multiple_of(member * PATCH, PATCH)
    copy = pltpu.make_async_copy(near_ref.at[:, pl.ds(start, PATCH)], index_ref, sem)
    copy.start()
    copy.wait()
    first_token = group * TOK + member * PATCH

    def column(k):
        return cols_ref[:, k : k + 1]

    cpe = cpe_ref[...].T
    places = iota((512, 256), 0)
    for c in range(4):
        span = slice(c * 256, c * 256 + 256)
        window = wide_ref[:, c * 256 : c * 256 + 512]
        origin = first_token + c * 256 - HALO

        def pick(k, carry):
            near = index_ref[pl.ds(k, 1), span]
            near = jnp.where(near < 0, -1, near - origin)
            rows = pl.ds(pl.multiple_of(k * C, C), C)
            picked_ref[rows, :] = dot(window, one_hot(places, near)).astype(bf16)
            return carry

        lax.fori_loop(0, OFFS, pick, 0, unroll=3)
        conv = (dot(conv_ref[...], picked_ref[...]) + column(COL_CONV)).astype(bf16)
        mixture = dot(cpe, conv) + column(COL_CPE)
        x_ref[:, span] = moved_ref[:, span] + norm_columns(
            mixture, column(COL_GAIN + 2), column(COL_SHIFT + 2)
        )

    pl.semaphore_wait(barrier, count)
    copies = []

    def emit(c, value):
        span = slice(c * 256, c * 256 + 256)
        place = pl.ds(pl.multiple_of(member * PATCH + c * 256, 256), 256)
        leave_ref[:, span] = value
        for d in (2, 3, 1):
            target = member ^ d
            copy = remote(
                leave_ref.at[pl.ds(pl.multiple_of(target * 64, 64), 64), span], out_ref.at[:, place],
                send_sem.at[c, d], recv_sem.at[c, d], (group, target),
            )
            copy.start()
            copies.append(copy)
        out_ref[:, place] = leave_ref[pl.ds(pl.multiple_of(member * 64, 64), 64), span]

    run_block(1, 3, x_ref, w_ref, 0, cols_ref, scratch, emit, lambda: None)
    for copy in copies:
        copy.wait()


def second_block(wide, moved, neighbours, conv, cpe, weights, cols):
    return pl.pallas_call(
        second_kernel,
        out_shape=S((64, TOK), f32),
        in_specs=[VMEM, VMEM, ANY, VMEM, VMEM, VMEM, VMEM],
        out_specs=VMEM,
        scratch_shapes=[
            pltpu.VMEM((C, PATCH), f32),
            pltpu.VMEM((OFFS, PATCH), i32),
            pltpu.VMEM((OFFS * C, 256), bf16),
            pltpu.VMEM((C, PATCH), f32),
            pltpu.SemaphoreType.DMA,
            pltpu.SemaphoreType.DMA((4, 4)),
            pltpu.SemaphoreType.DMA((4, 4)),
        ]
        + block_scratch(),
        compiler_params=kernel_params(collective_id=3, has_side_effects=True),
        name="second_block",
    )(wide, moved, neighbours, conv, cpe, weights, cols)


def shards(
    feats, serial_rank, neighbours, norm_gain, norm_bias, qkv_weight, qkv_bias, proj_weight, proj_bias,
    fc1_weight, fc1_bias, fc2_weight, fc2_bias, conv_weight, conv_bias, cpe_weight, cpe_bias,
):
    conv = conv_weight.transpose(2, 0, 1).reshape(64, OFFS * C)
    conv = lax.all_gather(conv, "mp", axis=0, tiled=True)
    own = jnp.concatenate(
        [qkv_weight[1].transpose(0, 2, 1).reshape(192, C), proj_weight[1], fc1_weight[1].T, fc2_weight[1].T],
        axis=0,
    )
    weights = lax.all_gather(own, "mp", axis=0, tiled=False)
    send, listed, landing, leave = routes(serial_rank.reshape(32, 128))
    rows, cols = first_block(
        feats, qkv_weight, proj_weight, fc1_weight, fc2_weight, norm_gain, norm_bias, qkv_bias, proj_bias,
        fc1_bias, fc2_bias, conv_bias.reshape(1, 64), cpe_bias.reshape(1, C), leave,
    )
    moved, wide = relay(rows, send, listed, landing)
    return second_block(wide, moved, neighbours, conv, cpe_weight, weights, cols)


def solution(mesh):
    in_specs = (
        P(None, "order"),
        P("order"),
        P(None, "order"),
        P(),
        P(),
        P(None, None, None, "mp"),
        P(None, None, "mp"),
        P(None, "mp", None),
        P(),
        P(None, None, "mp"),
        P(None, "mp"),
        P(None, "mp", None),
        P(),
        P(None, None, "mp"),
        P("mp"),
        P(),
        P(),
    )
    return jax.shard_map(shards, mesh=mesh, in_specs=in_specs, out_specs=P("mp", "order"), check_vma=False)
```

time: 324 us -> 243 us (0.75); the launches traced: 320 us -> 243 us
  waiting for transfers between devices: 98 us -> 0.06 us
  Pallas kernels: 135 us -> 217 us
  starting transfers between devices: 31.4 us -> 0.04 us
  blocking collectives: 23.3 us -> 0 us
  local copies, waits for them, and re-layouts: 16.6 us -> 10.9 us
    pallas_call x8 -> x4, Pallas kernels: 135 us -> 217 us  [the longest x1 66.4 us: first_block(): pl.pallas_call(first_kernel, out_shape=[S((4 * CAP_OUT, 2, 128), f32), S(...]
    all_gather x3 -> x1, waiting for transfers between devices: 53.7 us -> 0.02 us  [shards(): weights = lax.all_gather(own, 'mp', axis=0, tiled=False)]
    all_to_all x4 -> x0, waiting for transfers between devices: 43.2 us -> none  [the longest x1 30.9 us: shards(): lax.all_to_all(frames, 'order', split_axis=0, concat_axis=0, tiled=True)]
    all_to_all x4 -> x0, starting transfers between devices: 26.5 us -> none  [the longest x1 9.11 us: shards(): lax.all_to_all(spots, 'order', split_axis=0, concat_axis=0, tiled=True)]
    all_to_all x1 -> x0, blocking collectives: 16.9 us -> none  [shards(): return lax.all_to_all(result, 'mp', split_axis=0, concat_axis=1, tiled=True)]
    all_gather x1 -> x0, blocking collectives: 6.4 us -> none  [shards(): small = lax.all_gather(small, 'mp', axis=0, tiled=False).astype(f32)]
    ppermute x2 -> x0, starting transfers between devices: 4.8 us -> none  [the longest x1 2.74 us: shards(): before = lax.ppermute(low[:, PATCH - HALO:], ('order', 'mp'), up)]
  transfers between devices with their start and end apart: 10 -> 2, of which waited for: 5 -> 0; matrix products, arithmetic and copies ran while one was open for 3% -> 2% of each run, Pallas kernels for 16% -> 63%
where the time goes in v2:
time: 243 us
  Pallas kernels  217 us (89%)
  between operations  13.5 us (6%)
  local copies, waits for them, and re-layouts  10.9 us (4%)
    pallas_call x1, Pallas kernels, first_block(): pl.pallas_call(first_kernel, out_shape=[S((4 * CAP_OUT, 2, 128), f32), S(...  66.4 us
    pallas_call x1, Pallas kernels, second_block(): pl.pallas_call(second_kernel, out_shape=S((64, TOK), f32), in_specs=[VMEM...  64.1 us
    pallas_call x1, Pallas kernels, relay(): pl.pallas_call(relay_kernel, out_shape=[S((C, PATCH), f32), S((C, PATCH +...  61.1 us
    pallas_call x1, Pallas kernels, routes(): pl.pallas_call(routes_kernel, out_shape=[S((32, SLOTS), i32), S((4, CAP),...  25.5 us
  transfers between devices with their start and end apart: 2, of which 0 were waited for; matrix products, arithmetic and copies ran while one was open for 2% of the time, Pallas kernels for 63%

profile of v2, /device:TPU:1, one launch (start us, length us, event | category | flops | bytes accessed | tf_op | source)
XLA Modules:
  0.0 242.5 jit_solution(5944876461022394595)
XLA Ops:
  6.5 0.0 copy-start
  6.5 0.0 all-gather.6.cloned.1.call-start
  6.5 1.0 slice.12
  7.5 0.1 copy.28
  7.6 0.8 slice.13
  8.4 0.1 copy.30
  8.5 1.0 slice_bitcast_fusion
  9.5 0.9 pad_maximum_fusion
  10.4 0.0 copy-start.1
  10.4 0.0 all-gather.6.cloned.1.call-update
  10.4 0.0 all-gather.4.cloned.1.call-start
  10.5 0.0 copy-done
  10.5 0.0 copy-start.2
  10.5 0.0 copy-start.3
  10.5 1.0 copy.31
  11.5 0.0 all-gather.4.cloned.1.call-update
  11.5 0.0 copy-done.1
  11.5 0.9 copy.24.qkv_w_ref
  12.4 25.5 %routes.1 = (s32[32,64]{1,0:T(8,128)}, s32[4,288]{1,0:T(4,128)}, s32[1,1024]{1,0:T(1,128)}, s32[4,352]{1,0:T(4,128)}) custom-call(s32[32,128]{1,0:T(8,128)} %bitcast.25), custom_call_target="tpu_custom_call" | custom-call | tf_op jit(solution)/shard_map/routes/pallas_call | solution.py:231
  37.9 0.0 copy-done.2
  37.9 0.6 copy.25.qkv_b_ref
  38.5 0.0 copy-done.3
  38.5 0.6 reshape.16.cpe_b_ref
  39.1 66.4 %first_block.1 = (f32[1408,2,128]{2,1,0:T(2,128)}, f32[256,128]{1,0:T(8,128)}) custom-call(f32[256,4096]{1,0:T(8,128)} %feats_ref.1, bf16[2,3,256,64]{3,2,1,0:T(8,128)(2,1)} %copy.24.qkv_w_ref, bf16[2,64,256]{2,1,0:T(8,128)(2,1)} %proj_w_ref.1, bf16[2,256,256]{2,1,0:T(8,128)(2,1)} %fc1_w_ref.1, bf16[2,256,256]{2,1,0:T(8,128)(2,1)} %fc2_w_ref.1, ...), custom_call_target="tpu_custom_call" | custom-call | tf_op jit(solution)/shard_map/first_block/pallas_call | solution.py:555
  105.5 61.1 %relay.1 = (f32[256,1024]{1,0:T(8,128)}, bf16[256,1280]{1,0:T(8,128)(2,1)}) custom-call(f32[1408,2,128]{2,1,0:T(2,128)} %get-tuple-element.14.rows_ref, s32[32,64]{1,0:T(8,128)} %get-tuple-element.15.send_ref, s32[4,288]{1,0:T(4,128)} %get-tuple-element.16.listed_ref, s32[1,1024]{1,0:T(1,128)} %get-tuple-element.17.landing_ref), custom_call_target="tpu_custom_call" | custom-call | tf_op jit(solution)/shard_map/relay/pallas_call | solution.py:360
  166.6 0.0 all-gather.6.cloned.1.call-done
  166.7 2.6 %copy.29 = bf16[3072,256]{1,0:T(8,128)(2,1)} copy(bf16[3072,256]{0,1:T(8,128)(2,1)} %all-gather.6.cloned.1.call-done) | data formatting | bytes 3145728 | tf_op jit(solution)/shard_map/all_gather | solution.py:667
  169.3 0.0 all-gather.4.cloned.1.call-done.conv_ref
  169.3 64.1 %second_block.1 = f32[64,4096]{1,0:T(8,128)} custom-call(bf16[256,1280]{1,0:T(8,128)(2,1)} %get-tuple-element.18.wide_ref, f32[256,1024]{1,0:T(8,128)} %get-tuple-element.19.moved_ref, s32[27,4096]{1,0:T(8,128)} %near_ref.1, bf16[256,6912]{1,0:T(8,128)(2,1)} %all-gather.4.cloned.1.call-done.conv_ref, bf16[256,256]{1,0:T(8,128)(2,1)} %cpe_ref.1, ...), custom_call_target="tpu_custom_call" | custom-call | tf_op jit(solution)/shard_map/second_block/pallas_call | solution.py:637
  233.4 2.3 copy.33
Async XLA Ops:
  6.5 3.9 %copy-start = (bf16[27,256,64]{1,2,0:T(8,128)(2,1)S(1)}, bf16[27,256,64]{1,2,0:T(8,128)(2,1)}, u32[]{:S(2)}) copy-start(bf16[27,256,64]{1,2,0:T(8,128)(2,1)} %param.30) | copy-start | bytes 2654212
  6.5 160.1 %all-gather.6.cloned.1.call-start = ((), (), s32[]{:S(2)}) async-start(), calls=%async_computation.1 | async-start | bytes 1966080 | tf_op jit(solution)/shard_map/all_gather | solution.py:667
  10.4 1.1 copy-start.1
  10.4 158.9 %all-gather.4.cloned.1.call-start = ((), (), s32[]{:S(2)}) async-start(), calls=%async_computation | async-start | bytes 4423680 | tf_op jit(solution)/shard_map/all_gather | solution.py:662
  10.5 27.4 %copy-start.2 = (bf16[2,3,64]{2,0,1:T(2,128)(2,1)S(1)}, bf16[2,3,64]{2,0,1:T(2,128)(2,1)}, u32[]{:S(2)}) copy-start(bf16[2,3,64]{2,0,1:T(2,128)(2,1)} %param.23) | copy-start | bytes 2308
  10.5 28.0 %copy-start.3 = (bf16[256]{0:T(256)(128)(2,1)S(1)}, bf16[256]{0:T(256)(128)(2,1)}, u32[]{:S(2)}) copy-start(bf16[256]{0:T(256)(128)(2,1)} %param.33) | copy-start | bytes 1540
Sparse Core Ops, SparseCore 0:
  10.5 28.9 all-gather.5
  41.2 58.4 all-gather.3

commit v3 on v2

--- a/solution.py
+++ b/solution.py
@@ -57,7 +57,7 @@
     return centred * lax.rsqrt(variance + EPS) * gain + shift
 
 
-def greet(order_peers, halo):
+def greet(order_peers=False, halo=False, across=False):
     barrier = pltpu.get_barrier_semaphore()
     group, member = lax.axis_index("order"), lax.axis_index("mp")
     for d in range(1, 4):
@@ -71,6 +71,9 @@
 
         lax.fori_loop(1, ORDERS, step, 0)
         count += ORDERS - 1
+    if across:
+        pl.semaphore_signal(barrier, inc=1, device_id=(group ^ 1, member ^ 2), device_id_type=MESH)
+        count += 1
     if halo:
         for shift in (1, 127):
             pl.semaphore_signal(barrier, inc=1, device_id=neighbour(shift), device_id_type=MESH)
@@ -89,16 +92,15 @@
     )
 
 
-def routes_kernel(
-    rank_ref, send_ref, listed_ref, landing_ref, leave_ref,
-    made_ref, slot_ref, spot_ref, left_ref, right_ref, left2_ref, right2_ref,
-    pos_out, pos_in, place_out, place_in, send_sem, recv_sem, send2_sem, recv2_sem,
-):
+def prefix_matrix():
+    upper = jnp.where(iota((128, 128), 0) < iota((128, 128), 1), 1.0, 0.0).astype(bf16)
+    return jnp.concatenate([upper, jnp.ones((128, 128), bf16)], axis=1)
+
+
+def route_slots(rank_ref, send_ref, leave_ref, scratch):
+    (made_ref, slot_ref, spot_ref, left_ref, right_ref, left2_ref, right2_ref, pos_out, pos_in) = scratch[:9]
     group, member = lax.axis_index("order"), lax.axis_index("mp")
-    barrier, count = greet(True, False)
-    rank = rank_ref[...]
-    upper = jnp.where(iota((128, 128), 0) < iota((128, 128), 1), 1.0, 0.0).astype(bf16)
-    both = jnp.concatenate([upper, jnp.ones((128, 128), bf16)], axis=1)
+    both = prefix_matrix()
     lane = iota((1, 128), 1)
 
     def classes(c):
@@ -149,19 +151,8 @@
     pos_out[...] = jnp.broadcast_to(inside[:, None, :], (32, 8, 128))
     pos_in[group] = pos_out[group]
 
-    pl.semaphore_wait(barrier, count)
-
-    def frame_copy(d):
-        return remote(
-            pos_out.at[group ^ d], pos_in.at[group], send_sem.at[d], recv_sem.at[d], (group ^ d, member)
-        )
-
     def frame_start(d, carry):
-        frame_copy(d).start()
-        return carry
-
-    def frame_wait(d, carry):
-        frame_copy(d).wait()
+        place_frame_copy(scratch, d).start()
         return carry
 
     lax.fori_loop(1, ORDERS, frame_start, 0)
@@ -180,8 +171,19 @@
     acc = dot_rows(left2_ref[...], right2_ref[...])
     leave_ref[...] = (acc[0:4] * 64.0 + acc[8:12]).astype(i32)
 
+
+def route_lists(listed_ref, scratch):
+    _, slot_ref, spot_ref, _, _, _, _, _, pos_in, place_out, place_in = scratch[:11]
+    group, member = lax.axis_index("order"), lax.axis_index("mp")
+    both = prefix_matrix()
+    lane = iota((1, 128), 1)
+
+    def frame_wait(d, carry):
+        place_frame_copy(scratch, d).wait()
+        return carry
+
     lax.fori_loop(1, ORDERS, frame_wait, 0)
-
+    row, col = iota((256, 256), 0), iota((256, 256), 1)
     pos = pos_in[:, 0, :]
     hot = jnp.where(iota((32, 8, 128), 1) == (pos // PATCH)[:, None, :], 1.0, 0.0).reshape(256, 128)
     made = dot(hot.astype(bf16), both)
@@ -204,18 +206,14 @@
     place = jnp.where(acc[32:36] > 0.5, (acc[16:20] * 32.0 + acc[24:28]).astype(i32), -1)
     place_out[...] = jnp.broadcast_to(place[:, None, :], (4, 8, 384))
     place_in[member] = place_out[member]
-    copies = [
-        remote(
-            place_out.at[member ^ d], place_in.at[member], send2_sem.at[d], recv2_sem.at[d],
-            (group, member ^ d),
-        )
-        for d in range(1, 4)
-    ]
-    for copy in copies:
-        copy.start()
-    for copy in copies:
-        copy.wait()
-
+    for d in range(1, 4):
+        place_list_copy(scratch, d).start()
+
+
+def route_landing(landing_ref, scratch):
+    place_in = scratch[10]
+    for d in range(1, 4):
+        place_list_copy(scratch, d).wait()
     acc = jnp.zeros((8, PATCH), f32)
     entry = iota((1, 384), 1)
     kind = iota((8, 384), 0)
@@ -227,32 +225,40 @@
     landing_ref[...] = (acc[0:1] * 64.0 + acc[1:2]).astype(i32)
 
 
-def routes(rank):
-    return pl.pallas_call(
-        routes_kernel,
-        out_shape=[S((32, SLOTS), i32), S((4, CAP), i32), S((1, PATCH), i32), S((4, CAP_OUT), i32)],
-        in_specs=[VMEM],
-        out_specs=[VMEM] * 4,
-        scratch_shapes=[
-            pltpu.VMEM((32, 128, 256), f32),
-            pltpu.VMEM((32, 128), i32),
-            pltpu.VMEM((32, 128), i32),
-            pltpu.VMEM((160, TOK), bf16),
-            pltpu.VMEM((SLOTS, TOK), bf16),
-            pltpu.VMEM((16, PATCH), bf16),
-            pltpu.VMEM((CAP_OUT, PATCH), bf16),
-            pltpu.VMEM((32, 8, 128), i32),
-            pltpu.VMEM((32, 8, 128), i32),
-            pltpu.VMEM((4, 8, 384), i32),
-            pltpu.VMEM((4, 8, 384), i32),
-            pltpu.SemaphoreType.DMA((ORDERS,)),
-            pltpu.SemaphoreType.DMA((ORDERS,)),
-            pltpu.SemaphoreType.DMA((4,)),
-            pltpu.SemaphoreType.DMA((4,)),
-        ],
-        compiler_params=kernel_params(collective_id=0, has_side_effects=True),
-        name="routes",
-    )(rank)
+def place_frame_copy(scratch, d):
+    group, member = lax.axis_index("order"), lax.axis_index("mp")
+    pos_out, pos_in, send_sem, recv_sem = scratch[7], scratch[8], scratch[11], scratch[12]
+    return remote(
+        pos_out.at[group ^ d], pos_in.at[group], send_sem.at[d], recv_sem.at[d], (group ^ d, member)
+    )
+
+
+def place_list_copy(scratch, d):
+    group, member = lax.axis_index("order"), lax.axis_index("mp")
+    place_out, place_in, send_sem, recv_sem = scratch[9], scratch[10], scratch[13], scratch[14]
+    return remote(
+        place_out.at[member ^ d], place_in.at[member], send_sem.at[d], recv_sem.at[d], (group, member ^ d)
+    )
+
+
+def route_scratch():
+    return [
+        pltpu.VMEM((32, 128, 256), f32),
+        pltpu.VMEM((32, 128), i32),
+        pltpu.VMEM((32, 128), i32),
+        pltpu.VMEM((160, TOK), bf16),
+        pltpu.VMEM((SLOTS, TOK), bf16),
+        pltpu.VMEM((16, PATCH), bf16),
+        pltpu.VMEM((CAP_OUT, PATCH), bf16),
+        pltpu.VMEM((32, 8, 128), i32),
+        pltpu.VMEM((32, 8, 128), i32),
+        pltpu.VMEM((4, 8, 384), i32),
+        pltpu.VMEM((4, 8, 384), i32),
+        pltpu.SemaphoreType.DMA((ORDERS,)),
+        pltpu.SemaphoreType.DMA((ORDERS,)),
+        pltpu.SemaphoreType.DMA((4,)),
+        pltpu.SemaphoreType.DMA((4,)),
+    ]
 
 
 def move_rows(count, index, source, store):
@@ -266,13 +272,35 @@
 
 
 def relay_kernel(
-    rows_ref, send_ref, listed_ref, landing_ref, moved_ref, wide_ref,
-    out_ref, frames_ref, sorted_ref, lists_ref, land_ref,
-    send_sem, recv_sem, send2_sem, recv2_sem, send3_sem, recv3_sem,
+    records_ref, leave_ref, send_ref, listed_ref, landing_ref, moved_ref, wide_ref,
+    leaving_ref, rows_ref, out_ref, frames_ref, sorted_ref, lists_ref, land_ref,
+    send_sem, recv_sem, send2_sem, recv2_sem, send3_sem, recv3_sem, send4_sem, recv4_sem,
 ):
     group, member = lax.axis_index("order"), lax.axis_index("mp")
-    barrier, count = greet(True, True)
-    pl.semaphore_wait(barrier, count)
+    barrier, count = greet(order_peers=True, halo=True)
+    copies = []
+    for d in (2, 3, 1):
+        target = member ^ d
+
+        def store(r, record, d=d):
+            leaving_ref[d, r] = record
+
+        move_rows(CAP_OUT, lambda r: leave_ref[target, r], records_ref, store)
+        if d == 2:
+            pl.semaphore_wait(barrier, count)
+        copy = remote(
+            leaving_ref.at[d], rows_ref.at[pl.ds(member * CAP_OUT, CAP_OUT)], send4_sem.at[d], recv4_sem.at[d],
+            (group, target),
+        )
+        copy.start()
+        copies.append(copy)
+
+    def store_staying(r, record):
+        rows_ref[member * CAP_OUT + r] = record
+
+    move_rows(CAP_OUT, lambda r: leave_ref[member, r], records_ref, store_staying)
+    for copy in copies:
+        copy.wait()
 
     def frame_copy(d):
         return remote(
@@ -280,7 +308,8 @@
             send_sem.at[d], recv_sem.at[d], (group ^ d, member),
         )
 
-    def pack(d, carry):
+    def pack(t, carry):
+        d = 1 + (t + 8 * member + 7 * group) % (ORDERS - 1)
         target = group ^ d
 
         def store(r, record):
@@ -290,7 +319,7 @@
         frame_copy(d).start()
         return carry
 
-    lax.fori_loop(1, ORDERS, pack, 0)
+    lax.fori_loop(0, ORDERS - 1, pack, 0)
 
     def store_own(r, record):
         frames_ref[group * SLOTS + r] = record
@@ -331,20 +360,20 @@
 
         move_rows(rows, lambda r: landing_ref[0, start + r], lists_ref, store)
         for half in range(2):
-            part = land_ref[start : start + rows, half, :].T
+            part = land_ref[start : start + rows, half, :]
             at = slice(half * 128, half * 128 + 128)
-            moved_ref[at, start : start + rows] = part
-            wide_ref[at, HALO + start : HALO + start + rows] = part.astype(bf16)
+            moved_ref[at, start : start + rows] = part.T
+            wide_ref[HALO + start : HALO + start + rows, at] = part.astype(bf16)
 
     land(0, HALO)
     land(PATCH - HALO, HALO)
     halos = [
         remote(
-            wide_ref.at[:, HALO : 2 * HALO], wide_ref.at[:, HALO + PATCH : 2 * HALO + PATCH],
+            wide_ref.at[HALO : 2 * HALO], wide_ref.at[HALO + PATCH : 2 * HALO + PATCH],
             send3_sem.at[0], recv3_sem.at[0], neighbour(127),
         ),
         remote(
-            wide_ref.at[:, PATCH : PATCH + HALO], wide_ref.at[:, 0:HALO],
+            wide_ref.at[PATCH : PATCH + HALO], wide_ref.at[0:HALO],
             send3_sem.at[1], recv3_sem.at[1], neighbour(1),
         ),
     ]
@@ -356,13 +385,15 @@
         copy.wait()
 
 
-def relay(rows, send, listed, landing):
+def relay(records, leave, send, listed, landing):
     return pl.pallas_call(
         relay_kernel,
-        out_shape=[S((C, PATCH), f32), S((C, PATCH + 2 * HALO), bf16)],
-        in_specs=[VMEM, SMEM, SMEM, SMEM],
+        out_shape=[S((C, PATCH), f32), S((PATCH + 2 * HALO, C), bf16)],
+        in_specs=[VMEM, SMEM, SMEM, SMEM, SMEM],
         out_specs=[VMEM, VMEM],
         scratch_shapes=[
+            pltpu.VMEM((4, CAP_OUT, 2, 128), f32),
+            pltpu.VMEM((4 * CAP_OUT, 2, 128), f32),
             pltpu.VMEM((ORDERS, SLOTS, 2, 128), f32),
             pltpu.VMEM((ORDERS * SLOTS, 2, 128), f32),
             pltpu.VMEM((4, CAP, 2, 128), f32),
@@ -374,10 +405,12 @@
             pltpu.SemaphoreType.DMA((4,)),
             pltpu.SemaphoreType.DMA((2,)),
             pltpu.SemaphoreType.DMA((2,)),
+            pltpu.SemaphoreType.DMA((4,)),
+            pltpu.SemaphoreType.DMA((4,)),
         ],
         compiler_params=kernel_params(collective_id=2, has_side_effects=True),
         name="relay",
-    )(rows, send, listed, landing)
+    )(records, leave, send, listed, landing)
 
 
 def block_scratch():
@@ -392,7 +425,7 @@
     ]
 
 
-def run_block(block, first_norm, x_ref, w_ref, base, cols_ref, scratch, emit, arrive):
+def run_block(block, first_norm, x_ref, w_ref, base, cols_ref, scratch, emit, between):
     normed_ref, qkv_ref, keys_ref, s0_ref, s1_ref, top_ref, heads_ref = scratch
 
     def column(k):
@@ -441,7 +474,7 @@
 
     lax.fori_loop(0, HEADS // 2, pair, 0)
 
-    arrive()
+    between()
     proj = [w_ref[r, base + 192 : base + 256, :].T for r in range(4)]
     for c in range(4):
         span = slice(c * 256, c * 256 + 256)
@@ -463,11 +496,14 @@
 
 def first_kernel(
     feats_ref, qkv_w_ref, proj_w_ref, fc1_w_ref, fc2_w_ref, gain_ref, shift_ref, qkv_b_ref, proj_b_ref,
-    fc1_b_ref, fc2_b_ref, conv_b_ref, cpe_b_ref, leave_ref, rows_ref, cols_ref,
-    x_ref, w_ref, params_ref, records_ref, sorted_ref, sem, send_sem, recv_sem, send2_sem, recv2_sem, *scratch
+    fc1_b_ref, fc2_b_ref, conv_b_ref, cpe_b_ref, conv_w_ref, rank_ref,
+    records_ref, cols_ref, send_ref, listed_ref, landing_ref, leave_ref, conv_ref, later_ref,
+    x_ref, w_ref, params_ref, conv_own_ref, later_own_ref,
+    sem, send_sem, recv_sem, local_sem, send3_sem, recv3_sem, *scratch
 ):
     group, member = lax.axis_index("order"), lax.axis_index("mp")
-    barrier, count = greet(False, False)
+    routing, scratch = scratch[:15], scratch[15:]
+    barrier, count = greet(order_peers=True, across=True)
     start = pl.multiple_of(member * PATCH, PATCH)
     load = pltpu.make_async_copy(feats_ref.at[:, pl.ds(start, PATCH)], x_ref, sem)
     load.start()
@@ -498,6 +534,27 @@
     w_ref[member, 528:784, :] = fc2_w_ref[0].T
     for d in (2, 3, 1):
         weight_copy(1, d).start()
+
+    def turn(k, carry):
+        span = pl.ds(pl.multiple_of(k * C, C), C)
+        conv_own_ref[:, span] = conv_w_ref[k].T
+        return carry
+
+    lax.fori_loop(0, OFFS, turn, 0, unroll=3)
+    for j in range(3):
+        later_own_ref[j * 64 : j * 64 + 64, :] = qkv_w_ref[1, j].T
+    later_own_ref[192:256, :] = proj_w_ref[1]
+    later_own_ref[256:512, :] = fc1_w_ref[1].T
+    later_own_ref[512:768, :] = fc2_w_ref[1].T
+    later = [
+        remote(conv_own_ref, conv_ref.at[1], send3_sem.at[0], recv3_sem.at[0], (group ^ 1, member ^ 2)),
+        remote(later_own_ref, later_ref.at[1], send3_sem.at[1], recv3_sem.at[1], (group, member ^ 2)),
+        pltpu.make_async_copy(conv_own_ref, conv_ref.at[0], local_sem.at[0]),
+        pltpu.make_async_copy(later_own_ref, later_ref.at[0], local_sem.at[1]),
+    ]
+    for copy in later:
+        copy.start()
+    route_slots(rank_ref, send_ref, leave_ref, routing)
     load.wait()
     for d in (2, 3, 1):
         weight_copy(0, d).wait()
@@ -522,53 +579,46 @@
         for half in range(2):
             records_ref[c * 256 : c * 256 + 256, half, :] = rows[:, half * 128 : half * 128 + 128]
 
-    def arrive():
+    def between():
+        route_lists(listed_ref, routing)
         for d in (2, 3, 1):
             weight_copy(1, d).wait()
 
-    run_block(0, 0, x_ref, w_ref, 16, cols_ref, scratch, emit, arrive)
-
-    copies = []
-    for d in (2, 3, 1):
-        target = member ^ d
-
-        def store(r, record, d=d):
-            sorted_ref[d, r] = record
-
-        move_rows(CAP_OUT, lambda r: leave_ref[target, r], records_ref, store)
-        copy = remote(
-            sorted_ref.at[d], rows_ref.at[pl.ds(member * CAP_OUT, CAP_OUT)], send2_sem.at[d], recv2_sem.at[d],
-            (group, target),
-        )
-        copy.start()
-        copies.append(copy)
-
-    def store_mine(r, record):
-        rows_ref[member * CAP_OUT + r] = record
-
-    move_rows(CAP_OUT, lambda r: leave_ref[member, r], records_ref, store_mine)
-    for copy in copies:
+    run_block(0, 0, x_ref, w_ref, 16, cols_ref, scratch, emit, between)
+    route_landing(landing_ref, routing)
+    for copy in later:
         copy.wait()
 
 
 def first_block(*operands):
     return pl.pallas_call(
         first_kernel,
-        out_shape=[S((4 * CAP_OUT, 2, 128), f32), S((C, 128), f32)],
-        in_specs=[ANY] + [VMEM] * 12 + [SMEM],
-        out_specs=[VMEM, VMEM],
+        out_shape=[
+            S((PATCH, 2, 128), f32),
+            S((C, 128), f32),
+            S((ORDERS, SLOTS), i32),
+            S((4, CAP), i32),
+            S((1, PATCH), i32),
+            S((4, CAP_OUT), i32),
+            S((2, 64, OFFS * C), bf16),
+            S((2, 768, C), bf16),
+        ],
+        in_specs=[ANY] + [VMEM] * 14,
+        out_specs=[VMEM] * 6 + [ANY] * 2,
         scratch_shapes=[
             pltpu.VMEM((C, PATCH), f32),
             pltpu.VMEM((4, 784, C), bf16),
             pltpu.VMEM((128, C), f32),
-            pltpu.VMEM((PATCH, 2, 128), f32),
-            pltpu.VMEM((4, CAP_OUT, 2, 128), f32),
+            pltpu.VMEM((64, OFFS * C), bf16),
+            pltpu.VMEM((768, C), bf16),
             pltpu.SemaphoreType.DMA,
             pltpu.SemaphoreType.DMA((2, 4)),
             pltpu.SemaphoreType.DMA((2, 4)),
-            pltpu.SemaphoreType.DMA((4,)),
-            pltpu.SemaphoreType.DMA((4,)),
+            pltpu.SemaphoreType.DMA((2,)),
+            pltpu.SemaphoreType.DMA((2,)),
+            pltpu.SemaphoreType.DMA((2,)),
         ]
+        + route_scratch()
         + block_scratch(),
         compiler_params=kernel_params(collective_id=1, has_side_effects=True),
         name="first_block",
@@ -576,42 +626,67 @@
 
 
 def second_kernel(
-    wide_ref, moved_ref, near_ref, conv_ref, cpe_ref, w_ref, cols_ref, out_ref,
-    x_ref, index_ref, picked_ref, leave_ref, sem, send_sem, recv_sem, *scratch
+    wide_ref, moved_ref, near_ref, conv_ref, cpe_ref, later_ref, cols_ref, out_ref,
+    x_ref, index_ref, places_ref, hot_ref, picked_ref, conv_w_ref, w_ref, leave_ref,
+    sem, local_sem, send2_sem, recv2_sem, send_sem, recv_sem, *scratch
 ):
     member, group = lax.axis_index("mp"), lax.axis_index("order")
-    barrier, count = greet(False, False)
+    barrier, count = greet()
     start = pl.multiple_of(member * PATCH, PATCH)
-    copy = pltpu.make_async_copy(near_ref.at[:, pl.ds(start, PATCH)], index_ref, sem)
-    copy.start()
-    copy.wait()
+    load = pltpu.make_async_copy(near_ref.at[:, pl.ds(start, PATCH)], index_ref, sem)
+    load.start()
     first_token = group * TOK + member * PATCH
 
     def column(k):
         return cols_ref[:, k : k + 1]
 
+    shares = []
+    for i, owner in enumerate((member, member ^ 2)):
+        rows = pl.ds(pl.multiple_of(owner * 64, 64), 64)
+        shares += [
+            pltpu.make_async_copy(conv_ref.at[i], conv_w_ref.at[rows], local_sem.at[i]),
+            pltpu.make_async_copy(later_ref.at[i], w_ref.at[owner], local_sem.at[2 + i]),
+        ]
+    for copy in shares:
+        copy.start()
+    pl.semaphore_wait(barrier, count)
+    for i, owner in enumerate((member, member ^ 2)):
+        rows = pl.ds(pl.multiple_of(owner * 64, 64), 64)
+        crossing = [
+            remote(conv_ref.at[i], conv_w_ref.at[rows], send2_sem.at[i], recv2_sem.at[i], (group, member ^ 1)),
+            remote(later_ref.at[i], w_ref.at[owner], send2_sem.at[2 + i], recv2_sem.at[2 + i], (group, member ^ 1)),
+        ]
+        for copy in crossing:
+            copy.start()
+        shares += crossing
+
+    load.wait()
+    near = index_ref[...]
+    near = jnp.where(near < 0, -1, near - (first_token - HALO))
+    places_ref[...] = jnp.concatenate([near, jnp.full((128 - OFFS, PATCH), -1, i32)], axis=0).T
+    lanes = iota((256, 512), 1)
+    for c in range(4):
+        window = wide_ref[c * 256 : c * 256 + 512, :]
+        places = places_ref[c * 256 : c * 256 + 256, :] - c * 256
+        for b in range(OFFS // 3):
+            for k in range(3):
+                hot_ref[b % 2, k * 256 : k * 256 + 256, :] = one_hot(lanes, places[:, 3 * b + k : 3 * b + k + 1])
+            picked = dot(hot_ref[b % 2], window).astype(bf16)
+            for k in range(3):
+                at = (3 * b + k) * C
+                picked_ref[c * 256 : c * 256 + 256, at : at + C] = picked[k * 256 : k * 256 + 256]
+    for copy in shares:
+        copy.wait()
+    summed = dot_rows(picked_ref[...], conv_w_ref[...]).T
+    conv = (summed + column(COL_CONV)).astype(bf16)
     cpe = cpe_ref[...].T
-    places = iota((512, 256), 0)
     for c in range(4):
         span = slice(c * 256, c * 256 + 256)
-        window = wide_ref[:, c * 256 : c * 256 + 512]
-        origin = first_token + c * 256 - HALO
-
-        def pick(k, carry):
-            near = index_ref[pl.ds(k, 1), span]
-            near = jnp.where(near < 0, -1, near - origin)
-            rows = pl.ds(pl.multiple_of(k * C, C), C)
-            picked_ref[rows, :] = dot(window, one_hot(places, near)).astype(bf16)
-            return carry
-
-        lax.fori_loop(0, OFFS, pick, 0, unroll=3)
-        conv = (dot(conv_ref[...], picked_ref[...]) + column(COL_CONV)).astype(bf16)
-        mixture = dot(cpe, conv) + column(COL_CPE)
+        mixture = dot(cpe, conv[:, span]) + column(COL_CPE)
         x_ref[:, span] = moved_ref[:, span] + norm_columns(
             mixture, column(COL_GAIN + 2), column(COL_SHIFT + 2)
         )
 
-    pl.semaphore_wait(barrier, count)
     copies = []
 
     def emit(c, value):
@@ -633,45 +708,45 @@
         copy.wait()
 
 
-def second_block(wide, moved, neighbours, conv, cpe, weights, cols):
+def second_block(wide, moved, neighbours, conv, cpe, later, cols):
     return pl.pallas_call(
         second_kernel,
         out_shape=S((64, TOK), f32),
-        in_specs=[VMEM, VMEM, ANY, VMEM, VMEM, VMEM, VMEM],
+        in_specs=[VMEM, VMEM, ANY, ANY, VMEM, ANY, VMEM],
         out_specs=VMEM,
         scratch_shapes=[
             pltpu.VMEM((C, PATCH), f32),
             pltpu.VMEM((OFFS, PATCH), i32),
-            pltpu.VMEM((OFFS * C, 256), bf16),
+            pltpu.VMEM((PATCH, 128), i32),
+            pltpu.VMEM((2, 3 * 256, 512), bf16),
+            pltpu.VMEM((PATCH, OFFS * C), bf16),
+            pltpu.VMEM((C, OFFS * C), bf16),
+            pltpu.VMEM((4, 768, C), bf16),
             pltpu.VMEM((C, PATCH), f32),
             pltpu.SemaphoreType.DMA,
+            pltpu.SemaphoreType.DMA((4,)),
+            pltpu.SemaphoreType.DMA((4,)),
+            pltpu.SemaphoreType.DMA((4,)),
             pltpu.SemaphoreType.DMA((4, 4)),
             pltpu.SemaphoreType.DMA((4, 4)),
         ]
         + block_scratch(),
         compiler_params=kernel_params(collective_id=3, has_side_effects=True),
         name="second_block",
-    )(wide, moved, neighbours, conv, cpe, weights, cols)
+    )(wide, moved, neighbours, conv, cpe, later, cols)
 
 
 def shards(
     feats, serial_rank, neighbours, norm_gain, norm_bias, qkv_weight, qkv_bias, proj_weight, proj_bias,
     fc1_weight, fc1_bias, fc2_weight, fc2_bias, conv_weight, conv_bias, cpe_weight, cpe_bias,
 ):
-    conv = conv_weight.transpose(2, 0, 1).reshape(64, OFFS * C)
-    conv = lax.all_gather(conv, "mp", axis=0, tiled=True)
-    own = jnp.concatenate(
-        [qkv_weight[1].transpose(0, 2, 1).reshape(192, C), proj_weight[1], fc1_weight[1].T, fc2_weight[1].T],
-        axis=0,
+    records, cols, send, listed, landing, leave, conv, later = first_block(
+        feats, qkv_weight, proj_weight, fc1_weight, fc2_weight, norm_gain, norm_bias, qkv_bias, proj_bias,
+        fc1_bias, fc2_bias, conv_bias.reshape(1, 64), cpe_bias.reshape(1, C), conv_weight,
+        serial_rank.reshape(32, 128),
     )
-    weights = lax.all_gather(own, "mp", axis=0, tiled=False)
-    send, listed, landing, leave = routes(serial_rank.reshape(32, 128))
-    rows, cols = first_block(
-        feats, qkv_weight, proj_weight, fc1_weight, fc2_weight, norm_gain, norm_bias, qkv_bias, proj_bias,
-        fc1_bias, fc2_bias, conv_bias.reshape(1, 64), cpe_bias.reshape(1, C), leave,
-    )
-    moved, wide = relay(rows, send, listed, landing)
-    return second_block(wide, moved, neighbours, conv, cpe_weight, weights, cols)
+    moved, wide = relay(records, leave, send, listed, landing)
+    return second_block(wide, moved, neighbours, conv, cpe_weight, later, cols)
 
 
 def solution(mesh):

time: 243 us -> 191 us (0.79)
  Pallas kernels: 217 us -> 181 us
  between operations: 13.5 us -> 0.03 us
    pallas_call x3 -> x2, Pallas kernels: 153 us -> 122 us  [the longest x1 70.2 us: relay(): pl.pallas_call(relay_kernel, out_shape=[S((C, PATCH), f32), S((PATCH + 2...]
    pallas_call x1, Pallas kernels: 64.1 us -> 59.3 us  [second_block(): pl.pallas_call(second_kernel, out_shape=S((64, TOK), f32), in_specs=[VMEM...]
    unnamed x12 -> x4, local copies, waits for them, and re-layouts: 3.91 us -> 7.95 us
    all_gather x1 -> x0, local copies, waits for them, and re-layouts: 2.62 us -> none  [shards(): weights = lax.all_gather(own, 'mp', axis=0, tiled=False)]
  transfers between devices with their start and end apart: 2 -> 0, of which waited for: 0 -> 0; matrix products, arithmetic and copies ran while one was open for 2% -> 0% of each run, Pallas kernels for 63% -> 0%
where the time goes in v3:
time: 191 us
  Pallas kernels  181 us (95%)
  local copies, waits for them, and re-layouts  9.15 us (5%)
    pallas_call x1, Pallas kernels, relay(): pl.pallas_call(relay_kernel, out_shape=[S((C, PATCH), f32), S((PATCH + 2...  70.2 us
    pallas_call x1, Pallas kernels, second_block(): pl.pallas_call(second_kernel, out_shape=S((64, TOK), f32), in_specs=[VMEM...  59.3 us
    pallas_call x1, Pallas kernels, first_block(): pl.pallas_call(first_kernel, out_shape=[S((PATCH, 2, 128), f32), S((C, 12...  51.9 us
    unnamed x4, local copies, waits for them, and re-layouts  7.95 us

profile of v3, /device:TPU:1, one launch (start us, length us, event | category | flops | bytes accessed | tf_op | source)
XLA Modules:
  0.0 190.5 jit_solution(7973936568427987880)
XLA Ops:
  0.0 1.2 reshape.10.cpe_b_ref
  1.2 1.3 copy.19.qkv_b_ref
  2.5 1.8 copy.18.qkv_w_ref
  4.3 2.6 %copy.20.conv_w_ref = bf16[27,256,64]{2,1,0:T(8,128)(2,1)} copy(bf16[27,256,64]{1,2,0:T(8,128)(2,1)} %param.30) | data formatting | bytes 1769472 | tf_op args[13]
  6.9 51.9 %first_block.1 = (f32[1024,2,128]{2,1,0:T(2,128)}, f32[256,128]{1,0:T(8,128)}, s32[32,64]{1,0:T(8,128)}, s32[4,288]{1,0:T(4,128)}, s32[1,1024]{1,0:T(1,128)}, /*...) custom-call(f32[256,4096]{1,0:T(8,128)} %feats_ref.1, ...), custom_call_target="tpu_custom_call" | custom-call | tf_op jit(solution)/shard_map/first_block/pallas_call | solution.py:594
  58.8 70.2 %relay.1 = (f32[256,1024]{1,0:T(8,128)}, bf16[1280,256]{1,0:T(8,128)(2,1)}) custom-call(f32[1024,2,128]{2,1,0:T(2,128)} %get-tuple-element.15.records_ref, s32[4,352]{1,0:T(4,128)} %get-tuple-element.16.leave_ref, s32[32,64]{1,0:T(8,128)} %get-tuple-element.17.send_ref, s32[4,288]{1,0:T(4,128)} %get-tuple-element.18.listed_ref, ...), custom_call_target="tpu_custom_call" | custom-call | tf_op jit(solution)/shard_map/relay/pallas_call | solution.py:389
  128.9 59.3 %second_block.1 = f32[64,4096]{1,0:T(8,128)} custom-call(bf16[1280,256]{1,0:T(8,128)(2,1)} %get-tuple-element.20.wide_ref, f32[256,1024]{1,0:T(8,128)} %get-tuple-element.21.moved_ref, s32[27,4096]{1,0:T(8,128)} %near_ref.1, bf16[2,64,6912]{2,1,0:T(8,128)(2,1)} %get-tuple-element.22.conv_ref, bf16[256,256]{1,0:T(8,128)(2,1)} %cpe_ref.1, ...), custom_call_target="tpu_custom_call" | custom-call | tf_op jit(solution)/shard_map/second_block/pallas_call | solution.py:712
  188.2 2.3 %copy.22 = f32[64,4096]{1,0:T(8,128)} copy(f32[64,4096]{1,0:T(8,128)} %second_block.1) | data formatting | bytes 2097152

commit v4 on v3

--- a/solution.py
+++ b/solution.py
@@ -31,7 +31,7 @@
 
 
 def kernel_params(**more):
-    return pltpu.CompilerParams(vmem_limit_bytes=56 * 2**20, **more)
+    return pltpu.CompilerParams(vmem_limit_bytes=61 * 2**20, **more)
 
 
 def iota(shape, dim):
@@ -271,148 +271,6 @@
     lax.fori_loop(0, count // 16, step, 0)
 
 
-def relay_kernel(
-    records_ref, leave_ref, send_ref, listed_ref, landing_ref, moved_ref, wide_ref,
-    leaving_ref, rows_ref, out_ref, frames_ref, sorted_ref, lists_ref, land_ref,
-    send_sem, recv_sem, send2_sem, recv2_sem, send3_sem, recv3_sem, send4_sem, recv4_sem,
-):
-    group, member = lax.axis_index("order"), lax.axis_index("mp")
-    barrier, count = greet(order_peers=True, halo=True)
-    copies = []
-    for d in (2, 3, 1):
-        target = member ^ d
-
-        def store(r, record, d=d):
-            leaving_ref[d, r] = record
-
-        move_rows(CAP_OUT, lambda r: leave_ref[target, r], records_ref, store)
-        if d == 2:
-            pl.semaphore_wait(barrier, count)
-        copy = remote(
-            leaving_ref.at[d], rows_ref.at[pl.ds(member * CAP_OUT, CAP_OUT)], send4_sem.at[d], recv4_sem.at[d],
-            (group, target),
-        )
-        copy.start()
-        copies.append(copy)
-
-    def store_staying(r, record):
-        rows_ref[member * CAP_OUT + r] = record
-
-    move_rows(CAP_OUT, lambda r: leave_ref[member, r], records_ref, store_staying)
-    for copy in copies:
-        copy.wait()
-
-    def frame_copy(d):
-        return remote(
-            out_ref.at[d], frames_ref.at[pl.ds(pl.multiple_of(group * SLOTS, SLOTS), SLOTS)],
-            send_sem.at[d], recv_sem.at[d], (group ^ d, member),
-        )
-
-    def pack(t, carry):
-        d = 1 + (t + 8 * member + 7 * group) % (ORDERS - 1)
-        target = group ^ d
-
-        def store(r, record):
-            out_ref[d, r] = record
-
-        move_rows(SLOTS, lambda r: send_ref[target, r], rows_ref, store)
-        frame_copy(d).start()
-        return carry
-
-    lax.fori_loop(0, ORDERS - 1, pack, 0)
-
-    def store_own(r, record):
-        frames_ref[group * SLOTS + r] = record
-
-    move_rows(SLOTS, lambda r: send_ref[group, r], rows_ref, store_own)
-
-    def frame_wait(d, carry):
-        frame_copy(d).wait()
-        return carry
-
-    lax.fori_loop(1, ORDERS, frame_wait, 0)
-
-    copies = []
-    for d in (2, 3, 1):
-        target = member ^ d
-
-        def store(r, record, d=d):
-            sorted_ref[d, r] = record
-
-        move_rows(CAP, lambda r: listed_ref[target, r], frames_ref, store)
-        copy = remote(
-            sorted_ref.at[d], lists_ref.at[pl.ds(member * CAP, CAP)], send2_sem.at[d], recv2_sem.at[d],
-            (group, target),
-        )
-        copy.start()
-        copies.append(copy)
-
-    def store_mine(r, record):
-        lists_ref[member * CAP + r] = record
-
-    move_rows(CAP, lambda r: listed_ref[member, r], frames_ref, store_mine)
-    for copy in copies:
-        copy.wait()
-
-    def land(start, rows):
-        def store(r, record):
-            land_ref[start + r] = record
-
-        move_rows(rows, lambda r: landing_ref[0, start + r], lists_ref, store)
-        for half in range(2):
-            part = land_ref[start : start + rows, half, :]
-            at = slice(half * 128, half * 128 + 128)
-            moved_ref[at, start : start + rows] = part.T
-            wide_ref[HALO + start : HALO + start + rows, at] = part.astype(bf16)
-
-    land(0, HALO)
-    land(PATCH - HALO, HALO)
-    halos = [
-        remote(
-            wide_ref.at[HALO : 2 * HALO], wide_ref.at[HALO + PATCH : 2 * HALO + PATCH],
-            send3_sem.at[0], recv3_sem.at[0], neighbour(127),
-        ),
-        remote(
-            wide_ref.at[PATCH : PATCH + HALO], wide_ref.at[0:HALO],
-            send3_sem.at[1], recv3_sem.at[1], neighbour(1),
-        ),
-    ]
-    for copy in halos:
-        copy.start()
-    for c in range(3):
-        land(HALO + c * 256, 256)
-    for copy in halos:
-        copy.wait()
-
-
-def relay(records, leave, send, listed, landing):
-    return pl.pallas_call(
-        relay_kernel,
-        out_shape=[S((C, PATCH), f32), S((PATCH + 2 * HALO, C), bf16)],
-        in_specs=[VMEM, SMEM, SMEM, SMEM, SMEM],
-        out_specs=[VMEM, VMEM],
-        scratch_shapes=[
-            pltpu.VMEM((4, CAP_OUT, 2, 128), f32),
-            pltpu.VMEM((4 * CAP_OUT, 2, 128), f32),
-            pltpu.VMEM((ORDERS, SLOTS, 2, 128), f32),
-            pltpu.VMEM((ORDERS * SLOTS, 2, 128), f32),
-            pltpu.VMEM((4, CAP, 2, 128), f32),
-            pltpu.VMEM((4 * CAP, 2, 128), f32),
-            pltpu.VMEM((PATCH, 2, 128), f32),
-            pltpu.SemaphoreType.DMA((ORDERS,)),
-            pltpu.SemaphoreType.DMA((ORDERS,)),
-            pltpu.SemaphoreType.DMA((4,)),
-            pltpu.SemaphoreType.DMA((4,)),
-            pltpu.SemaphoreType.DMA((2,)),
-            pltpu.SemaphoreType.DMA((2,)),
-            pltpu.SemaphoreType.DMA((4,)),
-            pltpu.SemaphoreType.DMA((4,)),
-        ],
-        compiler_params=kernel_params(collective_id=2, has_side_effects=True),
-        name="relay",
-    )(records, leave, send, listed, landing)
-
-
 def block_scratch():
     return [
         pltpu.VMEM((C, PATCH), bf16),
@@ -425,7 +283,7 @@
     ]
 
 
-def run_block(block, first_norm, x_ref, w_ref, base, cols_ref, scratch, emit, between):
+def run_block(block, first_norm, x_ref, w_ref, base, cols_ref, scratch, emit, between, parts=((0, 1024),)):
     normed_ref, qkv_ref, keys_ref, s0_ref, s1_ref, top_ref, heads_ref = scratch
 
     def column(k):
@@ -447,51 +305,57 @@
     head_of_row = iota((128, 1), 0) // HDIM
     buffers = (s0_ref, s1_ref)
 
-    def scores(h, b):
-        g = h // 8
-        queries = qkv_ref[0, pl.ds(pl.multiple_of(g * 128, 128), 128), :]
-        queries = jnp.where(head_of_row == h % 8, queries.astype(f32), 0.0).astype(bf16)
-        s = dot(keys_ref[g], queries)
-        buffers[b][...] = s
-        top_ref[b, 0:1, :] = jnp.max(s, axis=0, keepdims=True)
-
-    def finish(h, b):
-        p = jnp.exp2((buffers[b][...] - top_ref[b, 0:1, :]) * (0.25 * LOG2E))
-        inverse = 1.0 / jnp.sum(p, axis=0, keepdims=True)
-        chances = (p * inverse).astype(bf16)
-        rows = pl.ds(pl.multiple_of(h * HDIM, HDIM), HDIM)
-        heads_ref[rows, :] = dot(qkv_ref[2, rows, :], chances).astype(bf16)
-
-    scores(0, 0)
-
-    def pair(j, carry):
-        h = 2 * j
-        scores(h + 1, 1)
-        finish(h, 0)
-        scores(jnp.minimum(h + 2, HEADS - 1), 0)
-        finish(h + 1, 1)
-        return carry
-
-    lax.fori_loop(0, HEADS // 2, pair, 0)
-
-    between()
-    proj = [w_ref[r, base + 192 : base + 256, :].T for r in range(4)]
-    for c in range(4):
-        span = slice(c * 256, c * 256 + 256)
-        mixed = dot(proj[0], heads_ref[0:64, span])
-        for r in range(1, 4):
-            mixed = mixed + dot(proj[r], heads_ref[r * 64 : r * 64 + 64, span])
-        attended = x_ref[:, span] + (mixed + column(COL_PROJ + block))
-        normed = norm_columns(
-            attended, column(COL_GAIN + first_norm + 1), column(COL_SHIFT + first_norm + 1)
-        ).astype(bf16)
-        total = None
-        for r in range(4):
-            hidden = dot(w_ref[r, base + 256 : base + 512, :], normed) + column(COL_FC1 + 4 * block + r)
-            hidden = 0.5 * hidden * (1.0 + lax.erf(hidden * math.sqrt(0.5)))
-            part = dot(w_ref[r, base + 512 : base + 768, :], hidden.astype(bf16))
-            total = part if total is None else total + part
-        emit(c, attended + (total + column(COL_FC2 + block)))
+    def attention(first, width):
+        span = slice(first, first + width)
+
+        def scores(h, b):
+            g = h // 8
+            queries = qkv_ref[0, pl.ds(pl.multiple_of(g * 128, 128), 128), span]
+            queries = jnp.where(head_of_row == h % 8, queries.astype(f32), 0.0).astype(bf16)
+            s = dot(keys_ref[g], queries)
+            buffers[b][:, :width] = s
+            top_ref[b, 0:1, :width] = jnp.max(s, axis=0, keepdims=True)
+
+        def finish(h, b):
+            p = jnp.exp2((buffers[b][:, :width] - top_ref[b, 0:1, :width]) * (0.25 * LOG2E))
+            inverse = 1.0 / jnp.sum(p, axis=0, keepdims=True)
+            chances = (p * inverse).astype(bf16)
+            rows = pl.ds(pl.multiple_of(h * HDIM, HDIM), HDIM)
+            heads_ref[rows, span] = dot(qkv_ref[2, rows, :], chances).astype(bf16)
+
+        scores(0, 0)
+
+        def pair(j, carry):
+            h = 2 * j
+            scores(h + 1, 1)
+            finish(h, 0)
+            scores(jnp.minimum(h + 2, HEADS - 1), 0)
+            finish(h + 1, 1)
+            return carry
+
+        lax.fori_loop(0, HEADS // 2, pair, 0)
+
+    for n, (first, width) in enumerate(parts):
+        attention(first, width)
+        if n == 0:
+            between()
+            proj = [w_ref[r, base + 192 : base + 256, :].T for r in range(4)]
+        for c in range(first // 256, (first + width) // 256):
+            span = slice(c * 256, c * 256 + 256)
+            mixed = dot(proj[0], heads_ref[0:64, span])
+            for r in range(1, 4):
+                mixed = mixed + dot(proj[r], heads_ref[r * 64 : r * 64 + 64, span])
+            attended = x_ref[:, span] + (mixed + column(COL_PROJ + block))
+            normed = norm_columns(
+                attended, column(COL_GAIN + first_norm + 1), column(COL_SHIFT + first_norm + 1)
+            ).astype(bf16)
+            total = None
+            for r in range(4):
+                hidden = dot(w_ref[r, base + 256 : base + 512, :], normed) + column(COL_FC1 + 4 * block + r)
+                hidden = 0.5 * hidden * (1.0 + lax.erf(hidden * math.sqrt(0.5)))
+                part = dot(w_ref[r, base + 512 : base + 768, :], hidden.astype(bf16))
+                total = part if total is None else total + part
+            emit(c, attended + (total + column(COL_FC2 + block)))
 
 
 def first_kernel(
@@ -510,14 +374,15 @@
 
     pad = jnp.zeros((16, C - 64), f32)
     narrow = jnp.concatenate(
-        [qkv_b_ref[0].astype(f32), qkv_b_ref[1].astype(f32), conv_b_ref[...].astype(f32), jnp.zeros((9, 64), f32)],
+        [qkv_b_ref[j, b : b + 1].astype(f32) for b in range(2) for j in range(3)]
+        + [conv_b_ref[...].astype(f32), jnp.zeros((9, 64), f32)],
         axis=0,
     )
     narrow = jnp.concatenate([narrow, pad], axis=1)
     wide = jnp.concatenate([jnp.zeros((8, C), f32), fc1_b_ref[...].astype(f32), jnp.zeros((6, C), f32)], axis=0)
     w_ref[member, 0:16, :] = (narrow + wide).astype(bf16)
     for j in range(3):
-        w_ref[member, 16 + j * 64 : 80 + j * 64, :] = qkv_w_ref[0, j].T
+        w_ref[member, 16 + j * 64 : 80 + j * 64, :] = qkv_w_ref[0, j]
 
     def weight_copy(part, d):
         rows = (pl.ds(0, 208), pl.ds(208, 576))[part]
@@ -529,6 +394,7 @@
     pl.semaphore_wait(barrier, count)
     for d in (2, 3, 1):
         weight_copy(0, d).start()
+    route_slots(rank_ref, send_ref, leave_ref, routing)
     w_ref[member, 208:272, :] = proj_w_ref[0]
     w_ref[member, 272:528, :] = fc1_w_ref[0].T
     w_ref[member, 528:784, :] = fc2_w_ref[0].T
@@ -537,12 +403,12 @@
 
     def turn(k, carry):
         span = pl.ds(pl.multiple_of(k * C, C), C)
-        conv_own_ref[:, span] = conv_w_ref[k].T
+        conv_own_ref[:, span] = conv_w_ref[k]
         return carry
 
     lax.fori_loop(0, OFFS, turn, 0, unroll=3)
     for j in range(3):
-        later_own_ref[j * 64 : j * 64 + 64, :] = qkv_w_ref[1, j].T
+        later_own_ref[j * 64 : j * 64 + 64, :] = qkv_w_ref[1, j]
     later_own_ref[192:256, :] = proj_w_ref[1]
     later_own_ref[256:512, :] = fc1_w_ref[1].T
     later_own_ref[512:768, :] = fc2_w_ref[1].T
@@ -554,7 +420,6 @@
     ]
     for copy in later:
         copy.start()
-    route_slots(rank_ref, send_ref, leave_ref, routing)
     load.wait()
     for d in (2, 3, 1):
         weight_copy(0, d).wait()
@@ -571,7 +436,8 @@
     for r in range(4):
         for b in range(2):
             params_ref[COL_FC1 + 4 * b + r : COL_FC1 + 4 * b + r + 1, :] = bias[r][8 + b : 9 + b]
-    params_ref[COL_CPE : COL_CPE + 1, :] = cpe_b_ref[...].astype(f32)
+    halves = cpe_b_ref[...].astype(f32)
+    params_ref[COL_CPE : COL_CPE + 1, :] = jnp.concatenate([halves[0:1], halves[1:2]], axis=1)
     cols_ref[...] = params_ref[...].T
 
     def emit(c, value):
@@ -626,12 +492,15 @@
 
 
 def second_kernel(
-    wide_ref, moved_ref, near_ref, conv_ref, cpe_ref, later_ref, cols_ref, out_ref,
-    x_ref, index_ref, places_ref, hot_ref, picked_ref, conv_w_ref, w_ref, leave_ref,
-    sem, local_sem, send2_sem, recv2_sem, send_sem, recv_sem, *scratch
+    records_ref, leave_ref, send_ref, listed_ref, landing_ref, near_ref, conv_ref, cpe_ref, later_ref, cols_ref,
+    out_ref,
+    leaving_ref, rows_ref, packed_ref, frames_ref, sorted_ref, lists_ref, land_ref, wide_ref,
+    x_ref, index_ref, places_ref, hot_ref, picked_ref, conv_w_ref, w_ref, leave_out_ref,
+    sem, local_sem, send_sem, recv_sem, send2_sem, recv2_sem, send3_sem, recv3_sem, send4_sem, recv4_sem,
+    send5_sem, recv5_sem, send6_sem, recv6_sem, *scratch
 ):
-    member, group = lax.axis_index("mp"), lax.axis_index("order")
-    barrier, count = greet()
+    group, member = lax.axis_index("order"), lax.axis_index("mp")
+    barrier, count = greet(order_peers=True, halo=True)
     start = pl.multiple_of(member * PATCH, PATCH)
     load = pltpu.make_async_copy(near_ref.at[:, pl.ds(start, PATCH)], index_ref, sem)
     load.start()
@@ -649,21 +518,126 @@
         ]
     for copy in shares:
         copy.start()
-    pl.semaphore_wait(barrier, count)
+    copies = []
+    for d in (2, 3, 1):
+        target = member ^ d
+
+        def store(r, record, d=d):
+            leaving_ref[d, r] = record
+
+        move_rows(CAP_OUT, lambda r: leave_ref[target, r], records_ref, store)
+        if d == 2:
+            pl.semaphore_wait(barrier, count)
+        copy = remote(
+            leaving_ref.at[d], rows_ref.at[pl.ds(member * CAP_OUT, CAP_OUT)], send4_sem.at[d], recv4_sem.at[d],
+            (group, target),
+        )
+        copy.start()
+        copies.append(copy)
+
+    def store_staying(r, record):
+        rows_ref[member * CAP_OUT + r] = record
+
+    move_rows(CAP_OUT, lambda r: leave_ref[member, r], records_ref, store_staying)
+    for copy in copies:
+        copy.wait()
+
+    def frame_copy(d):
+        return remote(
+            packed_ref.at[d], frames_ref.at[pl.ds(pl.multiple_of(group * SLOTS, SLOTS), SLOTS)],
+            send_sem.at[d], recv_sem.at[d], (group ^ d, member),
+        )
+
+    def pack(t, carry):
+        d = 1 + (t + 8 * member + 7 * group) % (ORDERS - 1)
+        target = group ^ d
+
+        def store(r, record):
+            packed_ref[d, r] = record
+
+        move_rows(SLOTS, lambda r: send_ref[target, r], rows_ref, store)
+        frame_copy(d).start()
+        return carry
+
+    lax.fori_loop(0, ORDERS - 1, pack, 0)
+
+    def store_own(r, record):
+        frames_ref[group * SLOTS + r] = record
+
+    move_rows(SLOTS, lambda r: send_ref[group, r], rows_ref, store_own)
+
     for i, owner in enumerate((member, member ^ 2)):
         rows = pl.ds(pl.multiple_of(owner * 64, 64), 64)
         crossing = [
-            remote(conv_ref.at[i], conv_w_ref.at[rows], send2_sem.at[i], recv2_sem.at[i], (group, member ^ 1)),
-            remote(later_ref.at[i], w_ref.at[owner], send2_sem.at[2 + i], recv2_sem.at[2 + i], (group, member ^ 1)),
+            remote(conv_ref.at[i], conv_w_ref.at[rows], send5_sem.at[i], recv5_sem.at[i], (group, member ^ 1)),
+            remote(later_ref.at[i], w_ref.at[owner], send5_sem.at[2 + i], recv5_sem.at[2 + i], (group, member ^ 1)),
         ]
         for copy in crossing:
             copy.start()
         shares += crossing
-
     load.wait()
     near = index_ref[...]
     near = jnp.where(near < 0, -1, near - (first_token - HALO))
     places_ref[...] = jnp.concatenate([near, jnp.full((128 - OFFS, PATCH), -1, i32)], axis=0).T
+
+    def frame_wait(d, carry):
+        frame_copy(d).wait()
+        return carry
+
+    lax.fori_loop(1, ORDERS, frame_wait, 0)
+
+    copies = []
+    for d in (2, 3, 1):
+        target = member ^ d
+
+        def store(r, record, d=d):
+            sorted_ref[d, r] = record
+
+        move_rows(CAP, lambda r: listed_ref[target, r], frames_ref, store)
+        copy = remote(
+            sorted_ref.at[d], lists_ref.at[pl.ds(member * CAP, CAP)], send2_sem.at[d], recv2_sem.at[d],
+            (group, target),
+        )
+        copy.start()
+        copies.append(copy)
+
+    def store_mine(r, record):
+        lists_ref[member * CAP + r] = record
+
+    move_rows(CAP, lambda r: listed_ref[member, r], frames_ref, store_mine)
+    for copy in copies:
+        copy.wait()
+
+    def land(start, rows):
+        def store(r, record):
+            land_ref[start + r] = record
+
+        move_rows(rows, lambda r: landing_ref[0, start + r], lists_ref, store)
+        for half in range(2):
+            part = land_ref[start : start + rows, half, :]
+            at = slice(half * 128, half * 128 + 128)
+            x_ref[at, start : start + rows] = part.T
+            wide_ref[HALO + start : HALO + start + rows, at] = part.astype(bf16)
+
+    land(0, HALO)
+    land(PATCH - HALO, HALO)
+    halos = [
+        remote(
+            wide_ref.at[HALO : 2 * HALO], wide_ref.at[HALO + PATCH : 2 * HALO + PATCH],
+            send3_sem.at[0], recv3_sem.at[0], neighbour(127),
+        ),
+        remote(
+            wide_ref.at[PATCH : PATCH + HALO], wide_ref.at[0:HALO],
+            send3_sem.at[1], recv3_sem.at[1], neighbour(1),
+        ),
+    ]
+    for copy in halos:
+        copy.start()
+    for c in range(3):
+        land(HALO + c * 256, 256)
+    for copy in halos:
+        copy.wait()
+
     lanes = iota((256, 512), 1)
     for c in range(4):
         window = wide_ref[c * 256 : c * 256 + 512, :]
@@ -683,7 +657,7 @@
     for c in range(4):
         span = slice(c * 256, c * 256 + 256)
         mixture = dot(cpe, conv[:, span]) + column(COL_CPE)
-        x_ref[:, span] = moved_ref[:, span] + norm_columns(
+        x_ref[:, span] = x_ref[:, span] + norm_columns(
             mixture, column(COL_GAIN + 2), column(COL_SHIFT + 2)
         )
 
@@ -692,29 +666,40 @@
     def emit(c, value):
         span = slice(c * 256, c * 256 + 256)
         place = pl.ds(pl.multiple_of(member * PATCH + c * 256, 256), 256)
-        leave_ref[:, span] = value
+        leave_out_ref[:, span] = value
         for d in (2, 3, 1):
             target = member ^ d
             copy = remote(
-                leave_ref.at[pl.ds(pl.multiple_of(target * 64, 64), 64), span], out_ref.at[:, place],
-                send_sem.at[c, d], recv_sem.at[c, d], (group, target),
+                leave_out_ref.at[pl.ds(pl.multiple_of(target * 64, 64), 64), span], out_ref.at[:, place],
+                send6_sem.at[c, d], recv6_sem.at[c, d], (group, target),
             )
             copy.start()
             copies.append(copy)
-        out_ref[:, place] = leave_ref[pl.ds(pl.multiple_of(member * 64, 64), 64), span]
-
-    run_block(1, 3, x_ref, w_ref, 0, cols_ref, scratch, emit, lambda: None)
+        out_ref[:, place] = leave_out_ref[pl.ds(pl.multiple_of(member * 64, 64), 64), span]
+
+    run_block(1, 3, x_ref, w_ref, 0, cols_ref, scratch, emit, lambda: None, ((0, 768), (768, 256)))
     for copy in copies:
         copy.wait()
 
 
-def second_block(wide, moved, neighbours, conv, cpe, later, cols):
+def second_block(*operands):
+    pairs = [pltpu.SemaphoreType.DMA((ORDERS,))] * 2 + [pltpu.SemaphoreType.DMA((4,))] * 2
+    pairs += [pltpu.SemaphoreType.DMA((2,))] * 2 + [pltpu.SemaphoreType.DMA((4,))] * 4
+    pairs += [pltpu.SemaphoreType.DMA((4, 4))] * 2
     return pl.pallas_call(
         second_kernel,
         out_shape=S((64, TOK), f32),
-        in_specs=[VMEM, VMEM, ANY, ANY, VMEM, ANY, VMEM],
+        in_specs=[VMEM, SMEM, SMEM, SMEM, SMEM, ANY, ANY, VMEM, ANY, VMEM],
         out_specs=VMEM,
         scratch_shapes=[
+            pltpu.VMEM((4, CAP_OUT, 2, 128), f32),
+            pltpu.VMEM((4 * CAP_OUT, 2, 128), f32),
+            pltpu.VMEM((ORDERS, SLOTS, 2, 128), f32),
+            pltpu.VMEM((ORDERS * SLOTS, 2, 128), f32),
+            pltpu.VMEM((4, CAP, 2, 128), f32),
+            pltpu.VMEM((4 * CAP, 2, 128), f32),
+            pltpu.VMEM((PATCH, 2, 128), f32),
+            pltpu.VMEM((PATCH + 2 * HALO, C), bf16),
             pltpu.VMEM((C, PATCH), f32),
             pltpu.VMEM((OFFS, PATCH), i32),
             pltpu.VMEM((PATCH, 128), i32),
@@ -725,15 +710,12 @@
             pltpu.VMEM((C, PATCH), f32),
             pltpu.SemaphoreType.DMA,
             pltpu.SemaphoreType.DMA((4,)),
-            pltpu.SemaphoreType.DMA((4,)),
-            pltpu.SemaphoreType.DMA((4,)),
-            pltpu.SemaphoreType.DMA((4, 4)),
-            pltpu.SemaphoreType.DMA((4, 4)),
         ]
+        + pairs
         + block_scratch(),
-        compiler_params=kernel_params(collective_id=3, has_side_effects=True),
+        compiler_params=kernel_params(collective_id=2, has_side_effects=True),
         name="second_block",
-    )(wide, moved, neighbours, conv, cpe, later, cols)
+    )(*operands)
 
 
 def shards(
@@ -741,12 +723,14 @@
     fc1_weight, fc1_bias, fc2_weight, fc2_bias, conv_weight, conv_bias, cpe_weight, cpe_bias,
 ):
     records, cols, send, listed, landing, leave, conv, later = first_block(
-        feats, qkv_weight, proj_weight, fc1_weight, fc2_weight, norm_gain, norm_bias, qkv_bias, proj_bias,
-        fc1_bias, fc2_bias, conv_bias.reshape(1, 64), cpe_bias.reshape(1, C), conv_weight,
+        feats, qkv_weight.transpose(0, 1, 3, 2), proj_weight, fc1_weight, fc2_weight, norm_gain, norm_bias,
+        qkv_bias.transpose(1, 0, 2), proj_bias, fc1_bias, fc2_bias, conv_bias.reshape(1, 64),
+        cpe_bias.reshape(2, 128), conv_weight.transpose(0, 2, 1),
         serial_rank.reshape(32, 128),
     )
-    moved, wide = relay(records, leave, send, listed, landing)
-    return second_block(wide, moved, neighbours, conv, cpe_weight, later, cols)
+    return second_block(
+        records, leave, send, listed, landing, neighbours, conv, cpe_weight, later, cols
+    )
 
 
 def solution(mesh):

time: 191 us -> 174 us (0.911)
  Pallas kernels: 181 us -> 171 us
  local copies, waits for them, and re-layouts: 9.15 us -> 2.27 us
    pallas_call x1 -> x0, Pallas kernels: 70.2 us -> none  [relay(): pl.pallas_call(relay_kernel, out_shape=[S((C, PATCH), f32), S((PATCH + 2...]
    pallas_call x1, Pallas kernels: 59.3 us -> 121 us  [second_block(): pl.pallas_call(second_kernel, out_shape=S((64, TOK), f32), in_specs=[VMEM...]
    unnamed x4 -> x1, local copies, waits for them, and re-layouts: 7.95 us -> 2.27 us
where the time goes in v4:
time: 174 us
  Pallas kernels  171 us (98%)
  local copies, waits for them, and re-layouts  2.27 us (1%)
    pallas_call x1, Pallas kernels, second_block(): pl.pallas_call(second_kernel, out_shape=S((64, TOK), f32), in_specs=[VMEM...  121 us
    pallas_call x1, Pallas kernels, first_block(): pl.pallas_call(first_kernel, out_shape=[S((PATCH, 2, 128), f32), S((C, 12...  50.7 us

profile of v4, /device:TPU:1, one launch (start us, length us, event | category | flops | bytes accessed | tf_op | source)
XLA Modules:
  0.0 173.6 jit_solution(6731017904268649764)
XLA Ops:
  0.0 50.7 %first_block.1 = (f32[1024,2,128]{2,1,0:T(2,128)}, f32[256,128]{1,0:T(8,128)}, s32[32,64]{1,0:T(8,128)}, s32[4,288]{1,0:T(4,128)}, s32[1,1024]{1,0:T(1,128)}, /*...) custom-call(f32[256,4096]{1,0:T(8,128)} %feats_ref.1, bf16[2,3,64,256]{3,2,1,0:T(8,128)(2,1)} %bitcast.7, ...), custom_call_target="tpu_custom_call" | custom-call | tf_op jit(solution)/shard_map/first_block/pallas_call | solution.py:460
  50.7 120.6 %second_block.1 = f32[64,4096]{1,0:T(8,128)} custom-call(f32[1024,2,128]{2,1,0:T(2,128)} %get-tuple-element.13.records_ref, s32[4,352]{1,0:T(4,128)} %get-tuple-element.14.leave_ref, s32[32,64]{1,0:T(8,128)} %get-tuple-element.15.send_ref, s32[4,288]{1,0:T(4,128)} %get-tuple-element.16.listed_ref, s32[1,1024]{1,0:T(1,128)} %get-tuple-element.17.landing_ref, ...), custom_call_target="tpu_custom_call" | custom-call | tf_op jit(solution)/shard_map/second_block/pallas_call | solution.py:689
  171.3 2.3 %copy.19 = f32[64,4096]{1,0:T(8,128)} copy(f32[64,4096]{1,0:T(8,128)} %second_block.1) | data formatting | bytes 2097152

commit v5 on v4

--- a/solution.py
+++ b/solution.py
@@ -18,6 +18,7 @@
 SLOTS = 64
 CAP = 288
 CAP_OUT = 352
+STRIDE = 384
 ORDERS = 32
 MESH = pl.DeviceIdType.MESH
 EPS = 1e-05
@@ -90,6 +91,11 @@
     return pltpu.make_async_remote_copy(
         src_ref=src, dst_ref=dst, send_sem=send, recv_sem=recv, device_id=device, device_id_type=MESH
     )
+
+
+def in_rows(lists):
+    rows = [lists[q : q + 1, k * 128 : k * 128 + 128] for q in range(4) for k in range(STRIDE // 128)]
+    return jnp.concatenate(rows + [jnp.zeros((4, 128), i32)], axis=0)
 
 
 def prefix_matrix():
@@ -145,9 +151,15 @@
 
     lax.fori_loop(0, 32, frames, 0, unroll=2)
     acc = dot_rows(left_ref[...], right_ref[...])
-    send_ref[...] = (acc[0:32] * 64.0 + acc[32:64]).astype(i32)
+    send = (acc[0:32] * 64.0 + acc[32:64]).astype(i32)
+    send_ref[...] = jnp.concatenate([send, jnp.zeros((32, 128 - SLOTS), i32)], axis=1)
     inside = jnp.where(acc[128:160] > 0.5, (acc[64:96] * 64.0 + acc[96:128]).astype(i32), TOK)
-    inside = jnp.concatenate([inside, jnp.full((32, 128 - SLOTS), TOK, i32)], axis=1)
+    unused = jnp.full((32, SLOTS), TOK, i32)
+    inside = jnp.where(
+        group % 2 == 0,
+        jnp.concatenate([inside, unused], axis=1),
+        jnp.concatenate([unused, inside], axis=1),
+    )
     pos_out[...] = jnp.broadcast_to(inside[:, None, :], (32, 8, 128))
     pos_in[group] = pos_out[group]
 
@@ -169,7 +181,8 @@
 
     lax.fori_loop(0, 8, leaving, 0)
     acc = dot_rows(left2_ref[...], right2_ref[...])
-    leave_ref[...] = (acc[0:4] * 64.0 + acc[8:12]).astype(i32)
+    leave = (acc[0:4] * 64.0 + acc[8:12]).astype(i32)
+    leave_ref[...] = in_rows(jnp.concatenate([leave, jnp.zeros((4, STRIDE - CAP_OUT), i32)], axis=1))
 
 
 def route_lists(listed_ref, scratch):
@@ -183,26 +196,26 @@
         return carry
 
     lax.fori_loop(1, ORDERS, frame_wait, 0)
-    row, col = iota((256, 256), 0), iota((256, 256), 1)
-    pos = pos_in[:, 0, :]
-    hot = jnp.where(iota((32, 8, 128), 1) == (pos // PATCH)[:, None, :], 1.0, 0.0).reshape(256, 128)
+    row, col = iota((128, 128), 0), iota((128, 128), 1)
+    pos = jnp.min(pos_in[:, 0, :].reshape(16, 2, 128), axis=1)
+    hot = jnp.where(iota((16, 8, 128), 1) == (pos // PATCH)[:, None, :], 1.0, 0.0).reshape(128, 128)
     made = dot(hot.astype(bf16), both)
     earlier = (row % 8 == col % 8) & (col < row)
     carry = dot(jnp.where(earlier, 1.0, 0.0).astype(bf16), made[:, 128:].astype(bf16))
-    spot_ref[...] = jnp.sum((hot * (made[:, :128] + carry)).reshape(32, 8, 128), axis=1).astype(i32)
-    slot_ref[...] = pos
+    spot_ref[0:16, :] = jnp.sum((hot * (made[:, :128] + carry)).reshape(16, 8, 128), axis=1).astype(i32)
+    slot_ref[0:16, :] = pos
 
     def lists(c, acc):
         inside = slot_ref[pl.ds(c, 1), :]
         hot = jnp.where(iota((8, 128), 0) == inside // PATCH, 1.0, 0.0)
         inside = inside % PATCH
-        pieces = [jnp.broadcast_to(c, (1, 128)), lane, inside // 32, inside % 32]
+        pieces = [2 * c + lane // SLOTS, lane % SLOTS, inside // 32, inside % 32]
         left = jnp.concatenate([hot * p.astype(f32) for p in pieces] + [hot], axis=0)
         right = one_hot(iota((384, 128), 0), spot_ref[pl.ds(c, 1), :])
         return acc + dot_rows(left.astype(bf16), right)
 
-    acc = lax.fori_loop(0, 32, lists, jnp.zeros((40, 384), f32), unroll=4)
-    listed_ref[...] = (acc[0:4] * float(SLOTS) + acc[8:12]).astype(i32)[:, :CAP]
+    acc = lax.fori_loop(0, 16, lists, jnp.zeros((40, 384), f32), unroll=8)
+    listed_ref[...] = in_rows((acc[0:4] * float(SLOTS) + acc[8:12]).astype(i32))
     place = jnp.where(acc[32:36] > 0.5, (acc[16:20] * 32.0 + acc[24:28]).astype(i32), -1)
     place_out[...] = jnp.broadcast_to(place[:, None, :], (4, 8, 384))
     place_in[member] = place_out[member]
@@ -222,7 +235,8 @@
         at = q * CAP + entry
         left = jnp.where(kind == 0, at // 64, jnp.where(kind == 1, at % 64, 0))
         acc = acc + dot_rows(left.astype(f32).astype(bf16), right)
-    landing_ref[...] = (acc[0:1] * 64.0 + acc[1:2]).astype(i32)
+    landing = (acc[0:1] * 64.0 + acc[1:2]).astype(i32)
+    landing_ref[...] = jnp.concatenate([landing[:, k * 128 : k * 128 + 128] for k in range(8)], axis=0)
 
 
 def place_frame_copy(scratch, d):
@@ -263,12 +277,12 @@
 
 def move_rows(count, index, source, store):
     def step(i, carry):
-        records = [source[index(i * 16 + u)] for u in range(16)]
-        for u in range(16):
-            store(i * 16 + u, records[u])
+        records = [source[index(i * 32 + u)] for u in range(32)]
+        for u in range(32):
+            store(i * 32 + u, records[u])
         return carry
 
-    lax.fori_loop(0, count // 16, step, 0)
+    lax.fori_loop(0, count // 32, step, 0)
 
 
 def block_scratch():
@@ -462,10 +476,10 @@
         out_shape=[
             S((PATCH, 2, 128), f32),
             S((C, 128), f32),
-            S((ORDERS, SLOTS), i32),
-            S((4, CAP), i32),
-            S((1, PATCH), i32),
-            S((4, CAP_OUT), i32),
+            S((ORDERS, 128), i32),
+            S((16, 128), i32),
+            S((8, 128), i32),
+            S((16, 128), i32),
             S((2, 64, OFFS * C), bf16),
             S((2, 768, C), bf16),
         ],
@@ -495,7 +509,7 @@
     records_ref, leave_ref, send_ref, listed_ref, landing_ref, near_ref, conv_ref, cpe_ref, later_ref, cols_ref,
     out_ref,
     leaving_ref, rows_ref, packed_ref, frames_ref, sorted_ref, lists_ref, land_ref, wide_ref,
-    x_ref, index_ref, places_ref, hot_ref, picked_ref, conv_w_ref, w_ref, leave_out_ref,
+    x_ref, index_ref, places_ref, hot_ref, picked_ref, conv_w_ref, w_ref,
     sem, local_sem, send_sem, recv_sem, send2_sem, recv2_sem, send3_sem, recv3_sem, send4_sem, recv4_sem,
     send5_sem, recv5_sem, send6_sem, recv6_sem, *scratch
 ):
@@ -523,13 +537,13 @@
         target = member ^ d
 
         def store(r, record, d=d):
-            leaving_ref[d, r] = record
-
-        move_rows(CAP_OUT, lambda r: leave_ref[target, r], records_ref, store)
+            leaving_ref[d - 1, r] = record
+
+        move_rows(CAP_OUT, lambda r: leave_ref[target * STRIDE + r], records_ref, store)
         if d == 2:
             pl.semaphore_wait(barrier, count)
         copy = remote(
-            leaving_ref.at[d], rows_ref.at[pl.ds(member * CAP_OUT, CAP_OUT)], send4_sem.at[d], recv4_sem.at[d],
+            leaving_ref.at[d - 1], rows_ref.at[pl.ds(member * CAP_OUT, CAP_OUT)], send4_sem.at[d], recv4_sem.at[d],
             (group, target),
         )
         copy.start()
@@ -538,7 +552,7 @@
     def store_staying(r, record):
         rows_ref[member * CAP_OUT + r] = record
 
-    move_rows(CAP_OUT, lambda r: leave_ref[member, r], records_ref, store_staying)
+    move_rows(CAP_OUT, lambda r: leave_ref[member * STRIDE + r], records_ref, store_staying)
     for copy in copies:
         copy.wait()
 
@@ -555,7 +569,7 @@
         def store(r, record):
             packed_ref[d, r] = record
 
-        move_rows(SLOTS, lambda r: send_ref[target, r], rows_ref, store)
+        move_rows(SLOTS, lambda r: send_ref[target * 128 + r], rows_ref, store)
         frame_copy(d).start()
         return carry
 
@@ -564,7 +578,7 @@
     def store_own(r, record):
         frames_ref[group * SLOTS + r] = record
 
-    move_rows(SLOTS, lambda r: send_ref[group, r], rows_ref, store_own)
+    move_rows(SLOTS, lambda r: send_ref[group * 128 + r], rows_ref, store_own)
 
     for i, owner in enumerate((member, member ^ 2)):
         rows = pl.ds(pl.multiple_of(owner * 64, 64), 64)
@@ -591,11 +605,11 @@
         target = member ^ d
 
         def store(r, record, d=d):
-            sorted_ref[d, r] = record
-
-        move_rows(CAP, lambda r: listed_ref[target, r], frames_ref, store)
+            sorted_ref[d - 1, r] = record
+
+        move_rows(CAP, lambda r: listed_ref[target * STRIDE + r], frames_ref, store)
         copy = remote(
-            sorted_ref.at[d], lists_ref.at[pl.ds(member * CAP, CAP)], send2_sem.at[d], recv2_sem.at[d],
+            sorted_ref.at[d - 1], lists_ref.at[pl.ds(member * CAP, CAP)], send2_sem.at[d], recv2_sem.at[d],
             (group, target),
         )
         copy.start()
@@ -604,7 +618,7 @@
     def store_mine(r, record):
         lists_ref[member * CAP + r] = record
 
-    move_rows(CAP, lambda r: listed_ref[member, r], frames_ref, store_mine)
+    move_rows(CAP, lambda r: listed_ref[member * STRIDE + r], frames_ref, store_mine)
     for copy in copies:
         copy.wait()
 
@@ -612,7 +626,7 @@
         def store(r, record):
             land_ref[start + r] = record
 
-        move_rows(rows, lambda r: landing_ref[0, start + r], lists_ref, store)
+        move_rows(rows, lambda r: landing_ref[start + r], lists_ref, store)
         for half in range(2):
             part = land_ref[start : start + rows, half, :]
             at = slice(half * 128, half * 128 + 128)
@@ -666,16 +680,16 @@
     def emit(c, value):
         span = slice(c * 256, c * 256 + 256)
         place = pl.ds(pl.multiple_of(member * PATCH + c * 256, 256), 256)
-        leave_out_ref[:, span] = value
+        x_ref[:, span] = value
         for d in (2, 3, 1):
             target = member ^ d
             copy = remote(
-                leave_out_ref.at[pl.ds(pl.multiple_of(target * 64, 64), 64), span], out_ref.at[:, place],
+                x_ref.at[pl.ds(pl.multiple_of(target * 64, 64), 64), span], out_ref.at[:, place],
                 send6_sem.at[c, d], recv6_sem.at[c, d], (group, target),
             )
             copy.start()
             copies.append(copy)
-        out_ref[:, place] = leave_out_ref[pl.ds(pl.multiple_of(member * 64, 64), 64), span]
+        out_ref[:, place] = x_ref[pl.ds(pl.multiple_of(member * 64, 64), 64), span]
 
     run_block(1, 3, x_ref, w_ref, 0, cols_ref, scratch, emit, lambda: None, ((0, 768), (768, 256)))
     for copy in copies:
@@ -692,11 +706,11 @@
         in_specs=[VMEM, SMEM, SMEM, SMEM, SMEM, ANY, ANY, VMEM, ANY, VMEM],
         out_specs=VMEM,
         scratch_shapes=[
-            pltpu.VMEM((4, CAP_OUT, 2, 128), f32),
+            pltpu.VMEM((3, CAP_OUT, 2, 128), f32),
             pltpu.VMEM((4 * CAP_OUT, 2, 128), f32),
             pltpu.VMEM((ORDERS, SLOTS, 2, 128), f32),
             pltpu.VMEM((ORDERS * SLOTS, 2, 128), f32),
-            pltpu.VMEM((4, CAP, 2, 128), f32),
+            pltpu.VMEM((3, CAP, 2, 128), f32),
             pltpu.VMEM((4 * CAP, 2, 128), f32),
             pltpu.VMEM((PATCH, 2, 128), f32),
             pltpu.VMEM((PATCH + 2 * HALO, C), bf16),
@@ -707,7 +721,6 @@
             pltpu.VMEM((PATCH, OFFS * C), bf16),
             pltpu.VMEM((C, OFFS * C), bf16),
             pltpu.VMEM((4, 768, C), bf16),
-            pltpu.VMEM((C, PATCH), f32),
             pltpu.SemaphoreType.DMA,
             pltpu.SemaphoreType.DMA((4,)),
         ]
@@ -729,7 +742,8 @@
         serial_rank.reshape(32, 128),
     )
     return second_block(
-        records, leave, send, listed, landing, neighbours, conv, cpe_weight, later, cols
+        records, leave.reshape(-1), send.reshape(-1), listed.reshape(-1), landing.reshape(-1), neighbours, conv,
+        cpe_weight, later, cols,
     )
 
 

time: 174 us -> 172 us (0.989)
  no operation moved by 1% of the time
where the time goes in v5:
time: 172 us
  Pallas kernels  170 us (99%)
  local copies, waits for them, and re-layouts  2.27 us (1%)
    pallas_call x1, Pallas kernels, second_block(): pl.pallas_call(second_kernel, out_shape=S((64, TOK), f32), in_specs=[VMEM...  121 us
    pallas_call x1, Pallas kernels, first_block(): pl.pallas_call(first_kernel, out_shape=[S((PATCH, 2, 128), f32), S((C, 12...  49 us

profile of v5, /device:TPU:1, one launch (start us, length us, event | category | flops | bytes accessed | tf_op | source)
XLA Modules:
  0.0 172.0 jit_solution(7999978916342414670)
XLA Ops:
  0.0 49.0 %first_block.1 = (f32[1024,2,128]{2,1,0:T(2,128)}, f32[256,128]{1,0:T(8,128)}, s32[32,128]{1,0:T(8,128)}, s32[16,128]{1,0:T(8,128)}, s32[8,128]{1,0:T(8,128)}, /...) custom-call(f32[256,4096]{1,0:T(8,128)} %feats_ref.1, ...), custom_call_target="tpu_custom_call" | custom-call | tf_op jit(solution)/shard_map/first_block/pallas_call | solution.py:474
  49.0 120.7 %second_block.1 = f32[64,4096]{1,0:T(8,128)} custom-call(f32[1024,2,128]{2,1,0:T(2,128)} %get-tuple-element.13.records_ref, s32[2048]{0:T(1024)} %bitcast.15, s32[4096]{0:T(1024)} %bitcast.13, s32[2048]{0:T(1024)} %bitcast.14, s32[1024]{0:T(1024)} %bitcast.16, s32[27,4096]{1,0:T(8,128)} %near_ref.1, bf16[2,64,6912]{2,1,0:T(8,128)(2,1)} %get-tuple-element.18.conv_ref, ...), custom_call_target="tpu_custom_call" | custom-call | tf_op jit(solution)/shard_map/second_block/pallas_call | solution.py:703
  169.7 2.3 %copy.19 = f32[64,4096]{1,0:T(8,128)} copy(f32[64,4096]{1,0:T(8,128)} %second_block.1) | data formatting | bytes 2097152

commit v6 on v5

--- a/solution.py
+++ b/solution.py
@@ -539,15 +539,19 @@
         def store(r, record, d=d):
             leaving_ref[d - 1, r] = record
 
-        move_rows(CAP_OUT, lambda r: leave_ref[target * STRIDE + r], records_ref, store)
-        if d == 2:
-            pl.semaphore_wait(barrier, count)
-        copy = remote(
-            leaving_ref.at[d - 1], rows_ref.at[pl.ds(member * CAP_OUT, CAP_OUT)], send4_sem.at[d], recv4_sem.at[d],
-            (group, target),
-        )
-        copy.start()
-        copies.append(copy)
+        for n, (start, rows) in enumerate(((0, 160), (160, 192)) if d == 2 else ((0, CAP_OUT),)):
+            move_rows(
+                rows, lambda r: leave_ref[target * STRIDE + start + r], records_ref,
+                lambda r, record: store(start + r, record),
+            )
+            if d == 2 and n == 0:
+                pl.semaphore_wait(barrier, count)
+            copy = remote(
+                leaving_ref.at[d - 1, pl.ds(start, rows)], rows_ref.at[pl.ds(member * CAP_OUT + start, rows)],
+                send4_sem.at[d - 2 * n], recv4_sem.at[d - 2 * n], (group, target),
+            )
+            copy.start()
+            copies.append(copy)
 
     def store_staying(r, record):
         rows_ref[member * CAP_OUT + r] = record
@@ -607,13 +611,17 @@
         def store(r, record, d=d):
             sorted_ref[d - 1, r] = record
 
-        move_rows(CAP, lambda r: listed_ref[target * STRIDE + r], frames_ref, store)
-        copy = remote(
-            sorted_ref.at[d - 1], lists_ref.at[pl.ds(member * CAP, CAP)], send2_sem.at[d], recv2_sem.at[d],
-            (group, target),
-        )
-        copy.start()
-        copies.append(copy)
+        for n, (start, rows) in enumerate(((0, 128), (128, 160)) if d == 2 else ((0, CAP),)):
+            move_rows(
+                rows, lambda r: listed_ref[target * STRIDE + start + r], frames_ref,
+                lambda r, record: store(start + r, record),
+            )
+            copy = remote(
+                sorted_ref.at[d - 1, pl.ds(start, rows)], lists_ref.at[pl.ds(member * CAP + start, rows)],
+                send2_sem.at[d - 2 * n], recv2_sem.at[d - 2 * n], (group, target),
+            )
+            copy.start()
+            copies.append(copy)
 
     def store_mine(r, record):
         lists_ref[member * CAP + r] = record
@@ -649,11 +657,12 @@
         copy.start()
     for c in range(3):
         land(HALO + c * 256, 256)
-    for copy in halos:
-        copy.wait()
 
     lanes = iota((256, 512), 1)
-    for c in range(4):
+    for c in (1, 2, 0, 3):
+        if c == 0:
+            for copy in halos:
+                copy.wait()
         window = wide_ref[c * 256 : c * 256 + 512, :]
         places = places_ref[c * 256 : c * 256 + 256, :] - c * 256
         for b in range(OFFS // 3):

time: 172 us -> 172 us (level)
  no operation moved by 1% of the time
where the time goes in v6:
time: 172 us; the launch traced here: 171 us
  Pallas kernels  169 us (98%)
  local copies, waits for them, and re-layouts  2.27 us (1%)
    pallas_call x1, Pallas kernels, second_block(): pl.pallas_call(second_kernel, out_shape=S((64, TOK), f32), in_specs=[VMEM...  120 us
    pallas_call x1, Pallas kernels, first_block(): pl.pallas_call(first_kernel, out_shape=[S((PATCH, 2, 128), f32), S((C, 12...  49 us

profile of v6, /device:TPU:1, one launch (start us, length us, event | category | flops | bytes accessed | tf_op | source)
XLA Modules:
  0.0 171.4 jit_solution(3644778217917988860)
XLA Ops:
  0.0 49.0 %first_block.1 = (f32[1024,2,128]{2,1,0:T(2,128)}, f32[256,128]{1,0:T(8,128)}, s32[32,128]{1,0:T(8,128)}, s32[16,128]{1,0:T(8,128)}, s32[8,128]{1,0:T(8,128)}, /...) custom-call(f32[256,4096]{1,0:T(8,128)} %feats_ref.1, ...), custom_call_target="tpu_custom_call" | custom-call | tf_op jit(solution)/shard_map/first_block/pallas_call | solution.py:474
  49.0 120.1 %second_block.1 = f32[64,4096]{1,0:T(8,128)} custom-call(f32[1024,2,128]{2,1,0:T(2,128)} %get-tuple-element.13.records_ref, s32[2048]{0:T(1024)} %bitcast.15, s32[4096]{0:T(1024)} %bitcast.13, s32[2048]{0:T(1024)} %bitcast.14, s32[1024]{0:T(1024)} %bitcast.16, s32[27,4096]{1,0:T(8,128)} %near_ref.1, bf16[2,64,6912]{2,1,0:T(8,128)(2,1)} %get-tuple-element.18.conv_ref, ...), custom_call_target="tpu_custom_call" | custom-call | tf_op jit(solution)/shard_map/second_block/pallas_call | solution.py:712
  169.1 2.3 %copy.19 = f32[64,4096]{1,0:T(8,128)} copy(f32[64,4096]{1,0:T(8,128)} %second_block.1) | data formatting | bytes 2097152
